TPU v7x, 256 devices: a whole 4x4x8 slice. The times are simulated.
256 devices in a mesh: rep: 16 (over y, z_hi, core), shard: 16 (over z_lo, x).
Axes of the slice: x: 4, y: 4, z: 8 (z_hi: 2, z_lo: 4; z = z_hi * 4 + z_lo), core: 2. Of those that a mesh axis runs over, the one named last changes fastest.
Arguments:
- theta_outer: bfloat16 [16, 4096, 1792], P('rep', 'shard'), may hold values from -6 to 6
- theta_local: bfloat16 [16, 4096, 1792], P('rep', 'shard'), may hold values from -6 to 6
- momentum: float32 [16, 4096, 1792], P('rep', 'shard'), may hold values from -6 to 6
- gate_pre: bfloat16 [16, 4096, 1792], P('rep', 'shard'), may hold values from -8 to 8
- up_pre: bfloat16 [16, 4096, 1792], P('rep', 'shard'), may hold values from -6 to 6
- cotangent: bfloat16 [16, 4096, 4096], P('rep', 'shard'), may hold values from -6 to 6
- partner: int32 [16, 16], P('shard'), may hold values from 0 to 15, as said below
- chosen: int32 [16, 14], P('shard'), may hold values from 0 to 27, as said below
Outputs:
- momentum_new: float32 [16, 4096, 1792], P('rep', 'shard')
- grad_weight: bfloat16 [16, 4096, 1792], P('rep', 'shard')
- grad_gate: bfloat16 [16, 4096, 1792], P('rep', 'shard')
- grad_up: bfloat16 [16, 4096, 1792], P('rep', 'shard')
Inputs may be any that keep to these rules, and one draw needn't show every extreme that they name: For each shard s, partner[s, r] equals r XOR m_s for one number m_s of 1 to 15 that is common to all replicas of that shard, so partner[s, partner[s, r]] = r. `chosen`: each row holds 14 distinct tile indices.
All inputs are finite; a program needn't handle non-finite values.
Results may differ from a plain program's by a relative error of at most 0.023.
Values may be sent and summed in bfloat16 or wider, within the bound.
No kernel may reach another device: no remote copies, remote signals or barrier semaphores. Data moves between devices by JAX's collectives and lax.ppermute only.
A program may use at most 128 MiB of HBM per device.

v0:
```python
import jax
import jax.numpy as jnp
from jax import lax
from jax.sharding import PartitionSpec as P

TILE = 128


outer_rate = 0.7
outer_mu = 0.9


def from_partner(value, axis, stride):
    return lax.ppermute(value, axis, [(i, i ^ 1 << stride) for i in range(lax.axis_size(axis))])


def weight_gradient(cot_rows, hidden, scale):
    part = lax.dot_general(
        cot_rows, hidden, (((0,), (0,)), ((), ())), preferred_element_type=jnp.float32
    )
    return lax.psum_scatter(
        (scale * part).astype(jnp.bfloat16), "shard", scatter_dimension=0, tiled=True
    )


def cross_bit(moved, bit):
    return from_partner(moved, "rep", bit)


def local(theta_outer, theta_local, momentum, gate_pre, up_pre, cotangent, partner, chosen):
    outer = theta_outer[0].astype(jnp.float32)
    local_rows = theta_local[0].astype(jnp.float32)
    moment = momentum[0]
    gval = gate_pre[0].astype(jnp.float32)
    uval = up_pre[0].astype(jnp.float32)
    cot_rows = cotangent[0]
    listed = chosen[0]
    rows_here = outer.shape[0]
    width = outer.shape[1]
    scale = width ** (-0.5)
    sig = jax.nn.sigmoid(gval)
    silu_gate = gval * sig
    hidden = (silu_gate * uval).astype(jnp.bfloat16)
    delta = (outer - local_rows).astype(jnp.bfloat16)
    tiles = (
        delta.reshape(rows_here // TILE, TILE, width // TILE, TILE)
        .transpose(0, 2, 1, 3)
        .reshape(-1, TILE, TILE)
    )
    picked = tiles[listed]
    my_rep = lax.axis_index("rep")
    offset = jnp.bitwise_xor(partner[0][my_rep], my_rep)
    levels = lax.axis_size("rep").bit_length() - 1
    bit_list = list(range(levels))
    moved = picked
    for bit in bit_list:
        needed = offset // 2**bit % 2 == 1
        other = cross_bit(moved, bit)
        moved = jnp.where(needed, other, moved)
    averaged = 0.5 * (picked.astype(jnp.float32) + moved.astype(jnp.float32))
    tiles_f32 = tiles.astype(jnp.float32).at[listed].set(averaged)
    mixed = (
        tiles_f32.reshape(rows_here // TILE, width // TILE, TILE, TILE)
        .transpose(0, 2, 1, 3)
        .reshape(rows_here, width)
    )
    momentum_new = outer_mu * moment + mixed
    theta_new = (outer - outer_rate * (mixed + outer_mu * momentum_new)).astype(jnp.bfloat16)
    grad_hidden = scale * jnp.dot(
        cot_rows,
        lax.all_gather(theta_new, "shard", axis=0, tiled=True),
        preferred_element_type=jnp.float32,
    )
    grad_gate = (grad_hidden * uval * sig * (1.0 + gval * (1.0 - sig))).astype(jnp.bfloat16)
    grad_up = (grad_hidden * silu_gate).astype(jnp.bfloat16)
    grad_weight = weight_gradient(cot_rows, hidden, scale)
    return (momentum_new[None], grad_weight[None], grad_gate[None], grad_up[None])


def solution(mesh):
    placed = (
        P("rep", "shard", None),
        P("rep", "shard", None),
        P("rep", "shard", None),
        P("rep", "shard", None),
        P("rep", "shard", None),
        P("rep", "shard", None),
        P("shard", None),
        P("shard", None),
    )
    return jax.shard_map(
        local,
        mesh=mesh,
        in_specs=placed,
        out_specs=(
            P("rep", "shard", None),
            P("rep", "shard", None),
            P("rep", "shard", None),
            P("rep", "shard", None),
        ),
        check_vma=False,
    )
```

profile of v0, /device:TPU:6, one launch (start us, length us, event | category | flops | bytes accessed | tf_op | source)
XLA Modules:
  0.0 452.3 jit_solution(1370028562035143592)
XLA Ops:
  7.2 0.0 copy-start
  7.2 0.0 all-gather.2.cloned.1.call-start
  7.2 0.8 fusion.30
  8.0 1.5 copy.18
  9.5 2.2 copy.19
  11.7 2.3 fusion.7
  14.0 2.9 convert_element_type.73
  16.9 0.0 copy-start.4
  16.9 3.6 copy.20
  20.5 1.8 gather_fusion
  22.3 0.1 collective-permute-start
  22.4 0.0 copy-done.4
  22.5 0.6 constant_dynamic-slice_fusion
  23.7 0.7 collective-permute-done
  24.4 0.8 broadcast_select_fusion
  25.2 7.2 %collective-permute-start.1 = (bf16[14,128,128]{2,1,0:T(8,128)(2,1)}, bf16[14,128,128]{2,1,0:T(8,128)(2,1)}, u32[]{:S(2)}, u32[]{:S(2)}) collective-permute-start(bf16[14,128,128]{2,1,0:T(8,128)(2,1)} %broadcast_select_fusion), channel_id=1, source_target_pairs={{0,32},{16,48},{32,0},{48,16},{64,96},{80,112},{96,64},{112,80},{1... | collective-permute-start | bytes 1376264 | tf_op jit(solution)/shard_map/ppermute | solution.py:14
  32.4 20.3 %collective-permute-done.1 = bf16[14,128,128]{2,1,0:T(8,128)(2,1)} collective-permute-done((bf16[14,128,128]{2,1,0:T(8,128)(2,1)}, bf16[14,128,128]{2,1,0:T(8,128)(2,1)}, u32[]{:S(2)}, u32[]{:S(2)}) %collective-permute-start.1) | collective-permute-done | bytes 458784 | tf_op jit(solution)/shard_map/ppermute | solution.py:14
  52.6 1.8 broadcast_select_fusion.1
  54.5 1.6 collective-permute-start.2
  56.1 11.2 %collective-permute-done.2 = bf16[14,128,128]{2,1,0:T(8,128)(2,1)} collective-permute-done((bf16[14,128,128]{2,1,0:T(8,128)(2,1)}, bf16[14,128,128]{2,1,0:T(8,128)(2,1)}, u32[]{:S(2)}, u32[]{:S(2)}) %collective-permute-start.2) | collective-permute-done | bytes 458784 | tf_op jit(solution)/shard_map/ppermute | solution.py:14
  67.2 1.8 broadcast_select_fusion.2
  69.1 3.8 collective-permute-start.3
  72.8 2.8 copy.17
  75.6 2.6 bitcast_convert_fusion
  78.2 1.4 collective-permute-done.3
  79.6 2.1 add_multiply_fusion
  81.7 3.2 scatter_fusion
  85.0 4.0 copy.21
  88.9 3.4 fusion.9
  92.4 0.0 copy-start.1
  92.4 0.0 all-gather.2.cloned.1.call-update
  92.4 0.2 reduce-scatter.2.cloned.1.call-start
  92.6 2.2 copy.22
  94.9 0.0 copy-done.1
  94.9 1.3 copy.23
  96.2 0.0 copy-done
  96.2 9.2 %fusion = bf16[4096,1792]{0,1:T(8,128)(2,1)} fusion(bf16[1,256,4096]{2,1,0:T(8,128)(2,1)S(1)} %copy-done, bf16[1,256,1792]{1,2,0:T(8,128)(2,1)} %copy.23, bf16[1,256,1792]{1,2,0:T(8,128)(2,1)} %copy.22), kind=kOutput, calls=%fused_computation.3 | convolution fusion | flops 3776446464 | bytes 18612224 | tf_op jit(solution)/shard_map/dot_general | solution.py:18
  105.3 0.0 reduce-scatter.2.cloned.1.call-update
  105.4 3.6 reshape.68
  109.0 3.6 multiply_add_fusion
  112.6 0.0 copy-start.2
  112.6 2.8 copy.25
  115.4 164.1 %all-gather.2.cloned.1.call-done = bf16[4096,1792]{0,1:T(8,128)(2,1)} async-done(((bf16[256,1792]{0,1:T(8,128)(2,1)}), bf16[4096,1792]{0,1:T(8,128)(2,1)}) %all-gather.2.cloned.1.call-update) | async-done | bytes 14680080 | tf_op jit(solution)/shard_map/all_gather | solution.py:71
  279.5 0.0 copy-done.2
  279.5 11.5 %fusion.28 = (bf16[1,256,1792]{1,2,0:T(8,128)(2,1)}, bf16[1,256,1792]{1,2,0:T(8,128)(2,1)}) fusion(bf16[1,256,1792]{1,2,0:T(8,128)(2,1)S(1)} %copy-done.2, bf16[1,256,1792]{1,2,0:T(8,128)(2,1)} %copy.23, bf16[4096,1792]{0,1:T(8,128)(2,1)} %all-gather.2.cloned.1.call-done, bf16[1,256,4096]{2,1,0:T(8,128)(2,1)S(1)} %copy-done), kind=kOutput, calls=%fused_computation.42 | convolution fusion | flops 3765436416 | bytes 20447232 | tf_op jit(solution)/shard_map/dot_general | solution.py:69
  291.0 0.0 copy-start.3
  291.0 2.3 copy.28
  293.3 0.0 copy-done.3
  293.3 1.4 copy.27
  294.7 148.6 %reduce-scatter.2.cloned.1.call-done = bf16[256,1792]{0,1:T(8,128)(2,1)} async-done(((bf16[4096,1792]{0,1:T(8,128)(2,1)}), bf16[256,1792]{0,1:T(8,128)(2,1)}) %reduce-scatter.2.cloned.1.call-update) | async-done | bytes 917520 | tf_op jit(solution)/shard_map/reduce_scatter | solution.py:21
  443.3 2.2 copy.26
  (1 shorter events, 0.0 us)
Async XLA Ops:
  7.2 89.0 %copy-start = (bf16[1,256,4096]{2,1,0:T(8,128)(2,1)S(1)}, bf16[1,256,4096]{2,1,0:T(8,128)(2,1)}, u32[]{:S(2)}) copy-start(bf16[1,256,4096]{2,1,0:T(8,128)(2,1)} %param.13) | copy-start | bytes 6291460
  7.2 272.3 %all-gather.2.cloned.1.call-start = ((), (), s32[]{:S(2)}) async-start(), calls=%async_computation.2 | async-start | bytes 15597568 | tf_op jit(solution)/shard_map/all_gather | solution.py:71
  16.9 5.5 %copy-start.4 = (s32[1,16]{1,0:T(1,128)S(1)}, s32[1,16]{1,0:T(1,128)}, u32[]{:S(2)}) copy-start(s32[1,16]{1,0:T(1,128)} %param.14) | copy-start | bytes 196
  22.3 2.0 collective-permute-start
  25.2 27.4 %collective-permute-start.1 = (bf16[14,128,128]{2,1,0:T(8,128)(2,1)}, bf16[14,128,128]{2,1,0:T(8,128)(2,1)}, u32[]{:S(2)}, u32[]{:S(2)}) collective-permute-start(bf16[14,128,128]{2,1,0:T(8,128)(2,1)} %broadcast_select_fusion), channel_id=1, source_target_pairs={{0,32},{16,48},{32,0},{48,16},{64,96},{80,112},{96,64},{112,80},{1... | collective-permute-start | bytes 1376264 | tf_op jit(solution)/shard_map/ppermute | solution.py:14
  54.5 12.8 %collective-permute-start.2 = (bf16[14,128,128]{2,1,0:T(8,128)(2,1)}, bf16[14,128,128]{2,1,0:T(8,128)(2,1)}, u32[]{:S(2)}, u32[]{:S(2)}) collective-permute-start(bf16[14,128,128]{2,1,0:T(8,128)(2,1)} %broadcast_select_fusion.1), channel_id=1, source_target_pairs={{0,64},{16,80},{32,96},{48,112},{64,0},{80,16},{96,32},{112,48},{1... | collective-permute-start | bytes 1376264 | tf_op jit(solution)/shard_map/ppermute | solution.py:14
  69.1 10.5 %collective-permute-start.3 = (bf16[14,128,128]{2,1,0:T(8,128)(2,1)}, bf16[14,128,128]{2,1,0:T(8,128)(2,1)}, u32[]{:S(2)}, u32[]{:S(2)}) collective-permute-start(bf16[14,128,128]{2,1,0:T(8,128)(2,1)} %broadcast_select_fusion.2), channel_id=1, source_target_pairs={{0,128},{16,144},{32,160},{48,176},{64,192},{80,208},{96,224},{112... | collective-permute-start | bytes 1376264 | tf_op jit(solution)/shard_map/ppermute | solution.py:14
  92.4 2.5 copy-start.1
  92.4 350.9 %reduce-scatter.2.cloned.1.call-start = ((), (), s32[]{:S(2)}) async-start(), calls=%async_computation.1 | async-start | bytes 15597568 | tf_op jit(solution)/shard_map/reduce_scatter | solution.py:21
  112.6 166.9 %copy-start.2 = (bf16[1,256,1792]{1,2,0:T(8,128)(2,1)S(1)}, bf16[1,256,1792]{1,2,0:T(8,128)(2,1)}, u32[]{:S(2)}) copy-start(bf16[1,256,1792]{1,2,0:T(8,128)(2,1)} %copy.22) | copy-start | bytes 2752516
  291.0 2.3 copy-start.3
Sparse Core Ops, SparseCore 0:
  92.5 186.9 all-gather.1
  282.0 161.1 reduce-scatter.1
where the time goes:
time: 458 us; the launch traced here: 452 us
  waiting for transfers between devices  346 us (76%)
  local copies, waits for them, and re-layouts  38.3 us (8%)
  matrix products  20.7 us (5%)
  other arithmetic  19.5 us (4%)
  between operations  14.8 us (3%)
  starting transfers between devices  12.9 us (3%)
    all_gather x1, waiting for transfers between devices, local(): lax.all_gather(theta_new, 'shard', axis=0, tiled=True)  164 us
    reduce_scatter x1, waiting for transfers between devices, weight_gradient(): lax.psum_scatter((scale * part).astype(jnp.bfloat16), 'shard', scatter_di...  149 us
    ppermute x4, waiting for transfers between devices, from_partner(): lax.ppermute(value, axis, [(i, i ^ 1 << stride) for i in range(lax.axis_s...  33.5 us
    unnamed x19, local copies, waits for them, and re-layouts  18.6 us
    ppermute x4, starting transfers between devices, from_partner(): lax.ppermute(value, axis, [(i, i ^ 1 << stride) for i in range(lax.axis_s...  12.6 us
    dot_general x1, matrix products, local(): jnp.dot(cot_rows, lax.all_gather(theta_new, 'shard', axis=0, tiled=True),...  11.5 us
    dot_general x1, matrix products, weight_gradient(): lax.dot_general(cot_rows, hidden, (((0,), (0,)), ((), ())), preferred_ele...  9.18 us
  transfers between devices with their start and end apart: 6, of which 6 were waited for; matrix products, arithmetic and copies ran while one was open for 10% of the time, Pallas kernels for 0%

commit v1 on v0

v1 whole, which is shorter than its diff:
```python
import functools

import jax
import jax.numpy as jnp
from jax import lax
from jax.experimental import pallas as pl
from jax.experimental.pallas import tpu as pltpu
from jax.sharding import Mesh
from jax.sharding import PartitionSpec as P

TILE = 128
SIDE = 4
OUTER_RATE = 0.7
OUTER_MU = 0.9


def pick_kernel(chosen_ref, outer_ref, local_ref, picked_ref):
    across = outer_ref.shape[1] // TILE
    for i in range(picked_ref.shape[0]):
        tile = chosen_ref[0, i]
        row = pl.multiple_of(tile // across * TILE, TILE)
        col = pl.multiple_of(tile % across * TILE, TILE)
        at = (pl.ds(row, TILE), pl.ds(col, TILE))
        delta = outer_ref[at].astype(jnp.float32) - local_ref[at].astype(jnp.float32)
        picked_ref[i] = delta.astype(jnp.bfloat16)


def pick_tiles(chosen, outer, local_rows):
    count = chosen.shape[1]
    return pl.pallas_call(
        pick_kernel,
        out_shape=jax.ShapeDtypeStruct((count, TILE, TILE), jnp.bfloat16),
        in_specs=[
            pl.BlockSpec(memory_space=pltpu.SMEM),
            pl.BlockSpec(memory_space=pltpu.VMEM),
            pl.BlockSpec(memory_space=pltpu.VMEM),
        ],
        out_specs=pl.BlockSpec(memory_space=pltpu.VMEM),
        compiler_params=pltpu.CompilerParams(vmem_limit_bytes=16 * 2**20),
        cost_estimate=pl.CostEstimate(flops=count * TILE * TILE, bytes_accessed=3 * 2**20, transcendentals=0),
        name="pick_tiles",
    )(chosen, outer, local_rows)


def step_kernel(chosen_ref, outer_ref, local_ref, moment_ref, moved_ref, moment_out, theta_out, place):
    across = outer_ref.shape[1] // TILE
    half = pl.program_id(0)

    @pl.when(half == 0)
    def _():
        for t in range(place.shape[0]):
            place[t] = -1
        for i in range(moved_ref.shape[0]):
            place[chosen_ref[0, i]] = i

    for col in range(across):
        at = (slice(None), slice(col * TILE, (col + 1) * TILE))
        found = place[half * across + col]
        outer = outer_ref[at].astype(jnp.float32)
        delta = (outer - local_ref[at].astype(jnp.float32)).astype(jnp.bfloat16).astype(jnp.float32)
        other = moved_ref[jnp.maximum(found, 0)].astype(jnp.float32)
        mixed = jnp.where(found >= 0, 0.5 * (delta + other), delta)
        moment = OUTER_MU * moment_ref[at] + mixed
        moment_out[at] = moment
        theta_out[at] = (outer - OUTER_RATE * (mixed + OUTER_MU * moment)).astype(jnp.bfloat16)


def outer_step(chosen, outer, local_rows, moment, moved):
    rows, width = outer.shape
    block = pl.BlockSpec((TILE, width), lambda i: (i, 0))
    return pl.pallas_call(
        step_kernel,
        grid=(rows // TILE,),
        out_shape=[
            jax.ShapeDtypeStruct((rows, width), jnp.float32),
            jax.ShapeDtypeStruct((rows, width), jnp.bfloat16),
        ],
        in_specs=[
            pl.BlockSpec(memory_space=pltpu.SMEM),
            block,
            block,
            block,
            pl.BlockSpec(moved.shape, lambda i: (0, 0, 0)),
        ],
        out_specs=[block, block],
        scratch_shapes=[pltpu.SMEM((rows // TILE * (width // TILE),), jnp.int32)],
        compiler_params=pltpu.CompilerParams(vmem_limit_bytes=24 * 2**20),
        cost_estimate=pl.CostEstimate(flops=8 * rows * width, bytes_accessed=14 * rows * width, transcendentals=0),
        name="outer_step",
    )(chosen, outer, local_rows, moment, moved)


def turn(value, axis, by):
    return lax.ppermute(value, axis, [(i, (i + by) % SIDE) for i in range(SIDE)])


def block_at(blocks, index):
    return lax.dynamic_index_in_dim(blocks, index, 0, keepdims=False)


def swap_columns(cot_rows, x):
    rows, depth = cot_rows.shape
    piece = depth // (SIDE * SIDE)
    blocks = cot_rows.reshape(rows, SIDE, SIDE, piece).transpose(2, 0, 1, 3).reshape(SIDE, rows, SIDE * piece)
    return lax.all_to_all(blocks, "x", split_axis=0, concat_axis=0, tiled=True).reshape(SIDE * rows, SIDE * piece)


def gather_ring(own, x):
    half = own.shape[0] // 2
    left = turn(own, "x", 1)
    right = turn(own, "x", -1)
    far_top = turn(left[:half], "x", 1)
    far_low = turn(right[half:], "x", -1)
    far = jnp.concatenate([far_top, far_low], axis=0)
    out = jnp.zeros((SIDE,) + own.shape, own.dtype)
    for by, value in ((0, own), (-1, left), (1, right), (2, far)):
        out = lax.dynamic_update_index_in_dim(out, value, (x + by) % SIDE, 0)
    return out


def scatter_ring(blocks, x):
    half = blocks.shape[1] // 2
    across = block_at(blocks, (x + 2) % SIDE)
    from_left = turn(across[:half], "x", 1)
    from_right = turn(across[half:], "x", -1)
    up = block_at(blocks, (x + 1) % SIDE)
    down = block_at(blocks, (x - 1) % SIDE)
    up = jnp.concatenate([add(up[:half], from_left), up[half:]], axis=0)
    down = jnp.concatenate([down[:half], add(down[half:], from_right)], axis=0)
    return block_at(blocks, x), turn(up, "x", 1), turn(down, "x", -1)


def add(a, b):
    return (a.astype(jnp.float32) + b.astype(jnp.float32)).astype(jnp.bfloat16)


def up_pairs(first, last):
    return [(i, i + 1) for i in range(first, last)]


def down_pairs(first, last):
    return [(i + 1, i) for i in range(first, last)]


def gather_line(own, z):
    up, down = own, own
    ups, downs = [], []
    for far in range(1, SIDE):
        up = lax.ppermute(up, "z", up_pairs(far - 1, SIDE - 1))
        down = lax.ppermute(down, "z", down_pairs(0, SIDE - far))
        ups.append(up)
        downs.append(down)
    return [own] + [jnp.where(z >= far, ups[far - 1], downs[SIDE - far - 1]) for far in range(1, SIDE)]


def scatter_line(blocks, z):
    up = down = None
    for step in range(1, SIDE):
        far = SIDE - step
        mine_up = block_at(blocks, jnp.minimum(z + far, SIDE - 1))
        mine_down = block_at(blocks, jnp.maximum(z - far, 0))
        up = mine_up if up is None else add(mine_up, up)
        down = mine_down if down is None else add(mine_down, down)
        up = lax.ppermute(up, "z", up_pairs(0, step))
        down = lax.ppermute(down, "z", down_pairs(SIDE - 1 - step, SIDE - 1))
    return block_at(blocks, z), up, down


def local(theta_outer, theta_local, momentum, gate_pre, up_pre, cotangent, partner, chosen):
    outer, local_rows, moment = theta_outer[0], theta_local[0], momentum[0]
    cot_rows = cotangent[0]
    rows, width = outer.shape
    scale = width ** (-0.5)
    z, x = lax.axis_index("z"), lax.axis_index("x")
    gval = gate_pre[0].astype(jnp.float32)
    uval = up_pre[0].astype(jnp.float32)
    sig = jax.nn.sigmoid(gval)
    hidden = (gval * sig * uval).astype(jnp.bfloat16)

    picked = pick_tiles(chosen, outer, local_rows)
    my_rep = lax.axis_index("rep")
    replicas = lax.axis_size("rep")
    offset = jnp.bitwise_xor(partner[0, my_rep], my_rep)
    moved = picked
    for bit in range(replicas.bit_length() - 1):
        other = lax.ppermute(moved, "rep", [(i, i ^ (1 << bit)) for i in range(replicas)])
        moved = jnp.where((offset >> bit) & 1 == 1, other, moved)

    cot = swap_columns(cot_rows, x)
    hid = gather_ring(hidden, x).reshape(SIDE * rows, width)
    part = lax.dot_general(cot, hid, (((0,), (0,)), ((), ())), preferred_element_type=jnp.float32)
    part = (scale * part).astype(jnp.bfloat16).reshape(SIDE, rows, width)
    terms = scatter_line(part, z)
    grad_weight = sum(t.astype(jnp.float32) for t in terms).astype(jnp.bfloat16)

    momentum_new, theta_new = outer_step(chosen, outer, local_rows, moment, moved)
    pieces = gather_line(theta_new, z)
    columns = cot.reshape(SIDE * rows, SIDE, cot.shape[1] // SIDE)
    total = 0.0
    for far, piece in enumerate(pieces):
        cols = lax.dynamic_index_in_dim(columns, (z - far) % SIDE, 1, keepdims=False)
        total = total + jnp.dot(cols, piece, preferred_element_type=jnp.float32)
    part = (scale * total).astype(jnp.bfloat16).reshape(SIDE, rows, width)
    terms = scatter_ring(part, x)
    grad_hidden = sum(t.astype(jnp.float32) for t in terms)
    grad_gate = (grad_hidden * uval * sig * (1.0 + gval * (1.0 - sig))).astype(jnp.bfloat16)
    grad_up = (grad_hidden * (gval * sig)).astype(jnp.bfloat16)
    return (momentum_new[None], grad_weight[None], grad_gate[None], grad_up[None])


def solution(mesh):
    replicas, shards = mesh.devices.shape
    grid = Mesh(mesh.devices.reshape(replicas, shards // SIDE, SIDE), ("rep", "z", "x"))
    rows = P("rep", ("z", "x"), None)
    per_shard = P(("z", "x"), None)
    return jax.shard_map(
        local,
        mesh=grid,
        in_specs=(rows,) * 6 + (per_shard,) * 2,
        out_specs=(rows,) * 4,
        check_vma=False,
    )
```

time: 458 us -> 298 us (0.65); the launches traced: 452 us -> 297 us
  waiting for transfers between devices: 346 us -> 170 us
  starting transfers between devices: 12.9 us -> 61.2 us
  between operations: 14.8 us -> 1.66 us
  local copies, waits for them, and re-layouts: 38.3 us -> 29.3 us
  other arithmetic: 19.5 us -> 14.3 us
    all_gather x1 -> x0, waiting for transfers between devices: 164 us -> none  [local(): lax.all_gather(theta_new, 'shard', axis=0, tiled=True)]
    reduce_scatter x1 -> x0, waiting for transfers between devices: 149 us -> none  [weight_gradient(): lax.psum_scatter((scale * part).astype(jnp.bfloat16), 'shard', scatter_di...]
    ppermute x4 -> x24, waiting for transfers between devices: 33.5 us -> 170 us  [the longest x8 48.7 us: turn(): lax.ppermute(value, axis, [(i, (i + by) % SIDE) for i in range(SIDE)])]
    ppermute x4 -> x24, starting transfers between devices: 12.6 us -> 56.5 us  [the longest x3 14.9 us: gather_line(): up = lax.ppermute(up, 'z', up_pairs(far - 1, SIDE - 1))]
    unnamed x19 -> x34, local copies, waits for them, and re-layouts: 18.6 us -> 8.54 us
    another operation x0 -> x3, local copies, waits for them, and re-layouts: none -> 9.41 us  [the longest x2 6.08 us: swap_columns(): cot_rows.reshape(rows, SIDE, SIDE, piece).transpose(2, 0, 1, 3)]
    transpose x2 -> x0, local copies, waits for them, and re-layouts: 7.53 us -> none  [the longest x1 3.95 us: local(): mixed = tiles_f32.reshape(rows_here // TILE, width // TILE, TILE, TILE).t...]
    broadcast_in_dim x0 -> x2, other arithmetic: none -> 7.13 us  [the longest x1 4.42 us: local(): grad_up[None]]
  transfers between devices with their start and end apart: 6 -> 25, of which waited for: 6 -> 19; matrix products, arithmetic and copies ran while one was open for 10% -> 11% of each run, Pallas kernels for 0% -> 0%
where the time goes in v1:
time: 298 us; the launch traced here: 297 us
  waiting for transfers between devices  170 us (57%)
  starting transfers between devices  61.2 us (21%)
  local copies, waits for them, and re-layouts  29.3 us (10%)
  matrix products  17.8 us (6%)
  other arithmetic  14.3 us (5%)
  Pallas kernels  3.09 us (1%)
    ppermute x8, waiting for transfers between devices, turn(): lax.ppermute(value, axis, [(i, (i + by) % SIDE) for i in range(SIDE)])  48.7 us
    ppermute x3, waiting for transfers between devices, scatter_line(): up = lax.ppermute(up, 'z', up_pairs(0, step))  37.7 us
    ppermute x4, waiting for transfers between devices, local(): lax.ppermute(moved, 'rep', [(i, i ^ 1 << bit) for i in range(replicas)])  33.2 us
    ppermute x3, waiting for transfers between devices, scatter_line(): down = lax.ppermute(down, 'z', down_pairs(SIDE - 1 - step, SIDE - 1))  23.1 us
    ppermute x3, waiting for transfers between devices, gather_line(): down = lax.ppermute(down, 'z', down_pairs(0, SIDE - far))  17 us
    ppermute x3, starting transfers between devices, gather_line(): up = lax.ppermute(up, 'z', up_pairs(far - 1, SIDE - 1))  14.9 us
    ppermute x3, starting transfers between devices, scatter_line(): up = lax.ppermute(up, 'z', up_pairs(0, step))  13.2 us
    dot_general x4, matrix products, local(): total = total + jnp.dot(cols, piece, preferred_element_type=jnp.float32)  13.1 us
  transfers between devices with their start and end apart: 25, of which 19 were waited for; matrix products, arithmetic and copies ran while one was open for 11% of the time, Pallas kernels for 0%

profile of v1, /device:TPU:6, one launch (start us, length us, event | category | flops | bytes accessed | tf_op | source)
XLA Modules:
  0.0 297.2 jit_solution(16257351339316893810)
XLA Ops:
  0.7 1.2 copy-done.2
  1.8 1.2 copy-done.4
  6.3 7.3 %collective-permute-start.1 = (bf16[14,128,128]{2,1,0:T(8,128)(2,1)S(1)}, bf16[14,128,128]{2,1,0:T(8,128)(2,1)S(1)}, u32[]{:S(2)}, u32[]{:S(2)}) collective-permute-start(bf16[14,128,128]{2,1,0:T(8,128)(2,1)S(1)} %broadcast_select_fusion), channel_id=1, source_target_pairs={{0,32},{16,48},{32,0},{48,16},{64,96},{80,112},{96,64},{112,80},{1... | collective-permute-start | bytes 1376264 | tf_op jit(solution)/shard_map/ppermute | solution.py:186
  13.6 13.1 %collective-permute-done.1 = bf16[14,128,128]{2,1,0:T(8,128)(2,1)S(1)} collective-permute-done((bf16[14,128,128]{2,1,0:T(8,128)(2,1)S(1)}, bf16[14,128,128]{2,1,0:T(8,128)(2,1)S(1)}, u32[]{:S(2)}, u32[]{:S(2)}) %collective-permute-start.1) | collective-permute-done | bytes 458784 | tf_op jit(solution)/shard_map/ppermute | solution.py:186
  26.7 1.7 collective-permute-start.2
  28.4 10.3 %collective-permute-done.2 = bf16[14,128,128]{2,1,0:T(8,128)(2,1)S(1)} collective-permute-done((bf16[14,128,128]{2,1,0:T(8,128)(2,1)S(1)}, bf16[14,128,128]{2,1,0:T(8,128)(2,1)S(1)}, u32[]{:S(2)}, u32[]{:S(2)}) %collective-permute-start.2) | collective-permute-done | bytes 458784 | tf_op jit(solution)/shard_map/ppermute | solution.py:186
  38.8 3.3 %collective-permute-start.3 = (bf16[14,128,128]{2,1,0:T(8,128)(2,1)S(1)}, bf16[14,128,128]{2,1,0:T(8,128)(2,1)S(1)}, u32[]{:S(2)}, u32[]{:S(2)}) collective-permute-start(bf16[14,128,128]{2,1,0:T(8,128)(2,1)S(1)} %broadcast_select_fusion.2), channel_id=1, source_target_pairs={{0,128},{16,144},{32,160},{48,176},{64,192},{80,208},{96,224},{112... | collective-permute-start | bytes 1376264 | tf_op jit(solution)/shard_map/ppermute | solution.py:186
  42.0 9.3 %collective-permute-done.3 = bf16[14,128,128]{2,1,0:T(8,128)(2,1)S(1)} collective-permute-done((bf16[14,128,128]{2,1,0:T(8,128)(2,1)S(1)}, bf16[14,128,128]{2,1,0:T(8,128)(2,1)S(1)}, u32[]{:S(2)}, u32[]{:S(2)}) %collective-permute-start.3) | collective-permute-done | bytes 458784 | tf_op jit(solution)/shard_map/ppermute | solution.py:186
  51.4 1.5 copy-done.6
  52.9 2.4 outer_step.1
  55.3 1.3 collective-permute-start.15
  56.6 3.3 %reshape_squeeze.3 = bf16[256,4,4,256]{3,2,1,0:T(4,128)(2,1)S(1)} reshape(bf16[1,256,4096]{2,1,0:T(8,128)(2,1)} %param.13) | data formatting | bytes 4194304 | tf_op jit(solution)/shard_map/reshape;squeeze | solution.py:104
  59.9 2.8 copy.13
  62.7 4.8 %all-to-all-start = ((bf16[4,256,1024]{1,2,0:T(8,128)(2,1)}), bf16[4,256,1024]{1,2,0:T(8,128)(2,1)S(1)}, u32[]{:S(2)}, u32[]{:S(2)}) async-start(bf16[4,256,1024]{1,2,0:T(8,128)(2,1)} %bitcast.145), calls=%async_computation | async-start | bytes 4194304 | tf_op jit(solution)/shard_map/all_to_all | solution.py:105
  67.5 12.3 %collective-permute-start.14 = (bf16[256,1792]{1,0:T(8,128)(2,1)S(1)}, bf16[256,1792]{1,0:T(8,128)(2,1)}, u32[]{:S(2)}, u32[]{:S(2)}) collective-permute-start(bf16[256,1792]{1,0:T(8,128)(2,1)S(1)} %get-tuple-element.7), channel_id=1, source_target_pairs={{0,4},{4,8},{8,12},{1,5},{5,9},{9,13},{2,6},{6,10},{10,14},{3,7},{... | collective-permute-start | bytes 2752520 | tf_op jit(solution)/shard_map/ppermute | solution.py:149
  79.8 4.6 %collective-permute-done.15 = bf16[256,1792]{1,0:T(8,128)(2,1)} collective-permute-done((bf16[256,1792]{1,0:T(8,128)(2,1)S(1)}, bf16[256,1792]{1,0:T(8,128)(2,1)}, u32[]{:S(2)}, u32[]{:S(2)}) %collective-permute-start.15) | collective-permute-done | bytes 917536 | tf_op jit(solution)/shard_map/ppermute | solution.py:150
  84.4 1.3 collective-permute-start.16
  85.7 10.1 %collective-permute-done.14 = bf16[256,1792]{1,0:T(8,128)(2,1)} collective-permute-done((bf16[256,1792]{1,0:T(8,128)(2,1)S(1)}, bf16[256,1792]{1,0:T(8,128)(2,1)}, u32[]{:S(2)}, u32[]{:S(2)}) %collective-permute-start.14) | collective-permute-done | bytes 917536 | tf_op jit(solution)/shard_map/ppermute | solution.py:149
  95.8 1.6 collective-permute-start.18
  97.4 1.4 copy-done.11
  98.8 2.5 copy.14
  101.3 3.3 %reshape_reshape.3 = bf16[1024,4,256]{2,1,0:T(4,128)(2,1)S(1)} reshape(bf16[4,256,1024]{2,1,0:T(8,128)(2,1)} %copy.14) | data formatting | bytes 4194304 | tf_op jit(solution)/shard_map/reshape;reshape | solution.py:198
  104.7 1.3 collective-permute-done.16
  106.0 1.3 collective-permute-start.17
  107.3 5.2 %constant_dynamic-slice_fusion = (bf16[1024,1,256]{2,1,0:T(2,128)(2,1)}, bf16[1024,1,256]{2,1,0:T(2,128)(2,1)S(1)}, bf16[1024,1,256]{2,1,0:T(2,128)(2,1)S(1)}, bf16[1024,1,256]{2,1,0:T(2,128)(2,1)S(1)}) fusion(bf16[1024,4,256]{2,1,0:T(4,128)(2,1)S(1)} %reshape_reshape.3, s32[]{:T(128)S(6)} %select_n.170, s32[]{:T(128)S(6)} %select_n.166, s32[]{:T(128)S(6)} %select_n.162, ...), kind=kLoop, calls=%fused_computation.82 | loop fusion | bytes 4194320 | tf_op jit(solution)/shard_map/jit(dynamic_index_in_dim)/dynamic_slice | solution.py:201
  112.4 1.1 fusion.46
  113.6 0.9 collective-permute-start.19
  114.5 2.3 fusion.32
  116.8 11.1 %collective-permute-done.17 = bf16[256,1792]{1,0:T(8,128)(2,1)S(1)} collective-permute-done((bf16[256,1792]{1,0:T(8,128)(2,1)}, bf16[256,1792]{1,0:T(8,128)(2,1)S(1)}, u32[]{:S(2)}, u32[]{:S(2)}) %collective-permute-start.17) | collective-permute-done | bytes 917536 | tf_op jit(solution)/shard_map/ppermute | solution.py:150
  127.9 4.1 %fusion.34 = f32[1024,1792]{1,0:T(8,128)} fusion(bf16[256,1792]{1,0:T(8,128)(2,1)} %collective-permute-done.14, bf16[256,1792]{1,0:T(8,128)(2,1)S(1)} %collective-permute-done.17, pred[]{:T(512)S(6)} %ge.9, bf16[1024,1,256]{2,1,0:T(2,128)(2,1)S(1)} %get-tuple-element.22), kind=kOutput, calls=%fused_computation.55 | convolution fusion | flops 939982848 | bytes 9699329 | tf_op jit(solution)/shard_map/dot_general | solution.py:202
  132.0 0.9 copy-done.16
  132.9 5.6 %multiply_convert_fusion = bf16[1024,1792]{1,0:T(8,128)(2,1)S(1)} fusion(f32[1024,1792]{1,0:T(8,128)S(1)} %fusion.32, f32[1024,1792]{1,0:T(8,128)S(1)} %fusion.46, f32[1024,1792]{1,0:T(8,128)} %fusion.34, bf16[256,1792]{1,0:T(8,128)(2,1)} %copy-done.16, bf16[256,1792]{1,0:T(8,128)(2,1)} %collective-permute-done.15, pred[]{:T(512)S(6)} %ge.11, ...), kind=kOutput, calls=%fused_computation.2 | convolution fusion | flops 949157888 | bytes 28049408 | tf_op jit(solution)/shard_map/dot_general | solution.py:202
  139.3 1.5 collective-permute-start.22
  140.7 7.7 %collective-permute-done.20 = bf16[128,1792]{1,0:T(8,128)(2,1)S(1)} collective-permute-done((bf16[128,1792]{1,0:T(8,128)(2,1)S(1)}, bf16[128,1792]{1,0:T(8,128)(2,1)S(1)}, u32[]{:S(2)}, u32[]{:S(2)}) %collective-permute-start.20) | collective-permute-done | bytes 458784 | tf_op jit(solution)/shard_map/ppermute | solution.py:94
  148.4 1.1 collective-permute-done.22
  149.9 1.0 collective-permute-start.21
  150.9 1.0 pad_maximum_fusion.1
  151.9 1.1 collective-permute-start.23
  153.0 14.0 %collective-permute-done.21 = bf16[256,1792]{1,0:T(8,128)(2,1)} collective-permute-done((bf16[256,1792]{1,0:T(8,128)(2,1)S(1)}, bf16[256,1792]{1,0:T(8,128)(2,1)}, u32[]{:S(2)}, u32[]{:S(2)}) %collective-permute-start.21) | collective-permute-done | bytes 917536 | tf_op jit(solution)/shard_map/ppermute | solution.py:94
  167.0 1.8 collective-permute-done.23
  168.7 4.4 %fusion.26 = (bf16[1,256,1792]{2,1,0:T(8,128)(2,1)}, bf16[1,256,1792]{2,1,0:T(8,128)(2,1)}, bf16[256,1792]{1,0:T(8,128)(2,1)}) fusion(bf16[256,1792]{1,0:T(8,128)(2,1)} %collective-permute-done.23, bf16[256,1792]{1,0:T(8,128)(2,1)} %collective-permute-done.21, bf16[4,256,1792]{2,1,0:T(8,128)(2,1)} %bitcast.139, s32[]{:T(128)S(6)} %select_n.173, ...), kind=kLoop, calls=%fused_computation.40 | loop fusion | flops 10092544 | bytes 7340036 | tf_op jit(solution)/shard_map/broadcast_in_dim | solution.py:208
  173.4 1.8 collective-permute-start.5
  176.1 16.6 %collective-permute-done.4 = bf16[256,1792]{1,0:T(8,128)(2,1)S(1)} collective-permute-done((bf16[256,1792]{1,0:T(8,128)(2,1)}, bf16[256,1792]{1,0:T(8,128)(2,1)S(1)}, u32[]{:S(2)}, u32[]{:S(2)}) %collective-permute-start.4) | collective-permute-done | bytes 917536 | tf_op jit(solution)/shard_map/ppermute | solution.py:94
  192.7 1.4 collective-permute-start.6
  194.1 1.0 slice.51
  195.2 1.0 collective-permute-start.7
  196.3 1.4 bitcast_dynamic-update-slice_fusion
  197.7 3.6 %collective-permute-done.6 = bf16[128,1792]{1,0:T(8,128)(2,1)S(1)} collective-permute-done((bf16[128,1792]{1,0:T(8,128)(2,1)S(1)}, bf16[128,1792]{1,0:T(8,128)(2,1)S(1)}, u32[]{:S(2)}, u32[]{:S(2)}) %collective-permute-start.6) | collective-permute-done | bytes 458784 | tf_op jit(solution)/shard_map/ppermute | solution.py:94
  201.3 3.9 %collective-permute-done.7 = bf16[128,1792]{1,0:T(8,128)(2,1)S(1)} collective-permute-done((bf16[128,1792]{1,0:T(8,128)(2,1)S(1)}, bf16[128,1792]{1,0:T(8,128)(2,1)S(1)}, u32[]{:S(2)}, u32[]{:S(2)}) %collective-permute-start.7) | collective-permute-done | bytes 458784 | tf_op jit(solution)/shard_map/ppermute | solution.py:94
  205.3 4.7 %fusion = bf16[1792,1024]{0,1:T(8,128)(2,1)S(1)} fusion(bf16[4,256,1024]{1,2,0:T(8,128)(2,1)S(1)} %copy-done.12, bf16[4,256,1792]{2,1,0:T(8,128)(2,1)S(1)} %fusion.28), kind=kOutput, calls=%fused_computation.1 | convolution fusion | flops 3761766400 | bytes 9437184 | tf_op jit(solution)/shard_map/dot_general | solution.py:191
  210.1 1.7 copy-done.10
  211.8 2.9 collective-permute-start.8
  214.7 1.6 collective-permute-start.11
  216.3 14.9 %collective-permute-done.8 = bf16[256,1792]{1,0:T(8,128)(2,1)S(1)} collective-permute-done((bf16[256,1792]{1,0:T(8,128)(2,1)S(1)}, bf16[256,1792]{1,0:T(8,128)(2,1)S(1)}, u32[]{:S(2)}, u32[]{:S(2)}) %collective-permute-start.8) | collective-permute-done | bytes 917536 | tf_op jit(solution)/shard_map/ppermute | solution.py:164
  231.2 1.4 fusion.21
  232.6 4.4 %collective-permute-start.9 = (bf16[256,1792]{1,0:T(8,128)(2,1)S(1)}, bf16[256,1792]{1,0:T(8,128)(2,1)S(1)}, u32[]{:S(2)}, u32[]{:S(2)}) collective-permute-start(bf16[256,1792]{1,0:T(8,128)(2,1)S(1)} %fusion.21), channel_id=1, source_target_pairs={{0,4},{4,8},{1,5},{5,9},{2,6},{6,10},{3,7},{7,11},{16,20},{20,24},... | collective-permute-start | bytes 2752520 | tf_op jit(solution)/shard_map/ppermute | solution.py:164
  237.1 15.6 %collective-permute-done.9 = bf16[256,1792]{1,0:T(8,128)(2,1)S(1)} collective-permute-done((bf16[256,1792]{1,0:T(8,128)(2,1)S(1)}, bf16[256,1792]{1,0:T(8,128)(2,1)S(1)}, u32[]{:S(2)}, u32[]{:S(2)}) %collective-permute-start.9) | collective-permute-done | bytes 917536 | tf_op jit(solution)/shard_map/ppermute | solution.py:164
  252.7 2.2 fusion.22
  255.6 5.9 %collective-permute-start.10 = (bf16[256,1792]{1,0:T(8,128)(2,1)S(1)}, bf16[256,1792]{1,0:T(8,128)(2,1)}, u32[]{:S(2)}, u32[]{:S(2)}) collective-permute-start(bf16[256,1792]{1,0:T(8,128)(2,1)S(1)} %get-tuple-element.16), channel_id=1, source_target_pairs={{0,4},{4,8},{8,12},{1,5},{5,9},{9,13},{2,6},{6,10},{10,14},{3,7},{... | collective-permute-start | bytes 2752520 | tf_op jit(solution)/shard_map/ppermute | solution.py:164
  261.5 1.4 fusion.20
  262.9 1.3 collective-permute-start.13
  264.2 7.2 %collective-permute-done.10 = bf16[256,1792]{1,0:T(8,128)(2,1)} collective-permute-done((bf16[256,1792]{1,0:T(8,128)(2,1)S(1)}, bf16[256,1792]{1,0:T(8,128)(2,1)}, u32[]{:S(2)}, u32[]{:S(2)}) %collective-permute-start.10) | collective-permute-done | bytes 917536 | tf_op jit(solution)/shard_map/ppermute | solution.py:164
  271.4 23.1 %collective-permute-done.13 = bf16[256,1792]{1,0:T(8,128)(2,1)S(1)} collective-permute-done((bf16[256,1792]{1,0:T(8,128)(2,1)S(1)}, bf16[256,1792]{1,0:T(8,128)(2,1)S(1)}, u32[]{:S(2)}, u32[]{:S(2)}) %collective-permute-start.13) | collective-permute-done | bytes 917536 | tf_op jit(solution)/shard_map/ppermute | solution.py:165
  294.5 2.7 fusion.27
  (54 shorter events, 6.1 us)
Async XLA Ops:
  0.6 3.8 %copy-start = (s32[1,16]{1,0:T(1,128)S(1)}, s32[1,16]{1,0:T(1,128)}, u32[]{:S(2)}) copy-start(s32[1,16]{1,0:T(1,128)} %param.14) | copy-start | bytes 196
  0.6 1.2 copy-start.2
  1.8 1.2 copy-start.4
  3.0 0.7 copy-start.7
  4.3 1.9 collective-permute-start
  6.3 20.4 %collective-permute-start.1 = (bf16[14,128,128]{2,1,0:T(8,128)(2,1)S(1)}, bf16[14,128,128]{2,1,0:T(8,128)(2,1)S(1)}, u32[]{:S(2)}, u32[]{:S(2)}) collective-permute-start(bf16[14,128,128]{2,1,0:T(8,128)(2,1)S(1)} %broadcast_select_fusion), channel_id=1, source_target_pairs={{0,32},{16,48},{32,0},{48,16},{64,96},{80,112},{96,64},{112,80},{1... | collective-permute-start | bytes 1376264 | tf_op jit(solution)/shard_map/ppermute | solution.py:186
  13.6 37.8 %copy-start.3 = (bf16[1,256,1792]{2,1,0:T(8,128)(2,1)S(1)}, bf16[1,256,1792]{2,1,0:T(8,128)(2,1)}, u32[]{:S(2)}) copy-start(bf16[1,256,1792]{2,1,0:T(8,128)(2,1)} %param.8) | copy-start | bytes 2752516
  13.6 37.8 %copy-start.5 = (bf16[1,256,1792]{2,1,0:T(8,128)(2,1)S(1)}, bf16[1,256,1792]{2,1,0:T(8,128)(2,1)}, u32[]{:S(2)}) copy-start(bf16[1,256,1792]{2,1,0:T(8,128)(2,1)} %param.9) | copy-start | bytes 2752516
  13.6 37.8 %copy-start.8 = (s32[1,14]{1,0:T(1,128)S(1)}, s32[1,14]{1,0:T(1,128)}, u32[]{:S(2)}) copy-start(s32[1,14]{1,0:T(1,128)} %chosen_ref.3) | copy-start | bytes 172
  26.7 12.0 %collective-permute-start.2 = (bf16[14,128,128]{2,1,0:T(8,128)(2,1)S(1)}, bf16[14,128,128]{2,1,0:T(8,128)(2,1)S(1)}, u32[]{:S(2)}, u32[]{:S(2)}) collective-permute-start(bf16[14,128,128]{2,1,0:T(8,128)(2,1)S(1)} %broadcast_select_fusion.1), channel_id=1, source_target_pairs={{0,64},{16,80},{32,96},{48,112},{64,0},{80,16},{96,32},{112,48},{1... | collective-permute-start | bytes 1376264 | tf_op jit(solution)/shard_map/ppermute | solution.py:186
  38.8 12.6 %collective-permute-start.3 = (bf16[14,128,128]{2,1,0:T(8,128)(2,1)S(1)}, bf16[14,128,128]{2,1,0:T(8,128)(2,1)S(1)}, u32[]{:S(2)}, u32[]{:S(2)}) collective-permute-start(bf16[14,128,128]{2,1,0:T(8,128)(2,1)S(1)} %broadcast_select_fusion.2), channel_id=1, source_target_pairs={{0,128},{16,144},{32,160},{48,176},{64,192},{80,208},{96,224},{112... | collective-permute-start | bytes 1376264 | tf_op jit(solution)/shard_map/ppermute | solution.py:186
  51.4 1.5 copy-start.6
  55.3 29.1 %collective-permute-start.15 = (bf16[256,1792]{1,0:T(8,128)(2,1)S(1)}, bf16[256,1792]{1,0:T(8,128)(2,1)}, u32[]{:S(2)}, u32[]{:S(2)}) collective-permute-start(bf16[256,1792]{1,0:T(8,128)(2,1)S(1)} %get-tuple-element.7), channel_id=1, source_target_pairs={{4,0},{8,4},{12,8},{5,1},{9,5},{13,9},{6,2},{10,6},{14,10},{7,3},{... | collective-permute-start | bytes 2752520 | tf_op jit(solution)/shard_map/ppermute | solution.py:150
  62.7 34.7 %all-to-all-start = ((bf16[4,256,1024]{1,2,0:T(8,128)(2,1)}), bf16[4,256,1024]{1,2,0:T(8,128)(2,1)S(1)}, u32[]{:S(2)}, u32[]{:S(2)}) async-start(bf16[4,256,1024]{1,2,0:T(8,128)(2,1)} %bitcast.145), calls=%async_computation | async-start | bytes 4194304 | tf_op jit(solution)/shard_map/all_to_all | solution.py:105
  67.5 28.3 %collective-permute-start.14 = (bf16[256,1792]{1,0:T(8,128)(2,1)S(1)}, bf16[256,1792]{1,0:T(8,128)(2,1)}, u32[]{:S(2)}, u32[]{:S(2)}) collective-permute-start(bf16[256,1792]{1,0:T(8,128)(2,1)S(1)} %get-tuple-element.7), channel_id=1, source_target_pairs={{0,4},{4,8},{8,12},{1,5},{5,9},{9,13},{2,6},{6,10},{10,14},{3,7},{... | collective-permute-start | bytes 2752520 | tf_op jit(solution)/shard_map/ppermute | solution.py:149
  84.4 21.5 %collective-permute-start.16 = (bf16[256,1792]{1,0:T(8,128)(2,1)}, bf16[256,1792]{1,0:T(8,128)(2,1)}, u32[]{:S(2)}, u32[]{:S(2)}) collective-permute-start(bf16[256,1792]{1,0:T(8,128)(2,1)} %collective-permute-done.15), channel_id=1, source_target_pairs={{4,0},{8,4},{5,1},{9,5},{6,2},{10,6},{7,3},{11,7},{20,16},{24,20},... | collective-permute-start | bytes 2752520 | tf_op jit(solution)/shard_map/ppermute | solution.py:150
  95.8 17.8 %collective-permute-start.18 = (bf16[256,1792]{1,0:T(8,128)(2,1)}, bf16[256,1792]{1,0:T(8,128)(2,1)}, u32[]{:S(2)}, u32[]{:S(2)}) collective-permute-start(bf16[256,1792]{1,0:T(8,128)(2,1)} %collective-permute-done.14), channel_id=1, source_target_pairs={{4,8},{8,12},{5,9},{9,13},{6,10},{10,14},{7,11},{11,15},{20,24},{2... | collective-permute-start | bytes 2752520 | tf_op jit(solution)/shard_map/ppermute | solution.py:149
  97.4 1.4 copy-start.11
  106.0 22.0 %collective-permute-start.17 = (bf16[256,1792]{1,0:T(8,128)(2,1)}, bf16[256,1792]{1,0:T(8,128)(2,1)S(1)}, u32[]{:S(2)}, u32[]{:S(2)}) collective-permute-start(bf16[256,1792]{1,0:T(8,128)(2,1)} %collective-permute-done.16), channel_id=1, source_target_pairs={{4,0},{5,1},{6,2},{7,3},{20,16},{21,17},{22,18},{23,19},{36,32},{3... | collective-permute-start | bytes 2752520 | tf_op jit(solution)/shard_map/ppermute | solution.py:150
  113.6 18.4 %collective-permute-start.19 = (bf16[256,1792]{1,0:T(8,128)(2,1)}, bf16[256,1792]{1,0:T(8,128)(2,1)S(1)}, u32[]{:S(2)}, u32[]{:S(2)}) collective-permute-start(bf16[256,1792]{1,0:T(8,128)(2,1)} %collective-permute-done.18), channel_id=1, source_target_pairs={{8,12},{9,13},{10,14},{11,15},{24,28},{25,29},{26,30},{27,31},{40,... | collective-permute-start | bytes 2752520 | tf_op jit(solution)/shard_map/ppermute | solution.py:149
  127.9 5.0 %copy-start.15 = (bf16[1024,1,256]{2,1,0:T(2,128)(2,1)S(1)}, bf16[1024,1,256]{2,1,0:T(2,128)(2,1)}, u32[]{:S(2)}) copy-start(bf16[1024,1,256]{2,1,0:T(2,128)(2,1)} %get-tuple-element.20) | copy-start | bytes 1572868
  132.0 0.9 copy-start.16
  138.5 11.1 %copy-start.9 = (bf16[1024,1792]{1,0:T(8,128)(2,1)}, bf16[1024,1792]{1,0:T(8,128)(2,1)S(1)}, u32[]{:S(2)}) copy-start(bf16[1024,1792]{1,0:T(8,128)(2,1)S(1)} %multiply_convert_fusion) | copy-start | bytes 11010052
  138.6 9.8 %collective-permute-start.20 = (bf16[128,1792]{1,0:T(8,128)(2,1)S(1)}, bf16[128,1792]{1,0:T(8,128)(2,1)S(1)}, u32[]{:S(2)}, u32[]{:S(2)}) collective-permute-start(bf16[128,1792]{1,0:T(8,128)(2,1)S(1)} %get-tuple-element.12), channel_id=1, source_target_pairs={{0,1},{1,2},{2,3},{3,0},{4,5},{5,6},{6,7},{7,4},{8,9},{9,10},{10,1... | collective-permute-start | bytes 1376264 | tf_op jit(solution)/shard_map/ppermute | solution.py:94
  139.3 10.3 %collective-permute-start.22 = (bf16[128,1792]{1,0:T(8,128)(2,1)S(1)}, bf16[128,1792]{1,0:T(8,128)(2,1)S(1)}, u32[]{:S(2)}, u32[]{:S(2)}) collective-permute-start(bf16[128,1792]{1,0:T(8,128)(2,1)S(1)} %get-tuple-element.14), channel_id=1, source_target_pairs={{0,3},{1,0},{2,1},{3,2},{4,7},{5,4},{6,5},{7,6},{8,11},{9,8},{10,9... | collective-permute-start | bytes 1376264 | tf_op jit(solution)/shard_map/ppermute | solution.py:94
  149.8 18.9 %copy-start.13 = (bf16[1,256,1792]{2,1,0:T(8,128)(2,1)S(1)}, bf16[1,256,1792]{2,1,0:T(8,128)(2,1)}, u32[]{:S(2)}) copy-start(bf16[1,256,1792]{2,1,0:T(8,128)(2,1)} %param.12) | copy-start | bytes 2752516
  149.8 18.9 %copy-start.14 = (bf16[1,256,1792]{2,1,0:T(8,128)(2,1)S(1)}, bf16[1,256,1792]{2,1,0:T(8,128)(2,1)}, u32[]{:S(2)}) copy-start(bf16[1,256,1792]{2,1,0:T(8,128)(2,1)} %param.11) | copy-start | bytes 2752516
  149.9 17.1 %collective-permute-start.21 = (bf16[256,1792]{1,0:T(8,128)(2,1)S(1)}, bf16[256,1792]{1,0:T(8,128)(2,1)}, u32[]{:S(2)}, u32[]{:S(2)}) collective-permute-start(bf16[256,1792]{1,0:T(8,128)(2,1)S(1)} %pad_maximum_fusion), channel_id=1, source_target_pairs={{0,1},{1,2},{2,3},{3,0},{4,5},{5,6},{6,7},{7,4},{8,9},{9,10},{10,1... | collective-permute-start | bytes 2752520 | tf_op jit(solution)/shard_map/ppermute | solution.py:94
  151.9 16.8 %collective-permute-start.23 = (bf16[256,1792]{1,0:T(8,128)(2,1)}, bf16[256,1792]{1,0:T(8,128)(2,1)}, u32[]{:S(2)}, u32[]{:S(2)}) collective-permute-start(bf16[256,1792]{1,0:T(8,128)(2,1)} %pad_maximum_fusion.1), channel_id=1, source_target_pairs={{0,3},{1,0},{2,1},{3,2},{4,7},{5,4},{6,5},{7,6},{8,11},{9,8},{10,9... | collective-permute-start | bytes 2752520 | tf_op jit(solution)/shard_map/ppermute | solution.py:94
  173.2 19.5 %collective-permute-start.4 = (bf16[256,1792]{1,0:T(8,128)(2,1)}, bf16[256,1792]{1,0:T(8,128)(2,1)S(1)}, u32[]{:S(2)}, u32[]{:S(2)}) collective-permute-start(bf16[256,1792]{1,0:T(8,128)(2,1)} %get-tuple-element.24), channel_id=1, source_target_pairs={{0,1},{1,2},{2,3},{3,0},{4,5},{5,6},{6,7},{7,4},{8,9},{9,10},{10,1... | collective-permute-start | bytes 2752520 | tf_op jit(solution)/shard_map/ppermute | solution.py:94
  173.4 20.7 %collective-permute-start.5 = (bf16[256,1792]{1,0:T(8,128)(2,1)}, bf16[256,1792]{1,0:T(8,128)(2,1)}, u32[]{:S(2)}, u32[]{:S(2)}) collective-permute-start(bf16[256,1792]{1,0:T(8,128)(2,1)} %get-tuple-element.24), channel_id=1, source_target_pairs={{0,3},{1,0},{2,1},{3,2},{4,7},{5,4},{6,5},{7,6},{8,11},{9,8},{10,9... | collective-permute-start | bytes 2752520 | tf_op jit(solution)/shard_map/ppermute | solution.py:94
  192.7 8.6 %collective-permute-start.6 = (bf16[128,1792]{1,0:T(8,128)(2,1)S(1)}, bf16[128,1792]{1,0:T(8,128)(2,1)S(1)}, u32[]{:S(2)}, u32[]{:S(2)}) collective-permute-start(bf16[128,1792]{1,0:T(8,128)(2,1)S(1)} %slice.50), channel_id=1, source_target_pairs={{0,1},{1,2},{2,3},{3,0},{4,5},{5,6},{6,7},{7,4},{8,9},{9,10},{10,1... | collective-permute-start | bytes 1376264 | tf_op jit(solution)/shard_map/ppermute | solution.py:94
  195.2 10.0 %collective-permute-start.7 = (bf16[128,1792]{1,0:T(8,128)(2,1)S(1)}, bf16[128,1792]{1,0:T(8,128)(2,1)S(1)}, u32[]{:S(2)}, u32[]{:S(2)}) collective-permute-start(bf16[128,1792]{1,0:T(8,128)(2,1)S(1)} %slice.51), channel_id=1, source_target_pairs={{0,3},{1,0},{2,1},{3,2},{4,7},{5,4},{6,5},{7,6},{8,11},{9,8},{10,9... | collective-permute-start | bytes 1376264 | tf_op jit(solution)/shard_map/ppermute | solution.py:94
  196.2 9.0 %copy-start.12 = (bf16[4,256,1024]{1,2,0:T(8,128)(2,1)S(1)}, bf16[4,256,1024]{1,2,0:T(8,128)(2,1)}, u32[]{:S(2)}) copy-start(bf16[4,256,1024]{1,2,0:T(8,128)(2,1)} %copy-done.11) | copy-start | bytes 6291460
  210.0 1.8 copy-start.10
  211.8 19.4 %collective-permute-start.8 = (bf16[256,1792]{1,0:T(8,128)(2,1)S(1)}, bf16[256,1792]{1,0:T(8,128)(2,1)S(1)}, u32[]{:S(2)}, u32[]{:S(2)}) collective-permute-start(bf16[256,1792]{1,0:T(8,128)(2,1)S(1)} %get-tuple-element.18), channel_id=1, source_target_pairs={{0,4},{1,5},{2,6},{3,7},{16,20},{17,21},{18,22},{19,23},{32,36},{3... | collective-permute-start | bytes 2752520 | tf_op jit(solution)/shard_map/ppermute | solution.py:164
  214.7 22.4 %collective-permute-start.11 = (bf16[256,1792]{1,0:T(8,128)(2,1)S(1)}, bf16[256,1792]{1,0:T(8,128)(2,1)}, u32[]{:S(2)}, u32[]{:S(2)}) collective-permute-start(bf16[256,1792]{1,0:T(8,128)(2,1)S(1)} %get-tuple-element.19), channel_id=1, source_target_pairs={{12,8},{13,9},{14,10},{15,11},{28,24},{29,25},{30,26},{31,27},{44,... | collective-permute-start | bytes 2752520 | tf_op jit(solution)/shard_map/ppermute | solution.py:165
  232.6 20.0 %collective-permute-start.9 = (bf16[256,1792]{1,0:T(8,128)(2,1)S(1)}, bf16[256,1792]{1,0:T(8,128)(2,1)S(1)}, u32[]{:S(2)}, u32[]{:S(2)}) collective-permute-start(bf16[256,1792]{1,0:T(8,128)(2,1)S(1)} %fusion.21), channel_id=1, source_target_pairs={{0,4},{4,8},{1,5},{5,9},{2,6},{6,10},{3,7},{7,11},{16,20},{20,24},... | collective-permute-start | bytes 2752520 | tf_op jit(solution)/shard_map/ppermute | solution.py:164
  254.8 6.6 %collective-permute-start.12 = (bf16[256,1792]{1,0:T(8,128)(2,1)S(1)}, bf16[256,1792]{1,0:T(8,128)(2,1)S(1)}, u32[]{:S(2)}, u32[]{:S(2)}) collective-permute-start(bf16[256,1792]{1,0:T(8,128)(2,1)S(1)} %get-tuple-element.17), channel_id=1, source_target_pairs={{8,4},{12,8},{9,5},{13,9},{10,6},{14,10},{11,7},{15,11},{24,20},{2... | collective-permute-start | bytes 2752520 | tf_op jit(solution)/shard_map/ppermute | solution.py:165
  255.6 15.9 %collective-permute-start.10 = (bf16[256,1792]{1,0:T(8,128)(2,1)S(1)}, bf16[256,1792]{1,0:T(8,128)(2,1)}, u32[]{:S(2)}, u32[]{:S(2)}) collective-permute-start(bf16[256,1792]{1,0:T(8,128)(2,1)S(1)} %get-tuple-element.16), channel_id=1, source_target_pairs={{0,4},{4,8},{8,12},{1,5},{5,9},{9,13},{2,6},{6,10},{10,14},{3,7},{... | collective-permute-start | bytes 2752520 | tf_op jit(solution)/shard_map/ppermute | solution.py:164
  262.9 31.6 %collective-permute-start.13 = (bf16[256,1792]{1,0:T(8,128)(2,1)S(1)}, bf16[256,1792]{1,0:T(8,128)(2,1)S(1)}, u32[]{:S(2)}, u32[]{:S(2)}) collective-permute-start(bf16[256,1792]{1,0:T(8,128)(2,1)S(1)} %fusion.20), channel_id=1, source_target_pairs={{4,0},{8,4},{12,8},{5,1},{9,5},{13,9},{6,2},{10,6},{14,10},{7,3},{... | collective-permute-start | bytes 2752520 | tf_op jit(solution)/shard_map/ppermute | solution.py:165
  264.2 33.0 %copy-start.1 = (s32[1,16]{1,0:T(1,128)S(1)}, s32[1,16]{1,0:T(1,128)}, u32[]{:S(2)}) copy-start(s32[1,16]{1,0:T(1,128)} %param.14) | copy-start | bytes 196

commit v2 on v1

v2 whole, which is shorter than its diff:
```python
import jax
import jax.numpy as jnp
from jax import lax
from jax.experimental import pallas as pl
from jax.experimental.pallas import tpu as pltpu
from jax.sharding import Mesh
from jax.sharding import PartitionSpec as P

TILE = 128
SIDE = 4
OUTER_RATE = 0.7
OUTER_MU = 0.9
VMEM = pl.BlockSpec(memory_space=pltpu.VMEM)
SMEM = pl.BlockSpec(memory_space=pltpu.SMEM)


def pick_kernel(chosen_ref, outer_ref, local_ref, picked_ref):
    across = outer_ref.shape[1] // TILE
    for i in range(picked_ref.shape[0]):
        tile = chosen_ref[0, i]
        row = pl.multiple_of(tile // across * TILE, TILE)
        col = pl.multiple_of(tile % across * TILE, TILE)
        at = (pl.ds(row, TILE), pl.ds(col, TILE))
        delta = outer_ref[at].astype(jnp.float32) - local_ref[at].astype(jnp.float32)
        picked_ref[i] = delta.astype(jnp.bfloat16)


def pick_tiles(chosen, outer, local_rows):
    count = chosen.shape[1]
    return pl.pallas_call(
        pick_kernel,
        out_shape=jax.ShapeDtypeStruct((count, TILE, TILE), jnp.bfloat16),
        in_specs=[SMEM, VMEM, VMEM],
        out_specs=VMEM,
        compiler_params=pltpu.CompilerParams(vmem_limit_bytes=16 * 2**20),
        cost_estimate=pl.CostEstimate(flops=count * TILE * TILE, bytes_accessed=3 * 2**20, transcendentals=0),
        name="pick_tiles",
    )(chosen, outer, local_rows)


def step_kernel(chosen_ref, outer_ref, local_ref, moment_ref, moved_ref, moment_out, theta_out, place):
    across = outer_ref.shape[1] // TILE
    half = pl.program_id(0)

    @pl.when(half == 0)
    def _():
        for t in range(place.shape[0]):
            place[t] = -1
        for i in range(moved_ref.shape[0]):
            place[chosen_ref[0, i]] = i

    for col in range(across):
        at = (slice(None), slice(col * TILE, (col + 1) * TILE))
        found = place[half * across + col]
        outer = outer_ref[at].astype(jnp.float32)
        delta = (outer - local_ref[at].astype(jnp.float32)).astype(jnp.bfloat16).astype(jnp.float32)
        other = moved_ref[jnp.maximum(found, 0)].astype(jnp.float32)
        mixed = jnp.where(found >= 0, 0.5 * (delta + other), delta)
        moment = OUTER_MU * moment_ref[at] + mixed
        moment_out[at] = moment
        theta_out[at] = (outer - OUTER_RATE * (mixed + OUTER_MU * moment)).astype(jnp.bfloat16)


def outer_step(chosen, outer, local_rows, moment, moved):
    rows, width = outer.shape
    block = pl.BlockSpec((TILE, width), lambda i: (i, 0))
    tiles = pl.BlockSpec(moved.shape, lambda i: (0, 0, 0))
    return pl.pallas_call(
        step_kernel,
        grid=(rows // TILE,),
        out_shape=[
            jax.ShapeDtypeStruct((rows, width), jnp.float32),
            jax.ShapeDtypeStruct((rows, width), jnp.bfloat16),
        ],
        in_specs=[SMEM, block, block, block, tiles],
        out_specs=[block, block],
        scratch_shapes=[pltpu.SMEM((rows // TILE * (width // TILE),), jnp.int32)],
        compiler_params=pltpu.CompilerParams(vmem_limit_bytes=24 * 2**20),
        cost_estimate=pl.CostEstimate(flops=8 * rows * width, bytes_accessed=14 * rows * width, transcendentals=0),
        name="outer_step",
    )(chosen, outer, local_rows, moment, moved)


def regroup_kernel(where_ref, cot_ref, own_ref, up_ref, down_ref):
    rows = own_ref.shape[0]
    half = rows // 2
    piece = own_ref.shape[1] // SIDE
    for k in range(SIDE):
        group = (where_ref[0] + k) % SIDE * SIDE
        to = slice(k * piece, (k + 1) * piece)
        for by in range(SIDE):
            start = pl.multiple_of((group + (where_ref[1] + by) % SIDE) * piece, piece)
            value = cot_ref[:, pl.ds(start, piece)]
            if by == 0:
                own_ref[:, to] = value
            elif by == 1:
                up_ref[:rows, to] = value
            elif by == 2:
                up_ref[rows:, to] = value[:half]
                down_ref[rows:, to] = value[half:]
            else:
                down_ref[:rows, to] = value


def regroup(where, cot_rows):
    rows, depth = cot_rows.shape
    width = depth // SIDE
    sizes = (rows, rows + rows // 2, rows + rows // 2)
    return pl.pallas_call(
        regroup_kernel,
        out_shape=[jax.ShapeDtypeStruct((n, width), jnp.bfloat16) for n in sizes],
        in_specs=[SMEM, VMEM],
        out_specs=[VMEM] * 3,
        compiler_params=pltpu.CompilerParams(vmem_limit_bytes=16 * 2**20),
        cost_estimate=pl.CostEstimate(flops=0, bytes_accessed=4 * rows * depth, transcendentals=0),
        name="regroup",
    )(where, cot_rows)


def tie(*values):
    return lax.optimization_barrier(values)


def turn(value, by):
    return lax.ppermute(value, "x", [(i, (i + by) % SIDE) for i in range(SIDE)])


def up_line(value, step):
    return lax.ppermute(value, "z", [(i, i + 1) for i in range(*step)])


def down_line(value, step):
    return lax.ppermute(value, "z", [(SIDE - 1 - i, SIDE - 2 - i) for i in range(*step)])


def add(a, b):
    return (a.astype(jnp.float32) + b.astype(jnp.float32)).astype(jnp.bfloat16)


def local(theta_outer, theta_local, momentum, gate_pre, up_pre, cotangent, partner, chosen):
    outer, local_rows, moment = theta_outer[0], theta_local[0], momentum[0]
    rows, width = outer.shape
    half = rows // 2
    scale = width ** (-0.5)
    z, x = lax.axis_index("z"), lax.axis_index("x")
    my_rep = lax.axis_index("rep")
    replicas = lax.axis_size("rep")
    offset = jnp.bitwise_xor(partner[0, my_rep], my_rep)

    def to_partner(by):
        return lambda value: lax.ppermute(value, "rep", [(i, i ^ by) for i in range(replicas)])

    gval = gate_pre[0].astype(jnp.float32)
    uval = up_pre[0].astype(jnp.float32)
    hidden = (gval * jax.nn.sigmoid(gval) * uval).astype(jnp.bfloat16)
    cot_own, cot_up, cot_down = regroup(jnp.stack([z, x]).astype(jnp.int32), cotangent[0])
    picked = pick_tiles(chosen, outer, local_rows)
    picked, hidden, cot_up, cot_down = tie(picked, hidden, cot_up, cot_down)
    hid_left, hid_right = turn(hidden, 1), turn(hidden, -1)
    cot_left, cot_right = turn(cot_up, 1), turn(cot_down, -1)

    moved = lax.switch(offset - 1, [to_partner(by) for by in range(1, replicas)], picked)
    moved, hid_left, hid_right, cot_left, cot_right = tie(moved, hid_left, hid_right, cot_left, cot_right)
    hid_top, hid_low = turn(hid_left[:half], 1), turn(hid_right[half:], -1)
    cot_top, cot_low = turn(cot_left[rows:], 1), turn(cot_right[rows:], -1)
    momentum_new, theta_new = outer_step(chosen, outer, local_rows, moment, moved)
    up1, down1 = up_line(theta_new, (0, 3)), down_line(theta_new, (0, 3))

    cot = jnp.concatenate([cot_own, cot_right[:rows], cot_top, cot_low, cot_left[:rows]], axis=0)
    hid = jnp.concatenate([hidden, hid_right, hid_top, hid_low, hid_left], axis=0)
    part = lax.dot_general(cot, hid, (((0,), (0,)), ((), ())), preferred_element_type=jnp.float32)
    part = (scale * part).astype(jnp.bfloat16).reshape(SIDE, rows, width)
    up1, down1, part = tie(up1, down1, part)

    up2, down2 = up_line(up1, (1, 3)), down_line(down1, (1, 3))
    sum_up, sum_down = up_line(part[3], (0, 1)), down_line(part[1], (0, 1))
    near = jnp.concatenate([theta_new, down1, up1], axis=0)
    cols = [cot[:, k * rows : (k + 1) * rows] for k in range(SIDE)]
    total = jnp.dot(
        jnp.concatenate([cols[0], cols[1], cols[3]], axis=1), near, preferred_element_type=jnp.float32
    )
    sum_up, sum_down = add(part[2], sum_up), add(part[2], sum_down)
    up2, down2, sum_up, sum_down, total = tie(up2, down2, sum_up, sum_down, total)

    up3, down3 = up_line(up2, (2, 3)), down_line(down2, (2, 3))
    sum_up, sum_down = up_line(sum_up, (0, 2)), down_line(sum_down, (0, 2))
    total = total + jnp.dot(cols[2], jnp.where(z >= 2, up2, down2), preferred_element_type=jnp.float32)
    sum_up, sum_down = add(part[1], sum_up), add(part[3], sum_down)
    up3, down3, sum_up, sum_down, total = tie(up3, down3, sum_up, sum_down, total)

    sum_up, sum_down = up_line(sum_up, (0, 3)), down_line(sum_down, (0, 3))
    far = jnp.where(z == 0, cols[3], cols[1])
    total = total + jnp.dot(far, jnp.where(z == 0, down3, up3), preferred_element_type=jnp.float32)
    share = (scale * total).astype(jnp.bfloat16).reshape(SIDE, rows, width)
    left, right = turn(share[2, :half], 1), turn(share[2, half:], -1)
    ahead = jnp.concatenate([add(share[1, :half], left), share[1, half:]], axis=0)
    behind = jnp.concatenate([share[3, :half], add(share[3, half:], right)], axis=0)
    left, right = turn(ahead, 1), turn(behind, -1)
    grad_hidden = share[0].astype(jnp.float32) + left.astype(jnp.float32) + right.astype(jnp.float32)
    sig = jax.nn.sigmoid(gval)
    grad_gate = (grad_hidden * uval * sig * (1.0 + gval * (1.0 - sig))).astype(jnp.bfloat16)
    grad_up = (grad_hidden * (gval * sig)).astype(jnp.bfloat16)
    grad_weight = part[0].astype(jnp.float32) + sum_up.astype(jnp.float32) + sum_down.astype(jnp.float32)
    return momentum_new[None], grad_weight.astype(jnp.bfloat16)[None], grad_gate[None], grad_up[None]


def solution(mesh):
    replicas, shards = mesh.devices.shape
    grid = Mesh(mesh.devices.reshape(replicas, shards // SIDE, SIDE), ("rep", "z", "x"))
    rows = P("rep", ("z", "x"), None)
    per_shard = P(("z", "x"), None)
    return jax.shard_map(
        local,
        mesh=grid,
        in_specs=(rows,) * 6 + (per_shard,) * 2,
        out_specs=(rows,) * 4,
        check_vma=False,
    )
```

time: 298 us -> 183 us (0.61)
  waiting for transfers between devices: 170 us -> 84.8 us
  starting transfers between devices: 61.2 us -> 36.9 us
  local copies, waits for them, and re-layouts: 29.3 us -> 12.8 us
  other arithmetic: 14.3 us -> 25 us
  matrix products: 17.8 us -> 14.6 us
  Pallas kernels: 3.09 us -> 6.11 us
    ppermute x24 -> x25, waiting for transfers between devices: 170 us -> 84.8 us  [the longest x12 58 us: turn(): return lax.ppermute(value, 'x', [(i, (i + by) % SIDE) for i in range(SIDE)])]
    ppermute x24 -> x25, starting transfers between devices: 56.5 us -> 36.9 us  [the longest x6 16.9 us: up_line(): return lax.ppermute(value, 'z', [(i, i + 1) for i in range(*step)])]
    another operation x3 -> x0, local copies, waits for them, and re-layouts: 9.41 us -> none  [the longest x2 6.08 us: swap_columns(): cot_rows.reshape(rows, SIDE, SIDE, piece).transpose(2, 0, 1, 3)]
    convert_element_type x0 -> x2, other arithmetic: none -> 7.48 us  [the longest x1 4.55 us: local(): share = (scale * total).astype(jnp.bfloat16).reshape(SIDE, rows, width)]
    add x0 -> x1, other arithmetic: none -> 7.47 us  [local(): total + jnp.dot(cols[2], jnp.where(z >= 2, up2, down2), preferred_element...]
    dynamic_slice x1 -> x0, local copies, waits for them, and re-layouts: 5.17 us -> none  [local(): lax.dynamic_index_in_dim(columns, (z - far) % SIDE, 1, keepdims=False)]
    all_to_all x1 -> x0, starting transfers between devices: 4.77 us -> none  [swap_columns(): lax.all_to_all(blocks, 'x', split_axis=0, concat_axis=0, tiled=True)]
    unnamed x34 -> x36, local copies, waits for them, and re-layouts: 8.54 us -> 5.47 us
  transfers between devices with their start and end apart: 25 -> 25, of which waited for: 19 -> 16; matrix products, arithmetic and copies ran while one was open for 11% -> 21% of each run, Pallas kernels for 0% -> 0%
where the time goes in v2:
time: 183 us; the launch traced here: 182 us
  waiting for transfers between devices  84.8 us (46%)
  starting transfers between devices  36.9 us (20%)
  other arithmetic  25 us (14%)
  matrix products  14.6 us (8%)
  local copies, waits for them, and re-layouts  12.8 us (7%)
  Pallas kernels  6.11 us (3%)
    ppermute x12, waiting for transfers between devices, turn(): return lax.ppermute(value, 'x', [(i, (i + by) % SIDE) for i in range(SIDE)])  58 us
    ppermute x6, starting transfers between devices, up_line(): return lax.ppermute(value, 'z', [(i, i + 1) for i in range(*step)])  16.9 us
    ppermute x6, waiting for transfers between devices, down_line(): lax.ppermute(value, 'z', [(SIDE - 1 - i, SIDE - 2 - i) for i in range(*st...  14.1 us
    ppermute x12, starting transfers between devices, turn(): return lax.ppermute(value, 'x', [(i, (i + by) % SIDE) for i in range(SIDE)])  12.3 us
    ppermute x6, waiting for transfers between devices, up_line(): return lax.ppermute(value, 'z', [(i, i + 1) for i in range(*step)])  10.5 us
    ppermute x6, starting transfers between devices, down_line(): lax.ppermute(value, 'z', [(SIDE - 1 - i, SIDE - 2 - i) for i in range(*st...  7.7 us
    add x1, other arithmetic, local(): total + jnp.dot(cols[2], jnp.where(z >= 2, up2, down2), preferred_element...  7.47 us
    unnamed x36, local copies, waits for them, and re-layouts  5.47 us
  transfers between devices with their start and end apart: 25, of which 16 were waited for; matrix products, arithmetic and copies ran while one was open for 21% of the time, Pallas kernels for 0%

profile of v2, /device:TPU:6, one launch (start us, length us, event | category | flops | bytes accessed | tf_op | source)
XLA Modules:
  0.0 181.9 jit_solution(3335291891601831042)
XLA Ops:
  0.7 1.6 copy-done.4
  2.3 1.7 regroup.1
  4.1 2.9 %fusion.8 = bf16[256,1792]{1,0:T(8,128)(2,1)} fusion(bf16[1,256,1792]{2,1,0:T(8,128)(2,1)} %param.27, bf16[1,256,1792]{2,1,0:T(8,128)(2,1)} %param.26), kind=kLoop, calls=%fused_computation.17 | loop fusion | flops 3670016 | bytes 2752512 | tf_op jit(solution)/shard_map/convert_element_type | solution.py:155
  7.0 1.4 pick_tiles.1
  8.4 2.2 %collective-permute-start.15 = (bf16[256,1792]{1,0:T(8,128)(2,1)}, bf16[256,1792]{1,0:T(8,128)(2,1)}, u32[]{:S(2)}, u32[]{:S(2)}) collective-permute-start(bf16[256,1792]{1,0:T(8,128)(2,1)} %fusion.8), channel_id=1, source_target_pairs={{0,1},{1,2},{2,3},{3,0},{4,5},{5,6},{6,7},{7,4},{8,9},{9,10},{10,1... | collective-permute-start | bytes 2752520 | tf_op jit(solution)/shard_map/ppermute | solution.py:125
  10.7 3.2 %collective-permute-start.17 = (bf16[384,1024]{1,0:T(8,128)(2,1)}, bf16[384,1024]{1,0:T(8,128)(2,1)}, u32[]{:S(2)}, u32[]{:S(2)}) collective-permute-start(bf16[384,1024]{1,0:T(8,128)(2,1)} %get-tuple-element.66), channel_id=1, source_target_pairs={{0,1},{1,2},{2,3},{3,0},{4,5},{5,6},{6,7},{7,4},{8,9},{9,10},{10,1... | collective-permute-start | bytes 2359304 | tf_op jit(solution)/shard_map/ppermute | solution.py:125
  13.9 0.6 constant_dynamic-slice_fusion
  15.1 2.3 %conditional.1 = (bf16[14,128,128]{2,1,0:T(8,128)(2,1)}) conditional(s32[]{:T(128)} %clamp.3, bf16[14,128,128]{2,1,0:T(8,128)(2,1)} %pick_tiles.1, bf16[14,128,128]{2,1,0:T(8,128)(2,1)} %pick_tiles.1, bf16[14,128,128]{2,1,0:T(8,128)(2,1)} %pick_tiles.1, bf16[14,128,128]{2,1,0:T(8,128)(2,1)} %pick_tiles.1, ...), branch_computations={%region_0.0_spmd, %region_1.0_spmd, %region_2.0_spmd, %region_3.0_... | conditional | bytes 1835056 | solution.py:162
  15.3 2.1 %collective-permute-done = bf16[14,128,128]{2,1,0:T(8,128)(2,1)} collective-permute-done((bf16[14,128,128]{2,1,0:T(8,128)(2,1)}, bf16[14,128,128]{2,1,0:T(8,128)(2,1)}, u32[]{:S(2)}, u32[]{:S(2)}) %collective-permute-start) | collective-permute-done | bytes 458784 | tf_op jit(solution)/shard_map/cond/branch_0_fun/ppermute | solution.py:151
  17.4 1.4 constant_dynamic-update-slice_fusion.7
  18.8 28.9 %collective-permute-done.17 = bf16[384,1024]{1,0:T(8,128)(2,1)} collective-permute-done((bf16[384,1024]{1,0:T(8,128)(2,1)}, bf16[384,1024]{1,0:T(8,128)(2,1)}, u32[]{:S(2)}, u32[]{:S(2)}) %collective-permute-start.17) | collective-permute-done | bytes 786464 | tf_op jit(solution)/shard_map/ppermute | solution.py:125
  47.7 1.2 collective-permute-done.18
  48.9 2.9 %outer_step.1 = (f32[256,1792]{1,0:T(8,128)}, bf16[256,1792]{1,0:T(8,128)(2,1)S(1)}) custom-call(s32[1,14]{1,0:T(1,128)S(1)} %copy-done.6, bf16[256,1792]{1,0:T(8,128)(2,1)S(1)} %bitcast.68, bf16[256,1792]{1,0:T(8,128)(2,1)S(1)} %bitcast.70, f32[256,1792]{1,0:T(8,128)S(1)} %bitcast.72, bf16[14,128,128]{2,1,0:T(8,128)(2,1)} %get-tuple-element.103.moved_ref), custom_call_target="tpu_custom_call" | custom-call | flops 3670016 | bytes 6422528 | tf_op jit(solution)/shard_map/outer_step/pallas_call | solution.py:68
  51.9 4.1 %collective-permute-start.19 = (bf16[256,1792]{1,0:T(8,128)(2,1)S(1)}, bf16[256,1792]{1,0:T(8,128)(2,1)S(1)}, u32[]{:S(2)}, u32[]{:S(2)}) collective-permute-start(bf16[256,1792]{1,0:T(8,128)(2,1)S(1)} %get-tuple-element.70), channel_id=1, source_target_pairs={{0,4},{4,8},{8,12},{1,5},{5,9},{9,13},{2,6},{6,10},{10,14},{3,7},{... | collective-permute-start | bytes 2752520 | tf_op jit(solution)/shard_map/ppermute | solution.py:129
  55.9 1.3 collective-permute-start.20
  57.2 1.1 slice.73
  58.3 1.0 slice.69
  59.3 0.4 collective-permute-start.21
  59.6 1.2 constant_dynamic-update-slice_fusion.6
  60.9 1.0 slice.72
  61.9 1.6 collective-permute-start.23
  63.5 1.0 slice.70
  64.4 0.6 collective-permute-start.22
  65.1 1.1 slice_dynamic-update-slice_fusion.1
  66.2 2.4 %collective-permute-done.21 = bf16[128,1024]{1,0:T(8,128)(2,1)S(1)} collective-permute-done((bf16[128,1024]{1,0:T(8,128)(2,1)S(1)}, bf16[128,1024]{1,0:T(8,128)(2,1)S(1)}, u32[]{:S(2)}, u32[]{:S(2)}) %collective-permute-start.21) | collective-permute-done | bytes 262176 | tf_op jit(solution)/shard_map/ppermute | solution.py:125
  68.6 6.4 %collective-permute-done.22 = bf16[128,1024]{1,0:T(8,128)(2,1)S(1)} collective-permute-done((bf16[128,1024]{1,0:T(8,128)(2,1)S(1)}, bf16[128,1024]{1,0:T(8,128)(2,1)S(1)}, u32[]{:S(2)}, u32[]{:S(2)}) %collective-permute-start.22) | collective-permute-done | bytes 262176 | tf_op jit(solution)/shard_map/ppermute | solution.py:125
  75.0 1.1 slice_dynamic-update-slice_fusion
  76.1 5.4 %collective-permute-done.24 = bf16[128,1792]{1,0:T(8,128)(2,1)S(1)} collective-permute-done((bf16[128,1792]{1,0:T(8,128)(2,1)S(1)}, bf16[128,1792]{1,0:T(8,128)(2,1)S(1)}, u32[]{:S(2)}, u32[]{:S(2)}) %collective-permute-start.24) | collective-permute-done | bytes 458784 | tf_op jit(solution)/shard_map/ppermute | solution.py:125
  81.6 1.2 constant_dynamic-update-slice_fusion.3
  82.9 4.3 %multiply_convert_fusion.1 = bf16[1024,1792]{1,0:T(8,128)(2,1)S(1)} fusion(bf16[1024,1024]{1,0:T(8,128)(2,1)S(1)} %slice_dynamic-update-slice_fusion, bf16[1024,1792]{1,0:T(8,128)(2,1)S(1)} %constant_dynamic-update-slice_fusion.3), kind=kOutput, calls=%fused_computation.1 | convolution fusion | flops 3761766400 | bytes 9437184 | tf_op jit(solution)/shard_map/dot_general | solution.py:171
  87.3 4.5 %collective-permute-start.27 = (bf16[256,1792]{1,0:T(8,128)(2,1)S(1)}, bf16[256,1792]{1,0:T(8,128)(2,1)S(1)}, u32[]{:S(2)}, u32[]{:S(2)}) collective-permute-start(bf16[256,1792]{1,0:T(8,128)(2,1)S(1)} %get-tuple-element.102), channel_id=1, source_target_pairs={{0,4},{1,5},{2,6},{3,7},{16,20},{17,21},{18,22},{19,23},{32,36},{3... | collective-permute-start | bytes 2752520 | tf_op jit(solution)/shard_map/ppermute | solution.py:129
  91.8 0.7 collective-permute-start.28
  92.7 0.7 collective-permute-start.25
  93.4 1.3 collective-permute-start.26
  94.7 5.5 %fusion = f32[1024,1792]{1,0:T(8,128)} fusion(bf16[256,1792]{1,0:T(8,128)(2,1)S(1)} %collective-permute-done.19, bf16[256,1792]{1,0:T(8,128)(2,1)S(1)} %collective-permute-done.20, bf16[256,1792]{1,0:T(8,128)(2,1)S(1)} %get-tuple-element.70, bf16[1024,256]{1,0:T(8,128)(2,1)S(1)} %slice.90, bf16[1024,512]{1,0:T(8,128)(2,1)S(1)} %slice.89), kind=kOutput, calls=%fused_computation.2 | convolution fusion | flops 2829975552 | bytes 11665408 | tf_op jit(solution)/shard_map/dot_general | solution.py:179
  100.2 8.0 %collective-permute-done.27 = bf16[256,1792]{1,0:T(8,128)(2,1)S(1)} collective-permute-done((bf16[256,1792]{1,0:T(8,128)(2,1)S(1)}, bf16[256,1792]{1,0:T(8,128)(2,1)S(1)}, u32[]{:S(2)}, u32[]{:S(2)}) %collective-permute-start.27) | collective-permute-done | bytes 917536 | tf_op jit(solution)/shard_map/ppermute | solution.py:129
  108.2 1.6 fusion.7
  109.8 5.0 %collective-permute-done.26 = bf16[256,1792]{1,0:T(8,128)(2,1)S(1)} collective-permute-done((bf16[256,1792]{1,0:T(8,128)(2,1)S(1)}, bf16[256,1792]{1,0:T(8,128)(2,1)S(1)}, u32[]{:S(2)}, u32[]{:S(2)}) %collective-permute-start.26) | collective-permute-done | bytes 917536 | tf_op jit(solution)/shard_map/ppermute | solution.py:133
  114.8 4.6 %collective-permute-start.31 = (bf16[256,1792]{1,0:T(8,128)(2,1)}, bf16[256,1792]{1,0:T(8,128)(2,1)}, u32[]{:S(2)}, u32[]{:S(2)}) collective-permute-start(bf16[256,1792]{1,0:T(8,128)(2,1)} %get-tuple-element.81), channel_id=1, source_target_pairs={{0,4},{4,8},{1,5},{5,9},{2,6},{6,10},{3,7},{7,11},{16,20},{20,24},... | collective-permute-start | bytes 2752520 | tf_op jit(solution)/shard_map/ppermute | solution.py:129
  119.4 1.6 collective-permute-start.32
  121.0 1.6 collective-permute-start.29
  122.6 1.5 collective-permute-start.30
  124.1 2.2 %fusion.27 = f32[1024,1792]{1,0:T(8,128)S(1)} fusion(bf16[256,1792]{1,0:T(8,128)(2,1)S(1)} %collective-permute-done.25, bf16[256,1792]{1,0:T(8,128)(2,1)S(1)} %collective-permute-done.26, pred[]{:T(512)S(6)} %ge.3, bf16[1024,1024]{1,0:T(8,128)(2,1)} %copy-done.9), kind=kOutput, calls=%fused_computation.45 | convolution fusion | flops 939982848 | bytes 9699329 | tf_op jit(solution)/shard_map/dot_general | solution.py:187
  126.3 7.5 %add.53 = f32[1024,1792]{1,0:T(8,128)} add(f32[1024,1792]{1,0:T(8,128)} %fusion, f32[1024,1792]{1,0:T(8,128)S(1)} %fusion.27) | non-fusion elementwise | flops 1835008 | bytes 22020096 | tf_op jit(solution)/shard_map/add | solution.py:187
  133.8 0.3 collective-permute-done.31
  134.1 3.1 %add_convert_fusion = (bf16[256,1792]{1,0:T(8,128)(2,1)}, bf16[256,1792]{1,0:T(8,128)(2,1)}) fusion(bf16[256,1792]{1,0:T(8,128)(2,1)} %collective-permute-done.32, bf16[4,256,1792]{2,1,0:T(8,128)(2,1)S(1)} %bitcast.78, bf16[256,1792]{1,0:T(8,128)(2,1)} %collective-permute-done.31), kind=kLoop, calls=%fused_computation.30 | loop fusion | flops 3670016 | bytes 5505024 | tf_op jit(solution)/shard_map/convert_element_type | solution.py:137
  137.2 4.9 %collective-permute-done.30 = bf16[256,1792]{1,0:T(8,128)(2,1)} collective-permute-done((bf16[256,1792]{1,0:T(8,128)(2,1)S(1)}, bf16[256,1792]{1,0:T(8,128)(2,1)}, u32[]{:S(2)}, u32[]{:S(2)}) %collective-permute-start.30) | collective-permute-done | bytes 917536 | tf_op jit(solution)/shard_map/ppermute | solution.py:133
  142.2 2.7 %fusion.25 = f32[1024,1792]{1,0:T(8,128)S(1)} fusion(bf16[256,1792]{1,0:T(8,128)(2,1)} %collective-permute-done.30, bf16[256,1792]{1,0:T(8,128)(2,1)} %collective-permute-done.29, pred[]{:T(512)S(6)} %eq.4, bf16[1024,1024]{1,0:T(8,128)(2,1)} %copy-done.9), kind=kOutput, calls=%fused_computation.43 | convolution fusion | flops 940244992 | bytes 10224640 | tf_op jit(solution)/shard_map/dot_general | solution.py:193
  144.9 4.5 %multiply_convert_fusion = bf16[1024,1792]{1,0:T(8,128)(2,1)S(1)} fusion(f32[1024,1792]{1,0:T(8,128)} %add.53, f32[1024,1792]{1,0:T(8,128)S(1)} %fusion.25), kind=kLoop, calls=%fused_computation | loop fusion | flops 5505024 | bytes 18350080 | tf_op jit(solution)/shard_map/convert_element_type | solution.py:194
  149.6 0.5 collective-permute-start.35
  150.1 1.6 collective-permute-start.37
  151.7 1.4 collective-permute-start.33
  153.1 1.3 collective-permute-start.34
  154.4 5.8 %collective-permute-done.35 = bf16[128,1792]{1,0:T(8,128)(2,1)S(1)} collective-permute-done((bf16[128,1792]{1,0:T(8,128)(2,1)S(1)}, bf16[128,1792]{1,0:T(8,128)(2,1)S(1)}, u32[]{:S(2)}, u32[]{:S(2)}) %collective-permute-start.35) | collective-permute-done | bytes 458784 | tf_op jit(solution)/shard_map/ppermute | solution.py:125
  160.3 2.0 %collective-permute-done.37 = bf16[128,1792]{1,0:T(8,128)(2,1)S(1)} collective-permute-done((bf16[128,1792]{1,0:T(8,128)(2,1)S(1)}, bf16[128,1792]{1,0:T(8,128)(2,1)S(1)}, u32[]{:S(2)}, u32[]{:S(2)}) %collective-permute-start.37) | collective-permute-done | bytes 458784 | tf_op jit(solution)/shard_map/ppermute | solution.py:125
  162.2 0.2 fusion.24
  162.5 0.2 collective-permute-start.36
  162.8 2.0 %collective-permute-start.38 = (bf16[256,1792]{1,0:T(8,128)(2,1)S(1)}, bf16[256,1792]{1,0:T(8,128)(2,1)S(1)}, u32[]{:S(2)}, u32[]{:S(2)}) collective-permute-start(bf16[256,1792]{1,0:T(8,128)(2,1)S(1)} %pad_maximum_fusion.1), channel_id=1, source_target_pairs={{0,3},{1,0},{2,1},{3,2},{4,7},{5,4},{6,5},{7,6},{8,11},{9,8},{10,9... | collective-permute-start | bytes 2752520 | tf_op jit(solution)/shard_map/ppermute | solution.py:125
  164.8 2.1 %collective-permute-done.33 = bf16[256,1792]{1,0:T(8,128)(2,1)S(1)} collective-permute-done((bf16[256,1792]{1,0:T(8,128)(2,1)S(1)}, bf16[256,1792]{1,0:T(8,128)(2,1)S(1)}, u32[]{:S(2)}, u32[]{:S(2)}) %collective-permute-start.33) | collective-permute-done | bytes 917536 | tf_op jit(solution)/shard_map/ppermute | solution.py:129
  166.9 4.2 %collective-permute-done.34 = bf16[256,1792]{1,0:T(8,128)(2,1)S(1)} collective-permute-done((bf16[256,1792]{1,0:T(8,128)(2,1)S(1)}, bf16[256,1792]{1,0:T(8,128)(2,1)S(1)}, u32[]{:S(2)}, u32[]{:S(2)}) %collective-permute-start.34) | collective-permute-done | bytes 917536 | tf_op jit(solution)/shard_map/ppermute | solution.py:133
  171.1 2.4 %fusion.22 = bf16[1,256,1792]{2,1,0:T(8,128)(2,1)} fusion(bf16[256,1792]{1,0:T(8,128)(2,1)S(1)} %collective-permute-done.34, bf16[256,1792]{1,0:T(8,128)(2,1)S(1)} %collective-permute-done.33, bf16[4,256,1792]{2,1,0:T(8,128)(2,1)} %bitcast.77), kind=kLoop, calls=%fused_computation.36 | loop fusion | flops 2752512 | bytes 3670016 | tf_op jit(solution)/shard_map/broadcast_in_dim | solution.py:204
  173.6 4.2 %collective-permute-done.36 = bf16[256,1792]{1,0:T(8,128)(2,1)S(1)} collective-permute-done((bf16[256,1792]{1,0:T(8,128)(2,1)S(1)}, bf16[256,1792]{1,0:T(8,128)(2,1)S(1)}, u32[]{:S(2)}, u32[]{:S(2)}) %collective-permute-start.36) | collective-permute-done | bytes 917536 | tf_op jit(solution)/shard_map/ppermute | solution.py:125
  177.8 1.7 collective-permute-done.38
  179.5 2.5 %fusion.21 = (bf16[1,256,1792]{2,1,0:T(8,128)(2,1)}, bf16[1,256,1792]{2,1,0:T(8,128)(2,1)}) fusion(bf16[256,1792]{1,0:T(8,128)(2,1)S(1)} %collective-permute-done.38, bf16[256,1792]{1,0:T(8,128)(2,1)S(1)} %collective-permute-done.36, bf16[1024,1792]{1,0:T(8,128)(2,1)S(1)} %multiply_convert_fusion, bf16[1,256,1792]{2,1,0:T(8,128)(2,1)S(1)} %copy-done.11, ...), kind=kLoop, calls=%fused_computation.35 | loop fusion | flops 9175040 | bytes 6422528 | tf_op jit(solution)/shard_map/broadcast_in_dim | solution.py:204
  (52 shorter events, 0.9 us)
Async XLA Ops:
  0.6 13.3 %copy-start = (s32[1,16]{1,0:T(1,128)S(1)}, s32[1,16]{1,0:T(1,128)}, u32[]{:S(2)}) copy-start(s32[1,16]{1,0:T(1,128)} %param.29) | copy-start | bytes 196
  0.7 1.6 copy-start.4
  2.3 4.7 %copy-start.2 = (bf16[1,256,1792]{2,1,0:T(8,128)(2,1)S(1)}, bf16[1,256,1792]{2,1,0:T(8,128)(2,1)}, u32[]{:S(2)}) copy-start(bf16[1,256,1792]{2,1,0:T(8,128)(2,1)} %param.23) | copy-start | bytes 2752516
  2.3 4.7 %copy-start.3 = (bf16[1,256,1792]{2,1,0:T(8,128)(2,1)S(1)}, bf16[1,256,1792]{2,1,0:T(8,128)(2,1)}, u32[]{:S(2)}) copy-start(bf16[1,256,1792]{2,1,0:T(8,128)(2,1)} %param.24) | copy-start | bytes 2752516
  2.3 4.7 %copy-start.6 = (s32[1,14]{1,0:T(1,128)S(1)}, s32[1,14]{1,0:T(1,128)}, u32[]{:S(2)}) copy-start(s32[1,14]{1,0:T(1,128)} %chosen_ref.3) | copy-start | bytes 172
  8.4 40.5 %collective-permute-start.15 = (bf16[256,1792]{1,0:T(8,128)(2,1)}, bf16[256,1792]{1,0:T(8,128)(2,1)}, u32[]{:S(2)}, u32[]{:S(2)}) collective-permute-start(bf16[256,1792]{1,0:T(8,128)(2,1)} %fusion.8), channel_id=1, source_target_pairs={{0,1},{1,2},{2,3},{3,0},{4,5},{5,6},{6,7},{7,4},{8,9},{9,10},{10,1... | collective-permute-start | bytes 2752520 | tf_op jit(solution)/shard_map/ppermute | solution.py:125
  10.7 38.3 %collective-permute-start.16 = (bf16[256,1792]{1,0:T(8,128)(2,1)}, bf16[256,1792]{1,0:T(8,128)(2,1)}, u32[]{:S(2)}, u32[]{:S(2)}) collective-permute-start(bf16[256,1792]{1,0:T(8,128)(2,1)} %fusion.8), channel_id=1, source_target_pairs={{0,3},{1,0},{2,1},{3,2},{4,7},{5,4},{6,5},{7,6},{8,11},{9,8},{10,9... | collective-permute-start | bytes 2752520 | tf_op jit(solution)/shard_map/ppermute | solution.py:125
  10.7 37.0 %collective-permute-start.17 = (bf16[384,1024]{1,0:T(8,128)(2,1)}, bf16[384,1024]{1,0:T(8,128)(2,1)}, u32[]{:S(2)}, u32[]{:S(2)}) collective-permute-start(bf16[384,1024]{1,0:T(8,128)(2,1)} %get-tuple-element.66), channel_id=1, source_target_pairs={{0,1},{1,2},{2,3},{3,0},{4,5},{5,6},{6,7},{7,4},{8,9},{9,10},{10,1... | collective-permute-start | bytes 2359304 | tf_op jit(solution)/shard_map/ppermute | solution.py:125
  13.9 35.0 %collective-permute-start.18 = (bf16[384,1024]{1,0:T(8,128)(2,1)S(1)}, bf16[384,1024]{1,0:T(8,128)(2,1)}, u32[]{:S(2)}, u32[]{:S(2)}) collective-permute-start(bf16[384,1024]{1,0:T(8,128)(2,1)S(1)} %get-tuple-element.67), channel_id=1, source_target_pairs={{0,3},{1,0},{2,1},{3,2},{4,7},{5,4},{6,5},{7,6},{8,11},{9,8},{10,9... | collective-permute-start | bytes 2359304 | tf_op jit(solution)/shard_map/ppermute | solution.py:125
  15.1 2.2 %collective-permute-start = (bf16[14,128,128]{2,1,0:T(8,128)(2,1)}, bf16[14,128,128]{2,1,0:T(8,128)(2,1)}, u32[]{:S(2)}, u32[]{:S(2)}) collective-permute-start(bf16[14,128,128]{2,1,0:T(8,128)(2,1)} %param), channel_id=1, source_target_pairs={{0,16},{16,0},{32,48},{48,32},{64,80},{80,64},{96,112},{112,96},{1... | collective-permute-start | bytes 1376264 | tf_op jit(solution)/shard_map/cond/branch_0_fun/ppermute | solution.py:151
  17.4 31.5 %copy-start.5 = (f32[1,256,1792]{2,1,0:T(8,128)S(1)}, f32[1,256,1792]{2,1,0:T(8,128)}, u32[]{:S(2)}) copy-start(f32[1,256,1792]{2,1,0:T(8,128)} %param.25) | copy-start | bytes 5505028
  51.9 35.3 %collective-permute-start.19 = (bf16[256,1792]{1,0:T(8,128)(2,1)S(1)}, bf16[256,1792]{1,0:T(8,128)(2,1)S(1)}, u32[]{:S(2)}, u32[]{:S(2)}) collective-permute-start(bf16[256,1792]{1,0:T(8,128)(2,1)S(1)} %get-tuple-element.70), channel_id=1, source_target_pairs={{0,4},{4,8},{8,12},{1,5},{5,9},{9,13},{2,6},{6,10},{10,14},{3,7},{... | collective-permute-start | bytes 2752520 | tf_op jit(solution)/shard_map/ppermute | solution.py:129
  55.9 31.2 %collective-permute-start.20 = (bf16[256,1792]{1,0:T(8,128)(2,1)S(1)}, bf16[256,1792]{1,0:T(8,128)(2,1)S(1)}, u32[]{:S(2)}, u32[]{:S(2)}) collective-permute-start(bf16[256,1792]{1,0:T(8,128)(2,1)S(1)} %get-tuple-element.70), channel_id=1, source_target_pairs={{12,8},{8,4},{4,0},{13,9},{9,5},{5,1},{14,10},{10,6},{6,2},{15,11}... | collective-permute-start | bytes 2752520 | tf_op jit(solution)/shard_map/ppermute | solution.py:133
  59.3 9.3 %collective-permute-start.21 = (bf16[128,1024]{1,0:T(8,128)(2,1)S(1)}, bf16[128,1024]{1,0:T(8,128)(2,1)S(1)}, u32[]{:S(2)}, u32[]{:S(2)}) collective-permute-start(bf16[128,1024]{1,0:T(8,128)(2,1)S(1)} %slice.69), channel_id=1, source_target_pairs={{0,1},{1,2},{2,3},{3,0},{4,5},{5,6},{6,7},{7,4},{8,9},{9,10},{10,1... | collective-permute-start | bytes 786440 | tf_op jit(solution)/shard_map/ppermute | solution.py:125
  61.9 14.2 %collective-permute-start.23 = (bf16[128,1792]{1,0:T(8,128)(2,1)S(1)}, bf16[128,1792]{1,0:T(8,128)(2,1)S(1)}, u32[]{:S(2)}, u32[]{:S(2)}) collective-permute-start(bf16[128,1792]{1,0:T(8,128)(2,1)S(1)} %slice.72), channel_id=1, source_target_pairs={{0,1},{1,2},{2,3},{3,0},{4,5},{5,6},{6,7},{7,4},{8,9},{9,10},{10,1... | collective-permute-start | bytes 1376264 | tf_op jit(solution)/shard_map/ppermute | solution.py:125
  64.4 10.5 %collective-permute-start.22 = (bf16[128,1024]{1,0:T(8,128)(2,1)S(1)}, bf16[128,1024]{1,0:T(8,128)(2,1)S(1)}, u32[]{:S(2)}, u32[]{:S(2)}) collective-permute-start(bf16[128,1024]{1,0:T(8,128)(2,1)S(1)} %slice.70), channel_id=1, source_target_pairs={{0,3},{1,0},{2,1},{3,2},{4,7},{5,4},{6,5},{7,6},{8,11},{9,8},{10,9... | collective-permute-start | bytes 786440 | tf_op jit(solution)/shard_map/ppermute | solution.py:125
  68.6 13.0 %collective-permute-start.24 = (bf16[128,1792]{1,0:T(8,128)(2,1)S(1)}, bf16[128,1792]{1,0:T(8,128)(2,1)S(1)}, u32[]{:S(2)}, u32[]{:S(2)}) collective-permute-start(bf16[128,1792]{1,0:T(8,128)(2,1)S(1)} %slice.73), channel_id=1, source_target_pairs={{0,3},{1,0},{2,1},{3,2},{4,7},{5,4},{6,5},{7,6},{8,11},{9,8},{10,9... | collective-permute-start | bytes 1376264 | tf_op jit(solution)/shard_map/ppermute | solution.py:125
  76.1 16.5 %copy-start.9 = (bf16[1024,1024]{1,0:T(8,128)(2,1)}, bf16[1024,1024]{1,0:T(8,128)(2,1)S(1)}, u32[]{:S(2)}) copy-start(bf16[1024,1024]{1,0:T(8,128)(2,1)S(1)} %slice_dynamic-update-slice_fusion) | copy-start | bytes 6291460
  87.1 21.1 %copy-start.7 = (bf16[1024,1792]{1,0:T(8,128)(2,1)}, bf16[1024,1792]{1,0:T(8,128)(2,1)S(1)}, u32[]{:S(2)}) copy-start(bf16[1024,1792]{1,0:T(8,128)(2,1)S(1)} %multiply_convert_fusion.1) | copy-start | bytes 11010052
  87.3 20.9 %collective-permute-start.27 = (bf16[256,1792]{1,0:T(8,128)(2,1)S(1)}, bf16[256,1792]{1,0:T(8,128)(2,1)S(1)}, u32[]{:S(2)}, u32[]{:S(2)}) collective-permute-start(bf16[256,1792]{1,0:T(8,128)(2,1)S(1)} %get-tuple-element.102), channel_id=1, source_target_pairs={{0,4},{1,5},{2,6},{3,7},{16,20},{17,21},{18,22},{19,23},{32,36},{3... | collective-permute-start | bytes 2752520 | tf_op jit(solution)/shard_map/ppermute | solution.py:129
  91.8 16.4 %collective-permute-start.28 = (bf16[256,1792]{1,0:T(8,128)(2,1)S(1)}, bf16[256,1792]{1,0:T(8,128)(2,1)S(1)}, u32[]{:S(2)}, u32[]{:S(2)}) collective-permute-start(bf16[256,1792]{1,0:T(8,128)(2,1)S(1)} %get-tuple-element.101), channel_id=1, source_target_pairs={{12,8},{13,9},{14,10},{15,11},{28,24},{29,25},{30,26},{31,27},{44,... | collective-permute-start | bytes 2752520 | tf_op jit(solution)/shard_map/ppermute | solution.py:133
  92.7 17.1 %collective-permute-start.25 = (bf16[256,1792]{1,0:T(8,128)(2,1)S(1)}, bf16[256,1792]{1,0:T(8,128)(2,1)S(1)}, u32[]{:S(2)}, u32[]{:S(2)}) collective-permute-start(bf16[256,1792]{1,0:T(8,128)(2,1)S(1)} %collective-permute-done.19), channel_id=1, source_target_pairs={{4,8},{8,12},{5,9},{9,13},{6,10},{10,14},{7,11},{11,15},{20,24},{2... | collective-permute-start | bytes 2752520 | tf_op jit(solution)/shard_map/ppermute | solution.py:129
  93.4 21.4 %collective-permute-start.26 = (bf16[256,1792]{1,0:T(8,128)(2,1)S(1)}, bf16[256,1792]{1,0:T(8,128)(2,1)S(1)}, u32[]{:S(2)}, u32[]{:S(2)}) collective-permute-start(bf16[256,1792]{1,0:T(8,128)(2,1)S(1)} %collective-permute-done.20), channel_id=1, source_target_pairs={{8,4},{4,0},{9,5},{5,1},{10,6},{6,2},{11,7},{7,3},{24,20},{20,16},... | collective-permute-start | bytes 2752520 | tf_op jit(solution)/shard_map/ppermute | solution.py:133
  114.8 19.3 %collective-permute-start.31 = (bf16[256,1792]{1,0:T(8,128)(2,1)}, bf16[256,1792]{1,0:T(8,128)(2,1)}, u32[]{:S(2)}, u32[]{:S(2)}) collective-permute-start(bf16[256,1792]{1,0:T(8,128)(2,1)} %get-tuple-element.81), channel_id=1, source_target_pairs={{0,4},{4,8},{1,5},{5,9},{2,6},{6,10},{3,7},{7,11},{16,20},{20,24},... | collective-permute-start | bytes 2752520 | tf_op jit(solution)/shard_map/ppermute | solution.py:129
  119.4 14.7 %collective-permute-start.32 = (bf16[256,1792]{1,0:T(8,128)(2,1)}, bf16[256,1792]{1,0:T(8,128)(2,1)}, u32[]{:S(2)}, u32[]{:S(2)}) collective-permute-start(bf16[256,1792]{1,0:T(8,128)(2,1)} %get-tuple-element.82), channel_id=1, source_target_pairs={{12,8},{8,4},{13,9},{9,5},{14,10},{10,6},{15,11},{11,7},{28,24},{2... | collective-permute-start | bytes 2752520 | tf_op jit(solution)/shard_map/ppermute | solution.py:133
  121.0 16.2 %collective-permute-start.29 = (bf16[256,1792]{1,0:T(8,128)(2,1)S(1)}, bf16[256,1792]{1,0:T(8,128)(2,1)}, u32[]{:S(2)}, u32[]{:S(2)}) collective-permute-start(bf16[256,1792]{1,0:T(8,128)(2,1)S(1)} %collective-permute-done.25), channel_id=1, source_target_pairs={{8,12},{9,13},{10,14},{11,15},{24,28},{25,29},{26,30},{27,31},{40,... | collective-permute-start | bytes 2752520 | tf_op jit(solution)/shard_map/ppermute | solution.py:129
  122.6 19.5 %collective-permute-start.30 = (bf16[256,1792]{1,0:T(8,128)(2,1)S(1)}, bf16[256,1792]{1,0:T(8,128)(2,1)}, u32[]{:S(2)}, u32[]{:S(2)}) collective-permute-start(bf16[256,1792]{1,0:T(8,128)(2,1)S(1)} %collective-permute-done.26), channel_id=1, source_target_pairs={{4,0},{5,1},{6,2},{7,3},{20,16},{21,17},{22,18},{23,19},{36,32},{3... | collective-permute-start | bytes 2752520 | tf_op jit(solution)/shard_map/ppermute | solution.py:133
  126.3 7.8 %copy-start.8 = (bf16[1024,1792]{1,0:T(8,128)(2,1)S(1)}, bf16[1024,1792]{1,0:T(8,128)(2,1)}, u32[]{:S(2)}) copy-start(bf16[1024,1792]{1,0:T(8,128)(2,1)} %copy-done.7) | copy-start | bytes 11010052
  149.4 2.3 %copy-start.13 = (bf16[256,1792]{1,0:T(8,128)(2,1)S(1)}, bf16[256,1792]{1,0:T(8,128)(2,1)}, u32[]{:S(2)}) copy-start(bf16[256,1792]{1,0:T(8,128)(2,1)} %get-tuple-element.84) | copy-start | bytes 2752516
  149.4 3.7 %copy-start.12 = (bf16[256,1792]{1,0:T(8,128)(2,1)S(1)}, bf16[256,1792]{1,0:T(8,128)(2,1)}, u32[]{:S(2)}) copy-start(bf16[256,1792]{1,0:T(8,128)(2,1)} %get-tuple-element.85) | copy-start | bytes 2752516
  149.6 10.7 %collective-permute-start.35 = (bf16[128,1792]{1,0:T(8,128)(2,1)S(1)}, bf16[128,1792]{1,0:T(8,128)(2,1)S(1)}, u32[]{:S(2)}, u32[]{:S(2)}) collective-permute-start(bf16[128,1792]{1,0:T(8,128)(2,1)S(1)} %get-tuple-element.93), channel_id=1, source_target_pairs={{0,1},{1,2},{2,3},{3,0},{4,5},{5,6},{6,7},{7,4},{8,9},{9,10},{10,1... | collective-permute-start | bytes 1376264 | tf_op jit(solution)/shard_map/ppermute | solution.py:125
  150.1 12.1 %collective-permute-start.37 = (bf16[128,1792]{1,0:T(8,128)(2,1)S(1)}, bf16[128,1792]{1,0:T(8,128)(2,1)S(1)}, u32[]{:S(2)}, u32[]{:S(2)}) collective-permute-start(bf16[128,1792]{1,0:T(8,128)(2,1)S(1)} %get-tuple-element.94), channel_id=1, source_target_pairs={{0,3},{1,0},{2,1},{3,2},{4,7},{5,4},{6,5},{7,6},{8,11},{9,8},{10,9... | collective-permute-start | bytes 1376264 | tf_op jit(solution)/shard_map/ppermute | solution.py:125
  151.7 15.3 %collective-permute-start.33 = (bf16[256,1792]{1,0:T(8,128)(2,1)S(1)}, bf16[256,1792]{1,0:T(8,128)(2,1)S(1)}, u32[]{:S(2)}, u32[]{:S(2)}) collective-permute-start(bf16[256,1792]{1,0:T(8,128)(2,1)S(1)} %copy-done.13), channel_id=1, source_target_pairs={{0,4},{4,8},{8,12},{1,5},{5,9},{9,13},{2,6},{6,10},{10,14},{3,7},{... | collective-permute-start | bytes 2752520 | tf_op jit(solution)/shard_map/ppermute | solution.py:129
  153.1 18.0 %collective-permute-start.34 = (bf16[256,1792]{1,0:T(8,128)(2,1)S(1)}, bf16[256,1792]{1,0:T(8,128)(2,1)S(1)}, u32[]{:S(2)}, u32[]{:S(2)}) collective-permute-start(bf16[256,1792]{1,0:T(8,128)(2,1)S(1)} %copy-done.12), channel_id=1, source_target_pairs={{12,8},{8,4},{4,0},{13,9},{9,5},{5,1},{14,10},{10,6},{6,2},{15,11}... | collective-permute-start | bytes 2752520 | tf_op jit(solution)/shard_map/ppermute | solution.py:133
  162.5 15.3 %collective-permute-start.36 = (bf16[256,1792]{1,0:T(8,128)(2,1)S(1)}, bf16[256,1792]{1,0:T(8,128)(2,1)S(1)}, u32[]{:S(2)}, u32[]{:S(2)}) collective-permute-start(bf16[256,1792]{1,0:T(8,128)(2,1)S(1)} %pad_maximum_fusion), channel_id=1, source_target_pairs={{0,1},{1,2},{2,3},{3,0},{4,5},{5,6},{6,7},{7,4},{8,9},{9,10},{10,1... | collective-permute-start | bytes 2752520 | tf_op jit(solution)/shard_map/ppermute | solution.py:125
  162.8 16.7 %copy-start.10 = (bf16[1,256,1792]{2,1,0:T(8,128)(2,1)S(1)}, bf16[1,256,1792]{2,1,0:T(8,128)(2,1)}, u32[]{:S(2)}) copy-start(bf16[1,256,1792]{2,1,0:T(8,128)(2,1)} %param.27) | copy-start | bytes 2752516
  162.8 16.6 %copy-start.11 = (bf16[1,256,1792]{2,1,0:T(8,128)(2,1)S(1)}, bf16[1,256,1792]{2,1,0:T(8,128)(2,1)}, u32[]{:S(2)}) copy-start(bf16[1,256,1792]{2,1,0:T(8,128)(2,1)} %param.26) | copy-start | bytes 2752516
  162.8 16.6 %collective-permute-start.38 = (bf16[256,1792]{1,0:T(8,128)(2,1)S(1)}, bf16[256,1792]{1,0:T(8,128)(2,1)S(1)}, u32[]{:S(2)}, u32[]{:S(2)}) collective-permute-start(bf16[256,1792]{1,0:T(8,128)(2,1)S(1)} %pad_maximum_fusion.1), channel_id=1, source_target_pairs={{0,3},{1,0},{2,1},{3,2},{4,7},{5,4},{6,5},{7,6},{8,11},{9,8},{10,9... | collective-permute-start | bytes 2752520 | tf_op jit(solution)/shard_map/ppermute | solution.py:125
  171.1 10.8 %copy-start.1 = (s32[1,16]{1,0:T(1,128)S(1)}, s32[1,16]{1,0:T(1,128)}, u32[]{:S(2)}) copy-start(s32[1,16]{1,0:T(1,128)} %param.29) | copy-start | bytes 196

commit v3 on v2

--- a/solution.py
+++ b/solution.py
@@ -1,3 +1,5 @@
+import functools
+
 import jax
 import jax.numpy as jnp
 from jax import lax
@@ -81,40 +83,156 @@
     )(chosen, outer, local_rows, moment, moved)
 
 
-def regroup_kernel(where_ref, cot_ref, own_ref, up_ref, down_ref):
-    rows = own_ref.shape[0]
+def pack_kernel(where_ref, gate_ref, up_ref, cot_ref, hid_out, cot_out, far_up, near_up, far_down, near_down):
+    step = pl.program_id(0)
+    half, width = gate_ref.shape
+    across = cot_out.shape[1]
+    piece = across // SIDE
+    gate = gate_ref[...].astype(jnp.float32)
+    hidden = (gate * jax.nn.sigmoid(gate) * up_ref[...].astype(jnp.float32)).astype(jnp.bfloat16)
+    hid_out[...] = hidden
+
+    def columns(by, to_ref, start):
+        for k in range(SIDE):
+            group = (where_ref[0] + k) % SIDE * SIDE
+            at = pl.multiple_of((group + (where_ref[1] + by) % SIDE) * piece, piece)
+            to_ref[:, start + k * piece : start + (k + 1) * piece] = cot_ref[:, pl.ds(at, piece)]
+
+    columns(0, cot_out, 0)
+
+    @pl.when(step == 0)
+    def _():
+        far_up[:, :width] = hidden
+        columns(2, far_up, width)
+        columns(1, near_up, width)
+        near_down[:, :width] = hidden
+        columns(3, near_down, width)
+
+    @pl.when(step == 1)
+    def _():
+        far_down[:, :width] = hidden
+        columns(2, far_down, width)
+        columns(3, near_down, width + across)
+        near_up[:, :width] = hidden
+        columns(1, near_up, width + across)
+
+
+def pack(where, gate, up, cot_rows):
+    rows, width = gate.shape
+    depth = cot_rows.shape[1]
+    half, across = rows // 2, depth // SIDE
+    far, near = (half, width + across), (half, width + 2 * across)
+    moved = lambda shape: jax.ShapeDtypeStruct(shape, jnp.bfloat16)
+    block = lambda n: pl.BlockSpec((half, n), lambda i: (i, 0))
+    whole = lambda shape: pl.BlockSpec(shape, lambda i: (0, 0))
+    return pl.pallas_call(
+        pack_kernel,
+        grid=(2,),
+        out_shape=[moved((rows, width)), moved((rows, across)), moved(far), moved(near), moved(far), moved(near)],
+        in_specs=[SMEM, block(width), block(width), block(depth)],
+        out_specs=[block(width), block(across), whole(far), whole(near), whole(far), whole(near)],
+        compiler_params=pltpu.CompilerParams(vmem_limit_bytes=28 * 2**20),
+        cost_estimate=pl.CostEstimate(flops=4 * rows * width, bytes_accessed=11 * 2**20, transcendentals=rows * width),
+        name="pack",
+    )(where, gate, up, cot_rows)
+
+
+def product_of(z, total_ref, cot_ref, mid_ref, up_ref, down_ref, scale, at):
+    piece = cot_ref.shape[1] // SIDE
+    first = z == 0
+    last = jnp.where(first, down_ref[...], up_ref[...])
+    far = jnp.where(first, cot_ref[at, 3 * piece :], cot_ref[at, piece : 2 * piece])
+    mid = cot_ref[at, 2 * piece : 3 * piece]
+    total = total_ref[at]
+    total = total + jnp.dot(mid, mid_ref[...], preferred_element_type=jnp.float32)
+    total = total + jnp.dot(far, last, preferred_element_type=jnp.float32)
+    return (scale * total).astype(jnp.bfloat16)
+
+
+def far_kernel(scale, where_ref, total_ref, cot_ref, mid_ref, up_ref, down_ref, top_out, low_out):
+    half = top_out.shape[0]
+    for out, start in ((top_out, 0), (low_out, half)):
+        at = slice(start, start + half)
+        out[...] = product_of(where_ref[0], total_ref, cot_ref, mid_ref, up_ref, down_ref, scale, at)
+
+
+def near_kernel(scale, where_ref, total_ref, cot_ref, mid_ref, up_ref, down_ref, own_out, up_add, up_out, down_out, down_add):
+    step = pl.program_id(0)
+    half = up_add.shape[0]
+    for at, targets in (
+        (slice(0, half), (up_add, down_out, own_out.at[:half])),
+        (slice(half, 2 * half), (up_out, down_add, own_out.at[half:])),
+    ):
+        value = product_of(where_ref[0], total_ref, cot_ref, mid_ref, up_ref, down_ref, scale, at)
+        for n, target in enumerate(targets):
+
+            @pl.when(step == n)
+            def _(value=value, target=target):
+                target[...] = value
+
+
+def last_products(which, where, total, cot, mid, up, down, scale):
+    tokens, width = total.shape
+    rows = tokens // SIDE
     half = rows // 2
-    piece = own_ref.shape[1] // SIDE
-    for k in range(SIDE):
-        group = (where_ref[0] + k) % SIDE * SIDE
-        to = slice(k * piece, (k + 1) * piece)
-        for by in range(SIDE):
-            start = pl.multiple_of((group + (where_ref[1] + by) % SIDE) * piece, piece)
-            value = cot_ref[:, pl.ds(start, piece)]
-            if by == 0:
-                own_ref[:, to] = value
-            elif by == 1:
-                up_ref[:rows, to] = value
-            elif by == 2:
-                up_ref[rows:, to] = value[:half]
-                down_ref[rows:, to] = value[half:]
-            else:
-                down_ref[:rows, to] = value
-
-
-def regroup(where, cot_rows):
-    rows, depth = cot_rows.shape
-    width = depth // SIDE
-    sizes = (rows, rows + rows // 2, rows + rows // 2)
-    return pl.pallas_call(
-        regroup_kernel,
-        out_shape=[jax.ShapeDtypeStruct((n, width), jnp.bfloat16) for n in sizes],
-        in_specs=[SMEM, VMEM],
-        out_specs=[VMEM] * 3,
+    part = lambda n: jax.ShapeDtypeStruct((n, width), jnp.bfloat16)
+    whole = lambda n: pl.BlockSpec((n, width), lambda i: (0, 0))
+    if which == "far":
+        body, outs, steps, chunk = far_kernel, [half, half], 1, lambda i: (2, 0)
+    else:
+        body, outs, steps, chunk = near_kernel, [rows, half, half, half, half], 3, lambda i: ((2 * i + 1) % 5 % 4, 0)
+    return pl.pallas_call(
+        functools.partial(body, scale),
+        grid=(steps,),
+        out_shape=[part(n) for n in outs],
+        in_specs=[
+            SMEM,
+            pl.BlockSpec((rows, width), chunk),
+            pl.BlockSpec((rows, cot.shape[1]), chunk),
+            whole(rows),
+            whole(rows),
+            whole(rows),
+        ],
+        out_specs=[whole(n) for n in outs],
+        compiler_params=pltpu.CompilerParams(vmem_limit_bytes=32 * 2**20),
+        cost_estimate=pl.CostEstimate(
+            flops=4 * steps * rows * rows * width, bytes_accessed=(6 * steps + 6) * rows * width, transcendentals=0
+        ),
+        name=which + "_rows",
+    )(where, total, cot, mid, up, down)
+
+
+def finish_kernel(gate_ref, up_ref, own_ref, top_up, low_up, top_down, low_down, gate_out, up_out):
+    def write(first, second):
+        grad = own_ref[...].astype(jnp.float32) + first[...].astype(jnp.float32) + second[...].astype(jnp.float32)
+        gate = gate_ref[...].astype(jnp.float32)
+        sig = jax.nn.sigmoid(gate)
+        gate_out[...] = (grad * up_ref[...].astype(jnp.float32) * sig * (1.0 + gate * (1.0 - sig))).astype(jnp.bfloat16)
+        up_out[...] = (grad * (gate * sig)).astype(jnp.bfloat16)
+
+    @pl.when(pl.program_id(0) == 0)
+    def _():
+        write(top_up, top_down)
+
+    @pl.when(pl.program_id(0) == 1)
+    def _():
+        write(low_up, low_down)
+
+
+def finish(gate, up, own, top_up, low_up, top_down, low_down):
+    rows, width = gate.shape
+    block = pl.BlockSpec((rows // 2, width), lambda i: (i, 0))
+    whole = pl.BlockSpec((rows // 2, width), lambda i: (0, 0))
+    return pl.pallas_call(
+        finish_kernel,
+        grid=(2,),
+        out_shape=[jax.ShapeDtypeStruct((rows, width), jnp.bfloat16)] * 2,
+        in_specs=[block, block, block, whole, whole, whole, whole],
+        out_specs=[block, block],
         compiler_params=pltpu.CompilerParams(vmem_limit_bytes=16 * 2**20),
-        cost_estimate=pl.CostEstimate(flops=0, bytes_accessed=4 * rows * depth, transcendentals=0),
-        name="regroup",
-    )(where, cot_rows)
+        cost_estimate=pl.CostEstimate(flops=10 * rows * width, bytes_accessed=14 * rows * width, transcendentals=rows * width),
+        name="finish",
+    )(gate, up, own, top_up, low_up, top_down, low_down)
 
 
 def tie(*values):
@@ -140,7 +258,6 @@
 def local(theta_outer, theta_local, momentum, gate_pre, up_pre, cotangent, partner, chosen):
     outer, local_rows, moment = theta_outer[0], theta_local[0], momentum[0]
     rows, width = outer.shape
-    half = rows // 2
     scale = width ** (-0.5)
     z, x = lax.axis_index("z"), lax.axis_index("x")
     my_rep = lax.axis_index("rep")
@@ -150,56 +267,76 @@
     def to_partner(by):
         return lambda value: lax.ppermute(value, "rep", [(i, i ^ by) for i in range(replicas)])
 
-    gval = gate_pre[0].astype(jnp.float32)
-    uval = up_pre[0].astype(jnp.float32)
-    hidden = (gval * jax.nn.sigmoid(gval) * uval).astype(jnp.bfloat16)
-    cot_own, cot_up, cot_down = regroup(jnp.stack([z, x]).astype(jnp.int32), cotangent[0])
+    where = jnp.stack([z, x]).astype(jnp.int32)
+    gate, upper = gate_pre[0], up_pre[0]
+    hidden, cot_own, far_up, near_up, far_down, near_down = pack(where, gate, upper, cotangent[0])
     picked = pick_tiles(chosen, outer, local_rows)
-    picked, hidden, cot_up, cot_down = tie(picked, hidden, cot_up, cot_down)
-    hid_left, hid_right = turn(hidden, 1), turn(hidden, -1)
-    cot_left, cot_right = turn(cot_up, 1), turn(cot_down, -1)
+    picked, far_up, near_up, far_down, near_down = tie(picked, far_up, near_up, far_down, near_down)
+    far_up, far_down = turn(far_up, 1), turn(far_down, -1)
+    near_up, near_down = turn(near_up, 1), turn(near_down, -1)
 
     moved = lax.switch(offset - 1, [to_partner(by) for by in range(1, replicas)], picked)
-    moved, hid_left, hid_right, cot_left, cot_right = tie(moved, hid_left, hid_right, cot_left, cot_right)
-    hid_top, hid_low = turn(hid_left[:half], 1), turn(hid_right[half:], -1)
-    cot_top, cot_low = turn(cot_left[rows:], 1), turn(cot_right[rows:], -1)
+    moved, far_up, far_down = tie(moved, far_up, far_down)
     momentum_new, theta_new = outer_step(chosen, outer, local_rows, moment, moved)
     up1, down1 = up_line(theta_new, (0, 3)), down_line(theta_new, (0, 3))
-
-    cot = jnp.concatenate([cot_own, cot_right[:rows], cot_top, cot_low, cot_left[:rows]], axis=0)
-    hid = jnp.concatenate([hidden, hid_right, hid_top, hid_low, hid_left], axis=0)
+    last_up, last_down = turn(far_up, 1), turn(far_down, -1)
+    up1, down1, near_up, near_down = tie(up1, down1, near_up, near_down)
+
+    up2, down2 = up_line(up1, (1, 3)), down_line(down1, (1, 3))
+    across = cot_own.shape[1]
+    first, second = slice(width, width + across), slice(width + across, width + 2 * across)
+    cot = jnp.concatenate(
+        [
+            cot_own,
+            near_down[:, first],
+            near_down[:, second],
+            last_up[:, first],
+            last_down[:, first],
+            near_up[:, first],
+            near_up[:, second],
+        ],
+        axis=0,
+    )
+    hid = jnp.concatenate(
+        [
+            hidden,
+            near_down[:, :width],
+            far_down[:, :width],
+            last_up[:, :width],
+            last_down[:, :width],
+            far_up[:, :width],
+            near_up[:, :width],
+        ],
+        axis=0,
+    )
     part = lax.dot_general(cot, hid, (((0,), (0,)), ((), ())), preferred_element_type=jnp.float32)
     part = (scale * part).astype(jnp.bfloat16).reshape(SIDE, rows, width)
-    up1, down1, part = tie(up1, down1, part)
-
-    up2, down2 = up_line(up1, (1, 3)), down_line(down1, (1, 3))
+    up2, down2, part = tie(up2, down2, part)
+
+    up3, down3 = up_line(up2, (2, 3)), down_line(down2, (2, 3))
     sum_up, sum_down = up_line(part[3], (0, 1)), down_line(part[1], (0, 1))
-    near = jnp.concatenate([theta_new, down1, up1], axis=0)
     cols = [cot[:, k * rows : (k + 1) * rows] for k in range(SIDE)]
     total = jnp.dot(
-        jnp.concatenate([cols[0], cols[1], cols[3]], axis=1), near, preferred_element_type=jnp.float32
+        jnp.concatenate([cols[0], cols[1], cols[3]], axis=1),
+        jnp.concatenate([theta_new, down1, up1], axis=0),
+        preferred_element_type=jnp.float32,
     )
+    mid = jnp.where(z >= 2, up2, down2)
     sum_up, sum_down = add(part[2], sum_up), add(part[2], sum_down)
-    up2, down2, sum_up, sum_down, total = tie(up2, down2, sum_up, sum_down, total)
-
-    up3, down3 = up_line(up2, (2, 3)), down_line(down2, (2, 3))
+    up3, down3, sum_up, sum_down, total, mid = tie(up3, down3, sum_up, sum_down, total, mid)
+
     sum_up, sum_down = up_line(sum_up, (0, 2)), down_line(sum_down, (0, 2))
-    total = total + jnp.dot(cols[2], jnp.where(z >= 2, up2, down2), preferred_element_type=jnp.float32)
+    far_top, far_low = last_products("far", where, total, cot, mid, up3, down3, scale)
+    far_top, far_low = turn(far_top, 1), turn(far_low, -1)
+    own, up_add, up_near, down_near, down_add = last_products("near", where, total, cot, mid, up3, down3, scale)
+    low_up, top_down = turn(up_near, 1), turn(down_near, -1)
+    up_add, down_add = add(up_add, far_top), add(down_add, far_low)
     sum_up, sum_down = add(part[1], sum_up), add(part[3], sum_down)
-    up3, down3, sum_up, sum_down, total = tie(up3, down3, sum_up, sum_down, total)
-
+    up_add, down_add, sum_up, sum_down = tie(up_add, down_add, sum_up, sum_down)
+
+    top_up, low_down = turn(up_add, 1), turn(down_add, -1)
     sum_up, sum_down = up_line(sum_up, (0, 3)), down_line(sum_down, (0, 3))
-    far = jnp.where(z == 0, cols[3], cols[1])
-    total = total + jnp.dot(far, jnp.where(z == 0, down3, up3), preferred_element_type=jnp.float32)
-    share = (scale * total).astype(jnp.bfloat16).reshape(SIDE, rows, width)
-    left, right = turn(share[2, :half], 1), turn(share[2, half:], -1)
-    ahead = jnp.concatenate([add(share[1, :half], left), share[1, half:]], axis=0)
-    behind = jnp.concatenate([share[3, :half], add(share[3, half:], right)], axis=0)
-    left, right = turn(ahead, 1), turn(behind, -1)
-    grad_hidden = share[0].astype(jnp.float32) + left.astype(jnp.float32) + right.astype(jnp.float32)
-    sig = jax.nn.sigmoid(gval)
-    grad_gate = (grad_hidden * uval * sig * (1.0 + gval * (1.0 - sig))).astype(jnp.bfloat16)
-    grad_up = (grad_hidden * (gval * sig)).astype(jnp.bfloat16)
+    grad_gate, grad_up = finish(gate, upper, own, top_up, low_up, top_down, low_down)
     grad_weight = part[0].astype(jnp.float32) + sum_up.astype(jnp.float32) + sum_down.astype(jnp.float32)
     return momentum_new[None], grad_weight.astype(jnp.bfloat16)[None], grad_gate[None], grad_up[None]
 

time: 183 us -> 197 us (1.077)
  other arithmetic: 25 us -> 2.52 us
  waiting for transfers between devices: 84.8 us -> 105 us
  Pallas kernels: 6.11 us -> 14.7 us
  starting transfers between devices: 36.9 us -> 45.4 us
  matrix products: 14.6 us -> 8.74 us
  local copies, waits for them, and re-layouts: 12.8 us -> 17.6 us
    ppermute x6, waiting for transfers between devices: 10.5 us -> 32.5 us  [up_line(): return lax.ppermute(value, 'z', [(i, i + 1) for i in range(*step)])]
    ppermute x12, waiting for transfers between devices: 58 us -> 38.9 us  [turn(): return lax.ppermute(value, 'x', [(i, (i + by) % SIDE) for i in range(SIDE)])]
    ppermute x6, waiting for transfers between devices: 14.1 us -> 31.9 us  [down_line(): lax.ppermute(value, 'z', [(SIDE - 1 - i, SIDE - 2 - i) for i in range(*st...]
    unnamed x36 -> x38, local copies, waits for them, and re-layouts: 5.47 us -> 14.7 us
    pallas_call x1 -> x4, Pallas kernels: 1.73 us -> 10.2 us  [the longest x2 4.92 us: last_products(): pl.pallas_call(functools.partial(body, scale), grid=(steps,), out_shape=[...]
    convert_element_type x2 -> x0, other arithmetic: 7.48 us -> none  [the longest x1 4.55 us: local(): share = (scale * total).astype(jnp.bfloat16).reshape(SIDE, rows, width)]
    add x1 -> x0, other arithmetic: 7.47 us -> none  [local(): total + jnp.dot(cols[2], jnp.where(z >= 2, up2, down2), preferred_element...]
    ppermute x6, starting transfers between devices: 16.9 us -> 24.1 us  [up_line(): return lax.ppermute(value, 'z', [(i, i + 1) for i in range(*step)])]
  transfers between devices with their start and end apart: 25 -> 25, of which waited for: 16 -> 13; matrix products, arithmetic and copies ran while one was open for 21% -> 7% of each run, Pallas kernels for 0% -> 5%
where the time goes in v3:
time: 197 us; the launch traced here: 196 us
  waiting for transfers between devices  105 us (53%)
  starting transfers between devices  45.4 us (23%)
  local copies, waits for them, and re-layouts  17.6 us (9%)
  Pallas kernels  14.7 us (7%)
  matrix products  8.74 us (4%)
  other arithmetic  2.52 us (1%)
    ppermute x12, waiting for transfers between devices, turn(): return lax.ppermute(value, 'x', [(i, (i + by) % SIDE) for i in range(SIDE)])  38.9 us
    ppermute x6, waiting for transfers between devices, up_line(): return lax.ppermute(value, 'z', [(i, i + 1) for i in range(*step)])  32.5 us
    ppermute x6, waiting for transfers between devices, down_line(): lax.ppermute(value, 'z', [(SIDE - 1 - i, SIDE - 2 - i) for i in range(*st...  31.9 us
    ppermute x6, starting transfers between devices, up_line(): return lax.ppermute(value, 'z', [(i, i + 1) for i in range(*step)])  24.1 us
    unnamed x38, local copies, waits for them, and re-layouts  14.7 us
    ppermute x12, starting transfers between devices, turn(): return lax.ppermute(value, 'x', [(i, (i + by) % SIDE) for i in range(SIDE)])  14.5 us
    ppermute x6, starting transfers between devices, down_line(): lax.ppermute(value, 'z', [(SIDE - 1 - i, SIDE - 2 - i) for i in range(*st...  6.61 us
    pallas_call x2, Pallas kernels, last_products(): pl.pallas_call(functools.partial(body, scale), grid=(steps,), out_shape=[...  4.92 us
  transfers between devices with their start and end apart: 25, of which 13 were waited for; matrix products, arithmetic and copies ran while one was open for 7% of the time, Pallas kernels for 5%

profile of v3, /device:TPU:6, one launch (start us, length us, event | category | flops | bytes accessed | tf_op | source)
XLA Modules:
  0.0 196.1 jit_solution(9487986292270055479)
XLA Ops:
  0.7 1.2 copy-done.1
  1.9 1.2 copy-done.3
  3.1 0.7 copy-done.11
  3.7 1.4 pick_tiles.1
  5.2 1.2 copy-done.5
  6.4 1.2 copy-done.7
  7.5 1.6 copy-done.9
  9.1 3.1 %pack.1 = (bf16[256,1792]{1,0:T(8,128)(2,1)S(1)}, bf16[256,1024]{1,0:T(8,128)(2,1)S(1)}, bf16[128,2816]{1,0:T(8,128)(2,1)}, bf16[128,3840]{1,0:T(8,128)(2,1)}, b...) custom-call(s32[2]{0:T(128)S(1)} %pad_add_fusion.where_ref, bf16[256,1792]{1,0:T(8,128)(2,1)S(1)} %bitcast.36, ...), custom_call_target="tpu_custom_call" | custom-call | flops 1835008 | bytes 11534336 | tf_op jit(solution)/shard_map/pack/pallas_call | solution.py:128
  12.2 2.2 %collective-permute-start.15 = (bf16[128,2816]{1,0:T(8,128)(2,1)}, bf16[128,2816]{1,0:T(8,128)(2,1)}, u32[]{:S(2)}, u32[]{:S(2)}) collective-permute-start(bf16[128,2816]{1,0:T(8,128)(2,1)} %get-tuple-element.82), channel_id=1, source_target_pairs={{0,1},{1,2},{2,3},{3,0},{4,5},{5,6},{6,7},{7,4},{8,9},{9,10},{10,1... | collective-permute-start | bytes 2162696 | tf_op jit(solution)/shard_map/ppermute | solution.py:243
  14.5 3.2 %collective-permute-start.19 = (bf16[128,3840]{1,0:T(8,128)(2,1)}, bf16[128,3840]{1,0:T(8,128)(2,1)}, u32[]{:S(2)}, u32[]{:S(2)}) collective-permute-start(bf16[128,3840]{1,0:T(8,128)(2,1)} %get-tuple-element.87), channel_id=1, source_target_pairs={{0,1},{1,2},{2,3},{3,0},{4,5},{5,6},{6,7},{7,4},{8,9},{9,10},{10,1... | collective-permute-start | bytes 2949128 | tf_op jit(solution)/shard_map/ppermute | solution.py:243
  17.7 0.6 constant_dynamic-slice_fusion
  18.9 2.3 %conditional.1 = (bf16[14,128,128]{2,1,0:T(8,128)(2,1)}) conditional(s32[]{:T(128)} %clamp.3, bf16[14,128,128]{2,1,0:T(8,128)(2,1)} %pick_tiles.1, bf16[14,128,128]{2,1,0:T(8,128)(2,1)} %pick_tiles.1, bf16[14,128,128]{2,1,0:T(8,128)(2,1)} %pick_tiles.1, bf16[14,128,128]{2,1,0:T(8,128)(2,1)} %pick_tiles.1, ...), branch_computations={%region_0.0_spmd, %region_1.0_spmd, %region_2.0_spmd, %region_3.0_... | conditional | bytes 1835056 | solution.py:278
  19.1 2.1 %collective-permute-done = bf16[14,128,128]{2,1,0:T(8,128)(2,1)} collective-permute-done((bf16[14,128,128]{2,1,0:T(8,128)(2,1)}, bf16[14,128,128]{2,1,0:T(8,128)(2,1)}, u32[]{:S(2)}, u32[]{:S(2)}) %collective-permute-start) | collective-permute-done | bytes 458784 | tf_op jit(solution)/shard_map/cond/branch_0_fun/ppermute | solution.py:268
  21.2 10.4 %collective-permute-done.15 = bf16[128,2816]{1,0:T(8,128)(2,1)} collective-permute-done((bf16[128,2816]{1,0:T(8,128)(2,1)}, bf16[128,2816]{1,0:T(8,128)(2,1)}, u32[]{:S(2)}, u32[]{:S(2)}) %collective-permute-start.15) | collective-permute-done | bytes 720928 | tf_op jit(solution)/shard_map/ppermute | solution.py:243
  31.6 3.5 %collective-permute-done.16 = bf16[128,2816]{1,0:T(8,128)(2,1)} collective-permute-done((bf16[128,2816]{1,0:T(8,128)(2,1)}, bf16[128,2816]{1,0:T(8,128)(2,1)}, u32[]{:S(2)}, u32[]{:S(2)}) %collective-permute-start.16) | collective-permute-done | bytes 720928 | tf_op jit(solution)/shard_map/ppermute | solution.py:243
  35.1 1.5 copy-done.10
  36.6 3.1 %outer_step.1 = (f32[256,1792]{1,0:T(8,128)}, bf16[256,1792]{1,0:T(8,128)(2,1)}) custom-call(s32[1,14]{1,0:T(1,128)S(1)} %copy-done.12, bf16[256,1792]{1,0:T(8,128)(2,1)S(1)} %bitcast.33, bf16[256,1792]{1,0:T(8,128)(2,1)S(1)} %bitcast.35, f32[256,1792]{1,0:T(8,128)S(1)} %bitcast.41, bf16[14,128,128]{2,1,0:T(8,128)(2,1)} %get-tuple-element.125.moved_ref), custom_call_target="tpu_custom_call" | custom-call | flops 3670016 | bytes 6422528 | tf_op jit(solution)/shard_map/outer_step/pallas_call | solution.py:70
  39.7 12.2 %collective-permute-start.17 = (bf16[256,1792]{1,0:T(8,128)(2,1)}, bf16[256,1792]{1,0:T(8,128)(2,1)S(1)}, u32[]{:S(2)}, u32[]{:S(2)}) collective-permute-start(bf16[256,1792]{1,0:T(8,128)(2,1)} %get-tuple-element.86), channel_id=1, source_target_pairs={{0,4},{4,8},{8,12},{1,5},{5,9},{9,13},{2,6},{6,10},{10,14},{3,7},{... | collective-permute-start | bytes 2752520 | tf_op jit(solution)/shard_map/ppermute | solution.py:247
  51.8 1.3 collective-permute-start.18
  53.4 2.0 %collective-permute-start.24 = (bf16[128,2816]{1,0:T(8,128)(2,1)}, bf16[128,2816]{1,0:T(8,128)(2,1)S(1)}, u32[]{:S(2)}, u32[]{:S(2)}) collective-permute-start(bf16[128,2816]{1,0:T(8,128)(2,1)} %collective-permute-done.16), channel_id=1, source_target_pairs={{0,3},{1,0},{2,1},{3,2},{4,7},{5,4},{6,5},{7,6},{8,11},{9,8},{10,9... | collective-permute-start | bytes 2162696 | tf_op jit(solution)/shard_map/ppermute | solution.py:243
  55.4 16.3 %collective-permute-done.17 = bf16[256,1792]{1,0:T(8,128)(2,1)S(1)} collective-permute-done((bf16[256,1792]{1,0:T(8,128)(2,1)}, bf16[256,1792]{1,0:T(8,128)(2,1)S(1)}, u32[]{:S(2)}, u32[]{:S(2)}) %collective-permute-start.17) | collective-permute-done | bytes 917536 | tf_op jit(solution)/shard_map/ppermute | solution.py:247
  71.7 4.7 %collective-permute-done.18 = bf16[256,1792]{1,0:T(8,128)(2,1)S(1)} collective-permute-done((bf16[256,1792]{1,0:T(8,128)(2,1)}, bf16[256,1792]{1,0:T(8,128)(2,1)S(1)}, u32[]{:S(2)}, u32[]{:S(2)}) %collective-permute-start.18) | collective-permute-done | bytes 917536 | tf_op jit(solution)/shard_map/ppermute | solution.py:251
  76.3 1.0 slice_dynamic-update-slice_fusion.5
  77.4 1.1 slice_dynamic-update-slice_fusion.4
  78.5 1.1 slice_dynamic-update-slice_fusion.3
  79.6 1.0 slice_dynamic-update-slice_fusion.11
  80.6 1.0 slice_dynamic-update-slice_fusion.10
  81.5 1.1 slice_dynamic-update-slice_fusion.2
  82.6 1.0 slice_dynamic-update-slice_fusion.9
  83.6 0.7 collective-permute-start.21
  84.3 1.3 collective-permute-start.22
  85.6 1.0 slice_dynamic-update-slice_fusion.8.cot_ref
  86.6 0.1 slice.81
  86.8 4.5 %multiply_convert_fusion = bf16[1024,1792]{1,0:T(8,128)(2,1)S(1)} fusion(bf16[1024,1024]{1,0:T(8,128)(2,1)S(1)} %slice_dynamic-update-slice_fusion.8.cot_ref, bf16[1024,1792]{1,0:T(8,128)(2,1)S(1)} %slice_dynamic-update-slice_fusion.2), kind=kOutput, calls=%fused_computation | convolution fusion | flops 3761766400 | bytes 9437184 | tf_op jit(solution)/shard_map/dot_general | solution.py:312
  91.4 17.8 %collective-permute-done.22 = bf16[256,1792]{1,0:T(8,128)(2,1)S(1)} collective-permute-done((bf16[256,1792]{1,0:T(8,128)(2,1)S(1)}, bf16[256,1792]{1,0:T(8,128)(2,1)S(1)}, u32[]{:S(2)}, u32[]{:S(2)}) %collective-permute-start.22) | collective-permute-done | bytes 917536 | tf_op jit(solution)/shard_map/ppermute | solution.py:251
  109.2 0.1 slice_bitcast_fusion
  109.3 2.8 %collective-permute-start.27 = (bf16[256,1792]{1,0:T(8,128)(2,1)S(1)}, bf16[256,1792]{1,0:T(8,128)(2,1)S(1)}, u32[]{:S(2)}, u32[]{:S(2)}) collective-permute-start(bf16[256,1792]{1,0:T(8,128)(2,1)S(1)} %get-tuple-element.124), channel_id=1, source_target_pairs={{0,4},{1,5},{2,6},{3,7},{16,20},{17,21},{18,22},{19,23},{32,36},{3... | collective-permute-start | bytes 2752520 | tf_op jit(solution)/shard_map/ppermute | solution.py:247
  112.1 0.7 collective-permute-start.28
  112.8 4.2 %fusion.total_ref = f32[1024,1792]{1,0:T(8,128)S(1)} fusion(bf16[256,1792]{1,0:T(8,128)(2,1)S(1)} %collective-permute-done.17, bf16[256,1792]{1,0:T(8,128)(2,1)S(1)} %collective-permute-done.18, bf16[256,1792]{1,0:T(8,128)(2,1)} %get-tuple-element.86, bf16[1024,256]{1,0:T(8,128)(2,1)S(1)} %slice.82, bf16[1024,512]{1,0:T(8,128)(2,1)S(1)} %slice.81), kind=kOutput, calls=%fused_computation.1 | convolution fusion | flops 2829975552 | bytes 11665408 | tf_op jit(solution)/shard_map/dot_general | solution.py:319
  117.0 0.7 collective-permute-start.25
  117.7 1.3 collective-permute-start.26
  119.0 0.1 broadcast_select_fusion.mid_ref
  119.1 12.7 %collective-permute-done.27 = bf16[256,1792]{1,0:T(8,128)(2,1)S(1)} collective-permute-done((bf16[256,1792]{1,0:T(8,128)(2,1)S(1)}, bf16[256,1792]{1,0:T(8,128)(2,1)S(1)}, u32[]{:S(2)}, u32[]{:S(2)}) %collective-permute-start.27) | collective-permute-done | bytes 917536 | tf_op jit(solution)/shard_map/ppermute | solution.py:247
  131.9 0.4 fusion.7
  132.3 9.4 %collective-permute-done.26.down_ref = bf16[256,1792]{1,0:T(8,128)(2,1)S(1)} collective-permute-done((bf16[256,1792]{1,0:T(8,128)(2,1)S(1)}, bf16[256,1792]{1,0:T(8,128)(2,1)S(1)}, u32[]{:S(2)}, u32[]{:S(2)}) %collective-permute-start.26) | collective-permute-done | bytes 917536 | tf_op jit(solution)/shard_map/ppermute | solution.py:251
  141.7 1.2 far_rows.1
  143.0 1.5 collective-permute-start.31
  144.5 0.7 collective-permute-start.32
  145.2 3.5 %collective-permute-start.29 = (bf16[128,1792]{1,0:T(8,128)(2,1)S(1)}, bf16[128,1792]{1,0:T(8,128)(2,1)S(1)}, u32[]{:S(2)}, u32[]{:S(2)}) collective-permute-start(bf16[128,1792]{1,0:T(8,128)(2,1)S(1)} %get-tuple-element.105), channel_id=1, source_target_pairs={{0,1},{1,2},{2,3},{3,0},{4,5},{5,6},{6,7},{7,4},{8,9},{9,10},{10,1... | collective-permute-start | bytes 1376264 | tf_op jit(solution)/shard_map/ppermute | solution.py:243
  148.8 3.7 %near_rows.1 = (bf16[256,1792]{1,0:T(8,128)(2,1)S(1)}, bf16[128,1792]{1,0:T(8,128)(2,1)S(1)}, bf16[128,1792]{1,0:T(8,128)(2,1)S(1)}, bf16[128,1792]{1,0:T(8,128)(2,1)S(1)}, bf16[128,1792]{1,0:T(8,128)(2,1)S(1)}) custom-call(s32[2]{0:T(128)S(1)} %pad_add_fusion.where_ref, f32[1024,1792]{1,0:T(8,128)S(1)} %fusion.total_ref, ...), custom_call_target="tpu_custom_call" | custom-call | flops 1409286144 | bytes 11010048 | tf_op jit(solution)/shard_map/near_rows/pallas_call | solution.py:184
  152.5 0.1 collective-permute-start.36
  152.6 3.0 %collective-permute-done.30 = bf16[128,1792]{1,0:T(8,128)(2,1)S(1)} collective-permute-done((bf16[128,1792]{1,0:T(8,128)(2,1)S(1)}, bf16[128,1792]{1,0:T(8,128)(2,1)S(1)}, u32[]{:S(2)}, u32[]{:S(2)}) %collective-permute-start.30) | collective-permute-done | bytes 458784 | tf_op jit(solution)/shard_map/ppermute | solution.py:243
  155.6 0.1 add_convert_fusion.2
  155.7 4.0 %collective-permute-done.29 = bf16[128,1792]{1,0:T(8,128)(2,1)S(1)} collective-permute-done((bf16[128,1792]{1,0:T(8,128)(2,1)S(1)}, bf16[128,1792]{1,0:T(8,128)(2,1)S(1)}, u32[]{:S(2)}, u32[]{:S(2)}) %collective-permute-start.29) | collective-permute-done | bytes 458784 | tf_op jit(solution)/shard_map/ppermute | solution.py:243
  159.7 0.1 add_convert_fusion.3
  159.9 3.4 %collective-permute-done.31 = bf16[256,1792]{1,0:T(8,128)(2,1)S(1)} collective-permute-done((bf16[256,1792]{1,0:T(8,128)(2,1)S(1)}, bf16[256,1792]{1,0:T(8,128)(2,1)S(1)}, u32[]{:S(2)}, u32[]{:S(2)}) %collective-permute-start.31) | collective-permute-done | bytes 917536 | tf_op jit(solution)/shard_map/ppermute | solution.py:247
  163.3 0.4 add_convert_fusion
  163.7 6.2 %collective-permute-start.33 = (bf16[256,1792]{1,0:T(8,128)(2,1)S(1)}, bf16[256,1792]{1,0:T(8,128)(2,1)S(1)}, u32[]{:S(2)}, u32[]{:S(2)}) collective-permute-start(bf16[256,1792]{1,0:T(8,128)(2,1)S(1)} %get-tuple-element.110), channel_id=1, source_target_pairs={{0,4},{4,8},{8,12},{1,5},{5,9},{9,13},{2,6},{6,10},{10,14},{3,7},{... | collective-permute-start | bytes 2752520 | tf_op jit(solution)/shard_map/ppermute | solution.py:247
  170.0 1.3 collective-permute-start.34
  171.4 3.2 %collective-permute-start.35 = (bf16[128,1792]{1,0:T(8,128)(2,1)S(1)}, bf16[128,1792]{1,0:T(8,128)(2,1)S(1)}, u32[]{:S(2)}, u32[]{:S(2)}) collective-permute-start(bf16[128,1792]{1,0:T(8,128)(2,1)S(1)} %add_convert_fusion.3), channel_id=1, source_target_pairs={{0,1},{1,2},{2,3},{3,0},{4,5},{5,6},{6,7},{7,4},{8,9},{9,10},{10,1... | collective-permute-start | bytes 1376264 | tf_op jit(solution)/shard_map/ppermute | solution.py:243
  174.6 11.4 %collective-permute-done.37.top_down = bf16[128,1792]{1,0:T(8,128)(2,1)S(1)} collective-permute-done((bf16[128,1792]{1,0:T(8,128)(2,1)S(1)}, bf16[128,1792]{1,0:T(8,128)(2,1)S(1)}, u32[]{:S(2)}, u32[]{:S(2)}) %collective-permute-start.37) | collective-permute-done | bytes 458784 | tf_op jit(solution)/shard_map/ppermute | solution.py:243
  186.0 6.6 %collective-permute-done.38.low_down = bf16[128,1792]{1,0:T(8,128)(2,1)S(1)} collective-permute-done((bf16[128,1792]{1,0:T(8,128)(2,1)S(1)}, bf16[128,1792]{1,0:T(8,128)(2,1)S(1)}, u32[]{:S(2)}, u32[]{:S(2)}) %collective-permute-start.38) | collective-permute-done | bytes 458784 | tf_op jit(solution)/shard_map/ppermute | solution.py:243
  192.6 2.1 %finish.1 = (bf16[256,1792]{1,0:T(8,128)(2,1)}, bf16[256,1792]{1,0:T(8,128)(2,1)}) custom-call(bf16[256,1792]{1,0:T(8,128)(2,1)S(1)} %bitcast.37, bf16[256,1792]{1,0:T(8,128)(2,1)S(1)} %bitcast.39, bf16[256,1792]{1,0:T(8,128)(2,1)S(1)} %get-tuple-element.112.own_ref, bf16[128,1792]{1,0:T(8,128)(2,1)S(1)} %collective-permute-done.35.top_up, ...), custom_call_target="tpu_custom_call" | custom-call | flops 4587520 | bytes 6422528 | tf_op jit(solution)/shard_map/finish/pallas_call | solution.py:226
  194.7 1.3 fusion.13
  (46 shorter events, 0.8 us)
Async XLA Ops:
  0.6 17.1 %copy-start = (s32[1,16]{1,0:T(1,128)S(1)}, s32[1,16]{1,0:T(1,128)}, u32[]{:S(2)}) copy-start(s32[1,16]{1,0:T(1,128)} %param.29) | copy-start | bytes 196
  0.7 1.2 copy-start.1
  1.9 1.2 copy-start.3
  3.1 0.7 copy-start.11
  3.7 31.3 %copy-start.2 = (bf16[1,256,1792]{2,1,0:T(8,128)(2,1)S(1)}, bf16[1,256,1792]{2,1,0:T(8,128)(2,1)}, u32[]{:S(2)}) copy-start(bf16[1,256,1792]{2,1,0:T(8,128)(2,1)} %param.23) | copy-start | bytes 2752516
  3.7 31.3 %copy-start.4 = (bf16[1,256,1792]{2,1,0:T(8,128)(2,1)S(1)}, bf16[1,256,1792]{2,1,0:T(8,128)(2,1)}, u32[]{:S(2)}) copy-start(bf16[1,256,1792]{2,1,0:T(8,128)(2,1)} %param.24) | copy-start | bytes 2752516
  3.7 31.3 %copy-start.12 = (s32[1,14]{1,0:T(1,128)S(1)}, s32[1,14]{1,0:T(1,128)}, u32[]{:S(2)}) copy-start(s32[1,14]{1,0:T(1,128)} %chosen_ref.3) | copy-start | bytes 172
  5.2 1.2 copy-start.5
  6.4 1.2 copy-start.7
  7.5 1.6 copy-start.9
  12.2 19.3 %collective-permute-start.15 = (bf16[128,2816]{1,0:T(8,128)(2,1)}, bf16[128,2816]{1,0:T(8,128)(2,1)}, u32[]{:S(2)}, u32[]{:S(2)}) collective-permute-start(bf16[128,2816]{1,0:T(8,128)(2,1)} %get-tuple-element.82), channel_id=1, source_target_pairs={{0,1},{1,2},{2,3},{3,0},{4,5},{5,6},{6,7},{7,4},{8,9},{9,10},{10,1... | collective-permute-start | bytes 2162696 | tf_op jit(solution)/shard_map/ppermute | solution.py:243
  14.5 20.6 %collective-permute-start.16 = (bf16[128,2816]{1,0:T(8,128)(2,1)}, bf16[128,2816]{1,0:T(8,128)(2,1)}, u32[]{:S(2)}, u32[]{:S(2)}) collective-permute-start(bf16[128,2816]{1,0:T(8,128)(2,1)} %get-tuple-element.83), channel_id=1, source_target_pairs={{0,3},{1,0},{2,1},{3,2},{4,7},{5,4},{6,5},{7,6},{8,11},{9,8},{10,9... | collective-permute-start | bytes 2162696 | tf_op jit(solution)/shard_map/ppermute | solution.py:243
  14.5 38.9 %collective-permute-start.19 = (bf16[128,3840]{1,0:T(8,128)(2,1)}, bf16[128,3840]{1,0:T(8,128)(2,1)}, u32[]{:S(2)}, u32[]{:S(2)}) collective-permute-start(bf16[128,3840]{1,0:T(8,128)(2,1)} %get-tuple-element.87), channel_id=1, source_target_pairs={{0,1},{1,2},{2,3},{3,0},{4,5},{5,6},{6,7},{7,4},{8,9},{9,10},{10,1... | collective-permute-start | bytes 2949128 | tf_op jit(solution)/shard_map/ppermute | solution.py:243
  17.7 37.7 %collective-permute-start.20 = (bf16[128,3840]{1,0:T(8,128)(2,1)}, bf16[128,3840]{1,0:T(8,128)(2,1)}, u32[]{:S(2)}, u32[]{:S(2)}) collective-permute-start(bf16[128,3840]{1,0:T(8,128)(2,1)} %get-tuple-element.88), channel_id=1, source_target_pairs={{0,3},{1,0},{2,1},{3,2},{4,7},{5,4},{6,5},{7,6},{8,11},{9,8},{10,9... | collective-permute-start | bytes 2949128 | tf_op jit(solution)/shard_map/ppermute | solution.py:243
  18.9 2.2 %collective-permute-start = (bf16[14,128,128]{2,1,0:T(8,128)(2,1)}, bf16[14,128,128]{2,1,0:T(8,128)(2,1)}, u32[]{:S(2)}, u32[]{:S(2)}) collective-permute-start(bf16[14,128,128]{2,1,0:T(8,128)(2,1)} %param), channel_id=1, source_target_pairs={{0,16},{16,0},{32,48},{48,32},{64,80},{80,64},{96,112},{112,96},{1... | collective-permute-start | bytes 1376264 | tf_op jit(solution)/shard_map/cond/branch_0_fun/ppermute | solution.py:268
  35.1 1.5 copy-start.10
  39.7 32.0 %collective-permute-start.17 = (bf16[256,1792]{1,0:T(8,128)(2,1)}, bf16[256,1792]{1,0:T(8,128)(2,1)S(1)}, u32[]{:S(2)}, u32[]{:S(2)}) collective-permute-start(bf16[256,1792]{1,0:T(8,128)(2,1)} %get-tuple-element.86), channel_id=1, source_target_pairs={{0,4},{4,8},{8,12},{1,5},{5,9},{9,13},{2,6},{6,10},{10,14},{3,7},{... | collective-permute-start | bytes 2752520 | tf_op jit(solution)/shard_map/ppermute | solution.py:247
  51.8 24.5 %collective-permute-start.18 = (bf16[256,1792]{1,0:T(8,128)(2,1)}, bf16[256,1792]{1,0:T(8,128)(2,1)S(1)}, u32[]{:S(2)}, u32[]{:S(2)}) collective-permute-start(bf16[256,1792]{1,0:T(8,128)(2,1)} %get-tuple-element.86), channel_id=1, source_target_pairs={{12,8},{8,4},{4,0},{13,9},{9,5},{5,1},{14,10},{10,6},{6,2},{15,11}... | collective-permute-start | bytes 2752520 | tf_op jit(solution)/shard_map/ppermute | solution.py:251
  53.3 25.2 %collective-permute-start.23 = (bf16[128,2816]{1,0:T(8,128)(2,1)}, bf16[128,2816]{1,0:T(8,128)(2,1)S(1)}, u32[]{:S(2)}, u32[]{:S(2)}) collective-permute-start(bf16[128,2816]{1,0:T(8,128)(2,1)} %collective-permute-done.15), channel_id=1, source_target_pairs={{0,1},{1,2},{2,3},{3,0},{4,5},{5,6},{6,7},{7,4},{8,9},{9,10},{10,1... | collective-permute-start | bytes 2162696 | tf_op jit(solution)/shard_map/ppermute | solution.py:243
  53.4 25.1 %collective-permute-start.24 = (bf16[128,2816]{1,0:T(8,128)(2,1)}, bf16[128,2816]{1,0:T(8,128)(2,1)S(1)}, u32[]{:S(2)}, u32[]{:S(2)}) collective-permute-start(bf16[128,2816]{1,0:T(8,128)(2,1)} %collective-permute-done.16), channel_id=1, source_target_pairs={{0,3},{1,0},{2,1},{3,2},{4,7},{5,4},{6,5},{7,6},{8,11},{9,8},{10,9... | collective-permute-start | bytes 2162696 | tf_op jit(solution)/shard_map/ppermute | solution.py:243
  83.6 7.7 %collective-permute-start.21 = (bf16[256,1792]{1,0:T(8,128)(2,1)S(1)}, bf16[256,1792]{1,0:T(8,128)(2,1)S(1)}, u32[]{:S(2)}, u32[]{:S(2)}) collective-permute-start(bf16[256,1792]{1,0:T(8,128)(2,1)S(1)} %collective-permute-done.17), channel_id=1, source_target_pairs={{4,8},{8,12},{5,9},{9,13},{6,10},{10,14},{7,11},{11,15},{20,24},{2... | collective-permute-start | bytes 2752520 | tf_op jit(solution)/shard_map/ppermute | solution.py:247
  84.3 24.8 %collective-permute-start.22 = (bf16[256,1792]{1,0:T(8,128)(2,1)S(1)}, bf16[256,1792]{1,0:T(8,128)(2,1)S(1)}, u32[]{:S(2)}, u32[]{:S(2)}) collective-permute-start(bf16[256,1792]{1,0:T(8,128)(2,1)S(1)} %collective-permute-done.18), channel_id=1, source_target_pairs={{8,4},{4,0},{9,5},{5,1},{10,6},{6,2},{11,7},{7,3},{24,20},{20,16},... | collective-permute-start | bytes 2752520 | tf_op jit(solution)/shard_map/ppermute | solution.py:251
  109.3 22.6 %collective-permute-start.27 = (bf16[256,1792]{1,0:T(8,128)(2,1)S(1)}, bf16[256,1792]{1,0:T(8,128)(2,1)S(1)}, u32[]{:S(2)}, u32[]{:S(2)}) collective-permute-start(bf16[256,1792]{1,0:T(8,128)(2,1)S(1)} %get-tuple-element.124), channel_id=1, source_target_pairs={{0,4},{1,5},{2,6},{3,7},{16,20},{17,21},{18,22},{19,23},{32,36},{3... | collective-permute-start | bytes 2752520 | tf_op jit(solution)/shard_map/ppermute | solution.py:247
  112.1 19.8 %collective-permute-start.28 = (bf16[256,1792]{1,0:T(8,128)(2,1)S(1)}, bf16[256,1792]{1,0:T(8,128)(2,1)S(1)}, u32[]{:S(2)}, u32[]{:S(2)}) collective-permute-start(bf16[256,1792]{1,0:T(8,128)(2,1)S(1)} %get-tuple-element.123), channel_id=1, source_target_pairs={{12,8},{13,9},{14,10},{15,11},{28,24},{29,25},{30,26},{31,27},{44,... | collective-permute-start | bytes 2752520 | tf_op jit(solution)/shard_map/ppermute | solution.py:251
  117.0 15.3 %collective-permute-start.25 = (bf16[256,1792]{1,0:T(8,128)(2,1)S(1)}, bf16[256,1792]{1,0:T(8,128)(2,1)S(1)}, u32[]{:S(2)}, u32[]{:S(2)}) collective-permute-start(bf16[256,1792]{1,0:T(8,128)(2,1)S(1)} %collective-permute-done.21), channel_id=1, source_target_pairs={{8,12},{9,13},{10,14},{11,15},{24,28},{25,29},{26,30},{27,31},{40,... | collective-permute-start | bytes 2752520 | tf_op jit(solution)/shard_map/ppermute | solution.py:247
  117.7 24.0 %collective-permute-start.26 = (bf16[256,1792]{1,0:T(8,128)(2,1)S(1)}, bf16[256,1792]{1,0:T(8,128)(2,1)S(1)}, u32[]{:S(2)}, u32[]{:S(2)}) collective-permute-start(bf16[256,1792]{1,0:T(8,128)(2,1)S(1)} %collective-permute-done.22), channel_id=1, source_target_pairs={{4,0},{5,1},{6,2},{7,3},{20,16},{21,17},{22,18},{23,19},{36,32},{3... | collective-permute-start | bytes 2752520 | tf_op jit(solution)/shard_map/ppermute | solution.py:251
  142.9 12.7 %collective-permute-start.30 = (bf16[128,1792]{1,0:T(8,128)(2,1)S(1)}, bf16[128,1792]{1,0:T(8,128)(2,1)S(1)}, u32[]{:S(2)}, u32[]{:S(2)}) collective-permute-start(bf16[128,1792]{1,0:T(8,128)(2,1)S(1)} %get-tuple-element.107), channel_id=1, source_target_pairs={{0,3},{1,0},{2,1},{3,2},{4,7},{5,4},{6,5},{7,6},{8,11},{9,8},{10,9... | collective-permute-start | bytes 1376264 | tf_op jit(solution)/shard_map/ppermute | solution.py:243
  143.0 20.3 %collective-permute-start.31 = (bf16[256,1792]{1,0:T(8,128)(2,1)S(1)}, bf16[256,1792]{1,0:T(8,128)(2,1)S(1)}, u32[]{:S(2)}, u32[]{:S(2)}) collective-permute-start(bf16[256,1792]{1,0:T(8,128)(2,1)S(1)} %get-tuple-element.108), channel_id=1, source_target_pairs={{0,4},{4,8},{1,5},{5,9},{2,6},{6,10},{3,7},{7,11},{16,20},{20,24},... | collective-permute-start | bytes 2752520 | tf_op jit(solution)/shard_map/ppermute | solution.py:247
  144.5 18.8 %collective-permute-start.32 = (bf16[256,1792]{1,0:T(8,128)(2,1)S(1)}, bf16[256,1792]{1,0:T(8,128)(2,1)S(1)}, u32[]{:S(2)}, u32[]{:S(2)}) collective-permute-start(bf16[256,1792]{1,0:T(8,128)(2,1)S(1)} %get-tuple-element.109), channel_id=1, source_target_pairs={{12,8},{8,4},{13,9},{9,5},{14,10},{10,6},{15,11},{11,7},{28,24},{2... | collective-permute-start | bytes 2752520 | tf_op jit(solution)/shard_map/ppermute | solution.py:251
  145.2 14.5 %collective-permute-start.29 = (bf16[128,1792]{1,0:T(8,128)(2,1)S(1)}, bf16[128,1792]{1,0:T(8,128)(2,1)S(1)}, u32[]{:S(2)}, u32[]{:S(2)}) collective-permute-start(bf16[128,1792]{1,0:T(8,128)(2,1)S(1)} %get-tuple-element.105), channel_id=1, source_target_pairs={{0,1},{1,2},{2,3},{3,0},{4,5},{5,6},{6,7},{7,4},{8,9},{9,10},{10,1... | collective-permute-start | bytes 1376264 | tf_op jit(solution)/shard_map/ppermute | solution.py:243
  152.5 22.1 %collective-permute-start.36 = (bf16[128,1792]{1,0:T(8,128)(2,1)S(1)}, bf16[128,1792]{1,0:T(8,128)(2,1)S(1)}, u32[]{:S(2)}, u32[]{:S(2)}) collective-permute-start(bf16[128,1792]{1,0:T(8,128)(2,1)S(1)} %get-tuple-element.114), channel_id=1, source_target_pairs={{0,1},{1,2},{2,3},{3,0},{4,5},{5,6},{6,7},{7,4},{8,9},{9,10},{10,1... | collective-permute-start | bytes 1376264 | tf_op jit(solution)/shard_map/ppermute | solution.py:243
  159.8 32.8 %copy-start.6 = (bf16[1,256,1792]{2,1,0:T(8,128)(2,1)S(1)}, bf16[1,256,1792]{2,1,0:T(8,128)(2,1)}, u32[]{:S(2)}) copy-start(bf16[1,256,1792]{2,1,0:T(8,128)(2,1)} %param.26) | copy-start | bytes 2752516
  159.9 32.8 %copy-start.8 = (bf16[1,256,1792]{2,1,0:T(8,128)(2,1)S(1)}, bf16[1,256,1792]{2,1,0:T(8,128)(2,1)}, u32[]{:S(2)}) copy-start(bf16[1,256,1792]{2,1,0:T(8,128)(2,1)} %param.27) | copy-start | bytes 2752516
  163.7 31.0 %collective-permute-start.33 = (bf16[256,1792]{1,0:T(8,128)(2,1)S(1)}, bf16[256,1792]{1,0:T(8,128)(2,1)S(1)}, u32[]{:S(2)}, u32[]{:S(2)}) collective-permute-start(bf16[256,1792]{1,0:T(8,128)(2,1)S(1)} %get-tuple-element.110), channel_id=1, source_target_pairs={{0,4},{4,8},{8,12},{1,5},{5,9},{9,13},{2,6},{6,10},{10,14},{3,7},{... | collective-permute-start | bytes 2752520 | tf_op jit(solution)/shard_map/ppermute | solution.py:247
  170.0 24.7 %collective-permute-start.34 = (bf16[256,1792]{1,0:T(8,128)(2,1)S(1)}, bf16[256,1792]{1,0:T(8,128)(2,1)S(1)}, u32[]{:S(2)}, u32[]{:S(2)}) collective-permute-start(bf16[256,1792]{1,0:T(8,128)(2,1)S(1)} %get-tuple-element.111), channel_id=1, source_target_pairs={{12,8},{8,4},{4,0},{13,9},{9,5},{5,1},{14,10},{10,6},{6,2},{15,11}... | collective-permute-start | bytes 2752520 | tf_op jit(solution)/shard_map/ppermute | solution.py:251
  171.3 14.7 %collective-permute-start.37 = (bf16[128,1792]{1,0:T(8,128)(2,1)S(1)}, bf16[128,1792]{1,0:T(8,128)(2,1)S(1)}, u32[]{:S(2)}, u32[]{:S(2)}) collective-permute-start(bf16[128,1792]{1,0:T(8,128)(2,1)S(1)} %get-tuple-element.115), channel_id=1, source_target_pairs={{0,3},{1,0},{2,1},{3,2},{4,7},{5,4},{6,5},{7,6},{8,11},{9,8},{10,9... | collective-permute-start | bytes 1376264 | tf_op jit(solution)/shard_map/ppermute | solution.py:243
  171.4 14.7 %collective-permute-start.35 = (bf16[128,1792]{1,0:T(8,128)(2,1)S(1)}, bf16[128,1792]{1,0:T(8,128)(2,1)S(1)}, u32[]{:S(2)}, u32[]{:S(2)}) collective-permute-start(bf16[128,1792]{1,0:T(8,128)(2,1)S(1)} %add_convert_fusion.3), channel_id=1, source_target_pairs={{0,1},{1,2},{2,3},{3,0},{4,5},{5,6},{6,7},{7,4},{8,9},{9,10},{10,1... | collective-permute-start | bytes 1376264 | tf_op jit(solution)/shard_map/ppermute | solution.py:243
  174.6 18.0 %collective-permute-start.38 = (bf16[128,1792]{1,0:T(8,128)(2,1)S(1)}, bf16[128,1792]{1,0:T(8,128)(2,1)S(1)}, u32[]{:S(2)}, u32[]{:S(2)}) collective-permute-start(bf16[128,1792]{1,0:T(8,128)(2,1)S(1)} %add_convert_fusion.2), channel_id=1, source_target_pairs={{0,3},{1,0},{2,1},{3,2},{4,7},{5,4},{6,5},{7,6},{8,11},{9,8},{10,9... | collective-permute-start | bytes 1376264 | tf_op jit(solution)/shard_map/ppermute | solution.py:243

commit v4 on v3

v4 whole, which is shorter than its diff:
```python
import functools

import jax
import jax.numpy as jnp
from jax import lax
from jax.experimental import pallas as pl
from jax.experimental.pallas import tpu as pltpu
from jax.sharding import Mesh
from jax.sharding import PartitionSpec as P

TILE = 128
SIDE = 4
OUTER_RATE = 0.7
OUTER_MU = 0.9
ALL_VMEM = 60 * 2**20
VMEM = pl.BlockSpec(memory_space=pltpu.VMEM)
SMEM = pl.BlockSpec(memory_space=pltpu.SMEM)


def step_kernel(chosen_ref, outer_ref, local_ref, moment_ref, moved_ref, moment_out, theta_out, place):
    across = outer_ref.shape[1] // TILE
    half = pl.program_id(0)

    @pl.when(half == 0)
    def _():
        for t in range(place.shape[0]):
            place[t] = -1
        for i in range(moved_ref.shape[0]):
            place[chosen_ref[0, i]] = i

    for col in range(across):
        at = (slice(None), slice(col * TILE, (col + 1) * TILE))
        found = place[half * across + col]
        outer = outer_ref[at].astype(jnp.float32)
        delta = (outer - local_ref[at].astype(jnp.float32)).astype(jnp.bfloat16).astype(jnp.float32)
        other = moved_ref[jnp.maximum(found, 0)].astype(jnp.float32)
        mixed = jnp.where(found >= 0, 0.5 * (delta + other), delta)
        moment = OUTER_MU * moment_ref[at] + mixed
        moment_out[at] = moment
        theta_out[at] = (outer - OUTER_RATE * (mixed + OUTER_MU * moment)).astype(jnp.bfloat16)


def outer_step(chosen, outer, local_rows, moment, moved):
    rows, width = outer.shape
    block = pl.BlockSpec((TILE, width), lambda i: (i, 0))
    tiles = pl.BlockSpec(moved.shape, lambda i: (0, 0, 0))
    return pl.pallas_call(
        step_kernel,
        grid=(rows // TILE,),
        out_shape=[
            jax.ShapeDtypeStruct((rows, width), jnp.float32),
            jax.ShapeDtypeStruct((rows, width), jnp.bfloat16),
        ],
        in_specs=[SMEM, block, block, block, tiles],
        out_specs=[block, block],
        scratch_shapes=[pltpu.SMEM((rows // TILE * (width // TILE),), jnp.int32)],
        compiler_params=pltpu.CompilerParams(vmem_limit_bytes=ALL_VMEM),
        cost_estimate=pl.CostEstimate(flops=8 * rows * width, bytes_accessed=14 * rows * width, transcendentals=0),
        name="outer_step",
    )(chosen, outer, local_rows, moment, moved)


def prepare_kernel(
    where_ref, chosen_ref, outer_ref, local_ref, gate_ref, up_ref, cot_ref, picked_out, hid_out, cot_out, go_up, go_down
):
    step = pl.program_id(0)
    half, width = gate_ref.shape
    across = cot_out.shape[1]
    piece = across // SIDE
    far = width + across
    gate = gate_ref[...].astype(jnp.float32)
    hidden = (gate * jax.nn.sigmoid(gate) * up_ref[...].astype(jnp.float32)).astype(jnp.bfloat16)
    hid_out[...] = hidden

    def columns(by, to_ref, start):
        for k in range(SIDE):
            group = (where_ref[0] + k) % SIDE * SIDE
            at = pl.multiple_of((group + (where_ref[1] + by) % SIDE) * piece, piece)
            to_ref[:, start + k * piece : start + (k + 1) * piece] = cot_ref[:, pl.ds(at, piece)]

    columns(0, cot_out, 0)

    @pl.when(step == 0)
    def _():
        go_up[:, :width] = hidden
        columns(2, go_up, width)
        columns(1, go_up, far + width)
        go_down[:, far : far + width] = hidden
        columns(3, go_down, far + width)

    @pl.when(step == 1)
    def _():
        go_down[:, :width] = hidden
        columns(2, go_down, width)
        columns(3, go_down, far + width + across)
        go_up[:, far : far + width] = hidden
        columns(1, go_up, far + width + across)

    tiles = width // TILE
    for i in range(picked_out.shape[0]):
        tile = chosen_ref[0, i]

        @pl.when(tile // tiles == step)
        def _(i=i, tile=tile):
            at = (slice(None), pl.ds(pl.multiple_of(tile % tiles * TILE, TILE), TILE))
            delta = outer_ref[at].astype(jnp.float32) - local_ref[at].astype(jnp.float32)
            picked_out[i] = delta.astype(jnp.bfloat16)


def prepare(where, chosen, outer, local_rows, gate, up, cot_rows):
    rows, width = gate.shape
    depth = cot_rows.shape[1]
    half, across = rows // 2, depth // SIDE
    assert half == TILE
    sent = (half, 2 * width + 3 * across)
    picked = (chosen.shape[1], TILE, TILE)
    moved = lambda shape: jax.ShapeDtypeStruct(shape, jnp.bfloat16)
    block = lambda n: pl.BlockSpec((half, n), lambda i: (i, 0))
    whole = lambda shape: pl.BlockSpec(shape, lambda i: (0,) * len(shape))
    return pl.pallas_call(
        prepare_kernel,
        grid=(2,),
        out_shape=[moved(shape) for shape in (picked, (rows, width), (rows, across), sent, sent)],
        in_specs=[SMEM, SMEM] + [block(width)] * 4 + [block(depth)],
        out_specs=[whole(picked), block(width), block(across), whole(sent), whole(sent)],
        compiler_params=pltpu.CompilerParams(vmem_limit_bytes=ALL_VMEM),
        cost_estimate=pl.CostEstimate(flops=4 * rows * width, bytes_accessed=11 * 2**20, transcendentals=rows * width),
        name="prepare",
    )(where, chosen, outer, local_rows, gate, up, cot_rows)


def some_features(scale, cot_ref, hid_ref, which, out_ref):
    piece = cot_ref.shape[1] // SIDE
    features = cot_ref[:, which * piece : (which + 1) * piece]
    part = lax.dot_general(features, hid_ref[...], (((0,), (0,)), ((), ())), preferred_element_type=jnp.float32)
    out_ref[...] = (scale * part).astype(jnp.bfloat16)


def first_kernel(scale, hidden, own, go_up, go_down, last_up, last_down, cot_out, hid_out, up_out, down_out):
    rows, width = hidden.shape
    half, across = rows // 2, own.shape[1]
    near = width + across
    first, second = slice(near + width, near + width + across), slice(near + width + across, near + width + 2 * across)
    cot_out[:rows] = own[...]
    hid_out[:rows] = hidden[...]
    far, other = slice(0, width), slice(near, near + width)
    for n, (ref, tokens, features) in enumerate(
        (
            (go_down, other, first),
            (go_down, far, second),
            (last_up, far, slice(width, near)),
            (last_down, far, slice(width, near)),
            (go_up, far, first),
            (go_up, other, second),
        )
    ):
        to = slice(rows + n * half, rows + (n + 1) * half)
        cot_out[to] = ref[:, features]
        hid_out[to] = ref[:, tokens]
    some_features(scale, cot_out, hid_out, 3, up_out)
    some_features(scale, cot_out, hid_out, 1, down_out)


def first_parts(scale, hidden, own, *moved):
    rows, width = hidden.shape
    across = own.shape[1]
    sizes = [(SIDE * rows, across), (SIDE * rows, width), (across // SIDE, width), (across // SIDE, width)]
    return pl.pallas_call(
        functools.partial(first_kernel, scale),
        out_shape=[jax.ShapeDtypeStruct(size, jnp.bfloat16) for size in sizes],
        in_specs=[VMEM] * (2 + len(moved)),
        out_specs=[VMEM] * 4,
        compiler_params=pltpu.CompilerParams(vmem_limit_bytes=48 * 2**20),
        cost_estimate=pl.CostEstimate(flops=2**20, bytes_accessed=2**20, transcendentals=0),
        name="first_parts",
    )(hidden, own, *moved)


def other_kernel(scale, cot_ref, hid_ref, mid_out, own_out):
    some_features(scale, cot_ref, hid_ref, 2, mid_out)
    some_features(scale, cot_ref, hid_ref, 0, own_out)


def other_parts(scale, cot, hid):
    tokens, width = hid.shape
    piece = cot.shape[1] // SIDE
    return pl.pallas_call(
        functools.partial(other_kernel, scale),
        out_shape=[jax.ShapeDtypeStruct((piece, width), jnp.bfloat16)] * 2,
        in_specs=[VMEM] * 2,
        out_specs=[VMEM] * 2,
        compiler_params=pltpu.CompilerParams(vmem_limit_bytes=32 * 2**20),
        cost_estimate=pl.CostEstimate(flops=4 * tokens * piece * width, bytes_accessed=2**20, transcendentals=0),
        name="other_parts",
    )(cot, hid)


def early_kernel(where_ref, cot_ref, own, down1, up1, up2, down2, total_out):
    piece = own.shape[0]
    mid = jnp.where(where_ref[0] >= SIDE // 2, up2[...], down2[...])
    total = 0.0
    for k, block in enumerate((own[...], down1[...], mid, up1[...])):
        total = total + jnp.dot(cot_ref[:, k * piece : (k + 1) * piece], block, preferred_element_type=jnp.float32)
    total_out[...] = total


def early_products(where, cot, *blocks):
    rows, width = blocks[0].shape
    return pl.pallas_call(
        early_kernel,
        grid=(SIDE,),
        out_shape=jax.ShapeDtypeStruct((SIDE * rows, width), jnp.float32),
        in_specs=[SMEM, pl.BlockSpec((rows, cot.shape[1]), lambda i: (i, 0))]
        + [pl.BlockSpec((rows, width), lambda i: (0, 0))] * 5,
        out_specs=pl.BlockSpec((rows, width), lambda i: (i, 0)),
        compiler_params=pltpu.CompilerParams(vmem_limit_bytes=ALL_VMEM),
        cost_estimate=pl.CostEstimate(flops=2**20, bytes_accessed=2**20, transcendentals=0),
        name="early_products",
    )(where, cot, *blocks)


def with_last(z, total_ref, cot_ref, up3, down3, scale):
    piece = up3.shape[0]
    last = jnp.where(z == 0, down3[...], up3[...])
    far = jnp.where(z == 0, cot_ref[:, 3 * piece :], cot_ref[:, piece : 2 * piece])
    return (scale * (total_ref[...] + jnp.dot(far, last, preferred_element_type=jnp.float32))).astype(jnp.bfloat16)


def far_kernel(scale, where_ref, total_ref, cot_ref, up3, down3, top_out, low_out):
    half = top_out.shape[0]
    value = with_last(where_ref[0], total_ref, cot_ref, up3, down3, scale)
    top_out[...] = value[:half]
    low_out[...] = value[half:]


def near_kernel(scale, where_ref, total_ref, cot_ref, up3, down3, own_out, up_add, up_out, down_out, down_add):
    step = pl.program_id(0)
    half = up_add.shape[0]
    value = with_last(where_ref[0], total_ref, cot_ref, up3, down3, scale)
    targets = ((up_add, up_out), (down_out, down_add), (own_out.at[:half], own_out.at[half:]))
    for n, (top, low) in enumerate(targets):

        @pl.when(step == n)
        def _(top=top, low=low):
            top[...] = value[:half]
            low[...] = value[half:]


def last_products(which, where, total, cot, up3, down3, scale):
    rows, width = up3.shape
    half = rows // 2
    part = lambda n: jax.ShapeDtypeStruct((n, width), jnp.bfloat16)
    whole = lambda n: pl.BlockSpec((n, width), lambda i: (0, 0))
    if which == "far":
        body, outs, steps, chunk = far_kernel, [half, half], 1, lambda i: (2, 0)
    else:
        body, outs, steps, chunk = near_kernel, [rows, half, half, half, half], 3, lambda i: ((2 * i + 1) % 5 % 4, 0)
    return pl.pallas_call(
        functools.partial(body, scale),
        grid=(steps,),
        out_shape=[part(n) for n in outs],
        in_specs=[
            SMEM,
            pl.BlockSpec((rows, width), chunk),
            pl.BlockSpec((rows, cot.shape[1]), chunk),
            whole(rows),
            whole(rows),
        ],
        out_specs=[whole(n) for n in outs],
        compiler_params=pltpu.CompilerParams(vmem_limit_bytes=ALL_VMEM),
        cost_estimate=pl.CostEstimate(
            flops=4 * steps * rows * rows * width, bytes_accessed=(6 * steps + 4) * rows * width, transcendentals=0
        ),
        name=which + "_rows",
    )(where, total, cot, up3, down3)


def finish_kernel(gate_ref, up_ref, own_ref, top_up, low_up, top_down, low_down, gate_out, up_out):
    def write(first, second):
        grad = own_ref[...].astype(jnp.float32) + first[...].astype(jnp.float32) + second[...].astype(jnp.float32)
        gate = gate_ref[...].astype(jnp.float32)
        sig = jax.nn.sigmoid(gate)
        gate_out[...] = (grad * up_ref[...].astype(jnp.float32) * sig * (1.0 + gate * (1.0 - sig))).astype(jnp.bfloat16)
        up_out[...] = (grad * (gate * sig)).astype(jnp.bfloat16)

    @pl.when(pl.program_id(0) == 0)
    def _():
        write(top_up, top_down)

    @pl.when(pl.program_id(0) == 1)
    def _():
        write(low_up, low_down)


def finish(gate, up, own, top_up, low_up, top_down, low_down):
    rows, width = gate.shape
    block = pl.BlockSpec((rows // 2, width), lambda i: (i, 0))
    whole = pl.BlockSpec((rows // 2, width), lambda i: (0, 0))
    return pl.pallas_call(
        finish_kernel,
        grid=(2,),
        out_shape=[jax.ShapeDtypeStruct((rows, width), jnp.bfloat16)] * 2,
        in_specs=[block, block, block, whole, whole, whole, whole],
        out_specs=[block, block],
        compiler_params=pltpu.CompilerParams(vmem_limit_bytes=16 * 2**20),
        cost_estimate=pl.CostEstimate(flops=10 * rows * width, bytes_accessed=14 * rows * width, transcendentals=rows * width),
        name="finish",
    )(gate, up, own, top_up, low_up, top_down, low_down)


def tie(*values):
    return lax.optimization_barrier(values)


def turn(value, by):
    return lax.ppermute(value, "x", [(i, (i + by) % SIDE) for i in range(SIDE)])


def up_line(value, step):
    return lax.ppermute(value, "z", [(i, i + 1) for i in range(*step)])


def down_line(value, step):
    return lax.ppermute(value, "z", [(SIDE - 1 - i, SIDE - 2 - i) for i in range(*step)])


def add(a, b):
    return (a.astype(jnp.float32) + b.astype(jnp.float32)).astype(jnp.bfloat16)


def local(theta_outer, theta_local, momentum, gate_pre, up_pre, cotangent, partner, chosen):
    outer, local_rows, moment = theta_outer[0], theta_local[0], momentum[0]
    rows, width = outer.shape
    scale = width ** (-0.5)
    z, x = lax.axis_index("z"), lax.axis_index("x")
    my_rep = lax.axis_index("rep")
    replicas = lax.axis_size("rep")
    offset = jnp.bitwise_xor(partner[0, my_rep], my_rep)

    def to_partner(by):
        return lambda value: lax.ppermute(value, "rep", [(i, i ^ by) for i in range(replicas)])

    where = jnp.stack([z, x]).astype(jnp.int32)
    gate, upper = gate_pre[0], up_pre[0]
    picked, hidden, cot_own, go_up, go_down = prepare(where, chosen, outer, local_rows, gate, upper, cotangent[0])
    go_up, go_down = turn(go_up, 1), turn(go_down, -1)

    moved = lax.switch(offset - 1, [to_partner(by) for by in range(1, replicas)], picked)
    momentum_new, theta_new = outer_step(chosen, outer, local_rows, moment, moved)
    up1, down1 = up_line(theta_new, (0, 3)), down_line(theta_new, (0, 3))
    far = width + cot_own.shape[1]
    last_up, last_down = turn(go_up[:, :far], 1), turn(go_down[:, :far], -1)

    up2, down2 = up_line(up1, (1, 3)), down_line(down1, (1, 3))
    cot, hid, part_up, part_down = first_parts(scale, hidden, cot_own, go_up, go_down, last_up, last_down)
    sum_up, sum_down = up_line(part_up, (0, 1)), down_line(part_down, (0, 1))
    up3, down3 = up_line(up2, (2, 3)), down_line(down2, (2, 3))
    total = early_products(where, cot, theta_new, down1, up1, up2, down2)
    part_mid, part_own = other_parts(scale, cot, hid)
    sum_up, sum_down = add(part_mid, sum_up), add(part_mid, sum_down)
    sum_up, sum_down = up_line(sum_up, (0, 2)), down_line(sum_down, (0, 2))

    far_top, far_low = last_products("far", where, total, cot, up3, down3, scale)
    far_top, far_low = turn(far_top, 1), turn(far_low, -1)
    own, up_add, up_near, down_near, down_add = last_products("near", where, total, cot, up3, down3, scale)
    low_up, top_down = turn(up_near, 1), turn(down_near, -1)
    far_top, far_low, sum_up, sum_down = tie(far_top, far_low, sum_up, sum_down)
    sum_up, sum_down = add(part_down, sum_up), add(part_up, sum_down)
    sum_up, sum_down = up_line(sum_up, (0, 3)), down_line(sum_down, (0, 3))
    up_add, down_add = add(up_add, far_top), add(down_add, far_low)
    up_add, down_add, low_up, top_down = tie(up_add, down_add, low_up, top_down)

    top_up, low_down = turn(up_add, 1), turn(down_add, -1)
    grad_weight = part_own.astype(jnp.float32) + sum_up.astype(jnp.float32) + sum_down.astype(jnp.float32)
    grad_gate, grad_up = finish(gate, upper, own, top_up, low_up, top_down, low_down)
    return momentum_new[None], grad_weight.astype(jnp.bfloat16)[None], grad_gate[None], grad_up[None]


def solution(mesh):
    replicas, shards = mesh.devices.shape
    grid = Mesh(mesh.devices.reshape(replicas, shards // SIDE, SIDE), ("rep", "z", "x"))
    rows = P("rep", ("z", "x"), None)
    per_shard = P(("z", "x"), None)
    return jax.shard_map(
        local,
        mesh=grid,
        in_specs=(rows,) * 6 + (per_shard,) * 2,
        out_specs=(rows,) * 4,
        check_vma=False,
    )
```

time: 197 us -> 166 us (0.84)
  waiting for transfers between devices: 105 us -> 47 us
  Pallas kernels: 14.7 us -> 39 us
  starting transfers between devices: 45.4 us -> 62.7 us
  local copies, waits for them, and re-layouts: 17.6 us -> 5.55 us
  matrix products: 8.74 us -> 0 us
  other arithmetic: 2.52 us -> 7.7 us
    ppermute x6, waiting for transfers between devices: 31.9 us -> 7.2 us  [down_line(): lax.ppermute(value, 'z', [(SIDE - 1 - i, SIDE - 2 - i) for i in range(*st...]
    ppermute x12 -> x10, waiting for transfers between devices: 38.9 us -> 16.8 us  [turn(): return lax.ppermute(value, 'x', [(i, (i + by) % SIDE) for i in range(SIDE)])]
    ppermute x6, waiting for transfers between devices: 32.5 us -> 12.3 us  [up_line(): return lax.ppermute(value, 'z', [(i, i + 1) for i in range(*step)])]
    pallas_call x2 -> x4, Pallas kernels: 4.55 us -> 23.1 us  [the longest x1 8.69 us: early_products(): pl.pallas_call(early_kernel, grid=(SIDE,), out_shape=jax.ShapeDtypeStruct...]
    unnamed x38 -> x28, local copies, waits for them, and re-layouts: 14.7 us -> 4.88 us
    dot_general x2 -> x0, matrix products: 8.74 us -> none  [the longest x1 4.54 us: local(): lax.dot_general(cot, hid, (((0,), (0,)), ((), ())), preferred_element_typ...]
    ppermute x1, waiting for transfers between devices: 2.14 us -> 10.7 us  [to_partner(): lax.ppermute(value, 'rep', [(i, i ^ by) for i in range(replicas)])]
    ppermute x1, starting transfers between devices: 0.09 us -> 6.97 us  [to_partner(): lax.ppermute(value, 'rep', [(i, i ^ by) for i in range(replicas)])]
  transfers between devices with their start and end apart: 25 -> 23, of which waited for: 13 -> 10; matrix products, arithmetic and copies ran while one was open for 7% -> 4% of each run, Pallas kernels for 5% -> 20%
where the time goes in v4:
time: 166 us; the launch traced here: 164 us
  starting transfers between devices  62.7 us (38%)
  waiting for transfers between devices  47 us (28%)
  Pallas kernels  39 us (23%)
  other arithmetic  7.7 us (5%)
  local copies, waits for them, and re-layouts  5.55 us (3%)
    ppermute x6, starting transfers between devices, up_line(): return lax.ppermute(value, 'z', [(i, i + 1) for i in range(*step)])  30.9 us
    ppermute x10, starting transfers between devices, turn(): return lax.ppermute(value, 'x', [(i, (i + by) % SIDE) for i in range(SIDE)])  17.3 us
    ppermute x10, waiting for transfers between devices, turn(): return lax.ppermute(value, 'x', [(i, (i + by) % SIDE) for i in range(SIDE)])  16.8 us
    ppermute x6, waiting for transfers between devices, up_line(): return lax.ppermute(value, 'z', [(i, i + 1) for i in range(*step)])  12.3 us
    ppermute x1, waiting for transfers between devices, to_partner(): lax.ppermute(value, 'rep', [(i, i ^ by) for i in range(replicas)])  10.7 us
    pallas_call x2, Pallas kernels, last_products(): pl.pallas_call(functools.partial(body, scale), grid=(steps,), out_shape=[...  10 us
    pallas_call x1, Pallas kernels, early_products(): pl.pallas_call(early_kernel, grid=(SIDE,), out_shape=jax.ShapeDtypeStruct...  8.69 us
    ppermute x6, starting transfers between devices, down_line(): lax.ppermute(value, 'z', [(SIDE - 1 - i, SIDE - 2 - i) for i in range(*st...  7.58 us
  transfers between devices with their start and end apart: 23, of which 10 were waited for; matrix products, arithmetic and copies ran while one was open for 4% of the time, Pallas kernels for 20%

profile of v4, /device:TPU:6, one launch (start us, length us, event | category | flops | bytes accessed | tf_op | source)
XLA Modules:
  0.0 163.6 jit_solution(17436935262583025563)
XLA Ops:
  0.6 0.0 copy-start
  0.7 0.7 pad_add_fusion.where_ref
  1.3 5.6 %prepare.1 = (bf16[14,128,128]{2,1,0:T(8,128)(2,1)}, bf16[256,1792]{1,0:T(8,128)(2,1)}, bf16[256,1024]{1,0:T(8,128)(2,1)}, bf16[128,6656]{1,0:T(8,128)(2,1)}, bf16[128,6656]{1,0:T(8,128)(2,1)}) custom-call(s32[2]{0:T(128)} %pad_add_fusion.where_ref, s32[1,14]{1,0:T(1,128)} %chosen_ref.3, bf16[256,1792]{1,0:T(8,128)(2,1)} %bitcast.18, ...), custom_call_target="tpu_custom_call" | custom-call | flops 1835008 | bytes 11534336 | tf_op jit(solution)/shard_map/prepare/pallas_call | solution.py:120
  6.9 2.3 %collective-permute-start.15 = (bf16[128,6656]{1,0:T(8,128)(2,1)}, bf16[128,6656]{1,0:T(8,128)(2,1)S(1)}, u32[]{:S(2)}, u32[]{:S(2)}) collective-permute-start(bf16[128,6656]{1,0:T(8,128)(2,1)} %get-tuple-element.69), channel_id=1, source_target_pairs={{0,1},{1,2},{2,3},{3,0},{4,5},{5,6},{6,7},{7,4},{8,9},{9,10},{10,1... | collective-permute-start | bytes 5111816 | tf_op jit(solution)/shard_map/ppermute | solution.py:316
  9.2 0.0 collective-permute-start.16
  9.2 0.6 constant_dynamic-slice_fusion
  10.4 17.7 %conditional.1 = (bf16[14,128,128]{2,1,0:T(8,128)(2,1)}) conditional(s32[]{:T(128)} %clamp.3, bf16[14,128,128]{2,1,0:T(8,128)(2,1)} %get-tuple-element.65, bf16[14,128,128]{2,1,0:T(8,128)(2,1)} %get-tuple-element.65, bf16[14,128,128]{2,1,0:T(8,128)(2,1)} %get-tuple-element.65, ...), branch_computations={%region_0.0_spmd, %region_1.0_spmd, %region_2.0_spmd, %region_3.0_... | conditional | bytes 1835056 | solution.py:348
  10.5 7.0 %collective-permute-start.6 = (bf16[14,128,128]{2,1,0:T(8,128)(2,1)}, bf16[14,128,128]{2,1,0:T(8,128)(2,1)}, u32[]{:S(2)}, u32[]{:S(2)}) collective-permute-start(bf16[14,128,128]{2,1,0:T(8,128)(2,1)} %param.6), channel_id=1, source_target_pairs={{0,112},{16,96},{32,80},{48,64},{64,48},{80,32},{96,16},{112,0},{1... | collective-permute-start | bytes 1376264 | tf_op jit(solution)/shard_map/cond/branch_6_fun/ppermute | solution.py:341
  17.4 10.7 %collective-permute-done.6 = bf16[14,128,128]{2,1,0:T(8,128)(2,1)} collective-permute-done((bf16[14,128,128]{2,1,0:T(8,128)(2,1)}, bf16[14,128,128]{2,1,0:T(8,128)(2,1)}, u32[]{:S(2)}, u32[]{:S(2)}) %collective-permute-start.6) | collective-permute-done | bytes 458784 | tf_op jit(solution)/shard_map/cond/branch_6_fun/ppermute | solution.py:341
  28.2 3.8 %outer_step.1 = (f32[256,1792]{1,0:T(8,128)}, bf16[256,1792]{1,0:T(8,128)(2,1)}) custom-call(s32[1,14]{1,0:T(1,128)} %chosen_ref.3, bf16[256,1792]{1,0:T(8,128)(2,1)} %bitcast.19, bf16[256,1792]{1,0:T(8,128)(2,1)} %bitcast.21, f32[256,1792]{1,0:T(8,128)} %bitcast.23, bf16[14,128,128]{2,1,0:T(8,128)(2,1)} %get-tuple-element.99.moved_ref), custom_call_target="tpu_custom_call" | custom-call | flops 3670016 | bytes 6422528 | tf_op jit(solution)/shard_map/outer_step/pallas_call | solution.py:47
  32.0 12.9 %collective-permute-start.20 = (bf16[256,1792]{1,0:T(8,128)(2,1)}, bf16[256,1792]{1,0:T(8,128)(2,1)S(1)}, u32[]{:S(2)}, u32[]{:S(2)}) collective-permute-start(bf16[256,1792]{1,0:T(8,128)(2,1)} %get-tuple-element.75.own), channel_id=1, source_target_pairs={{0,4},{4,8},{8,12},{1,5},{5,9},{9,13},{2,6},{6,10},{10,14},{3,7},{... | collective-permute-start | bytes 2752520 | tf_op jit(solution)/shard_map/ppermute | solution.py:320
  44.9 1.3 collective-permute-start.19
  46.2 0.0 collective-permute-done.15.go_up
  46.2 1.2 copy-done.8
  47.5 3.4 %collective-permute-start.17 = (bf16[128,2816]{1,0:T(8,128)(2,1)S(1)}, bf16[128,2816]{1,0:T(8,128)(2,1)S(1)}, u32[]{:S(2)}, u32[]{:S(2)}) collective-permute-start(bf16[128,2816]{1,0:T(8,128)(2,1)S(1)} %slice.8), channel_id=1, source_target_pairs={{0,1},{1,2},{2,3},{3,0},{4,5},{5,6},{6,7},{7,4},{8,9},{9,10},{10,1... | collective-permute-start | bytes 2162696 | tf_op jit(solution)/shard_map/ppermute | solution.py:316
  50.8 0.0 collective-permute-done.16.go_down
  50.9 0.1 collective-permute-start.18
  51.0 7.6 %collective-permute-done.20.up1 = bf16[256,1792]{1,0:T(8,128)(2,1)S(1)} collective-permute-done((bf16[256,1792]{1,0:T(8,128)(2,1)}, bf16[256,1792]{1,0:T(8,128)(2,1)S(1)}, u32[]{:S(2)}, u32[]{:S(2)}) %collective-permute-start.20) | collective-permute-done | bytes 917536 | tf_op jit(solution)/shard_map/ppermute | solution.py:320
  58.6 1.6 collective-permute-start.21
  60.2 2.5 %collective-permute-done.19.down1 = bf16[256,1792]{1,0:T(8,128)(2,1)S(1)} collective-permute-done((bf16[256,1792]{1,0:T(8,128)(2,1)}, bf16[256,1792]{1,0:T(8,128)(2,1)S(1)}, u32[]{:S(2)}, u32[]{:S(2)}) %collective-permute-start.19) | collective-permute-done | bytes 917536 | tf_op jit(solution)/shard_map/ppermute | solution.py:324
  62.7 1.3 collective-permute-start.22
  64.0 2.4 %collective-permute-done.17.last_up = bf16[128,2816]{1,0:T(8,128)(2,1)S(1)} collective-permute-done((bf16[128,2816]{1,0:T(8,128)(2,1)S(1)}, bf16[128,2816]{1,0:T(8,128)(2,1)S(1)}, u32[]{:S(2)}, u32[]{:S(2)}) %collective-permute-start.17) | collective-permute-done | bytes 720928 | tf_op jit(solution)/shard_map/ppermute | solution.py:316
  66.3 3.5 %collective-permute-done.18.last_down = bf16[128,2816]{1,0:T(8,128)(2,1)S(1)} collective-permute-done((bf16[128,2816]{1,0:T(8,128)(2,1)S(1)}, bf16[128,2816]{1,0:T(8,128)(2,1)S(1)}, u32[]{:S(2)}, u32[]{:S(2)}) %collective-permute-start.18) | collective-permute-done | bytes 720928 | tf_op jit(solution)/shard_map/ppermute | solution.py:316
  69.9 6.7 %first_parts.1 = (bf16[1024,1024]{1,0:T(8,128)(2,1)}, bf16[1024,1792]{1,0:T(8,128)(2,1)}, bf16[256,1792]{1,0:T(8,128)(2,1)S(1)}, bf16[256,1792]{1,0:T(8,128)(2,1)S(1)}) custom-call(bf16[256,1792]{1,0:T(8,128)(2,1)S(1)} %copy-done.4, bf16[256,1024]{1,0:T(8,128)(2,1)S(1)} %copy-done.6, bf16[128,6656]{1,0:T(8,128)(2,1)} %copy-done.8, ...), custom_call_target="tpu_custom_call" | custom-call | flops 1048576 | bytes 1048576 | tf_op jit(solution)/shard_map/first_parts/pallas_call | solution.py:168
  76.6 0.7 collective-permute-start.29
  77.3 4.3 %collective-permute-start.27 = (bf16[256,1792]{1,0:T(8,128)(2,1)S(1)}, bf16[256,1792]{1,0:T(8,128)(2,1)S(1)}, u32[]{:S(2)}, u32[]{:S(2)}) collective-permute-start(bf16[256,1792]{1,0:T(8,128)(2,1)S(1)} %get-tuple-element.79), channel_id=1, source_target_pairs={{0,4},{1,5},{2,6},{3,7},{16,20},{17,21},{18,22},{19,23},{32,36},{3... | collective-permute-start | bytes 2752520 | tf_op jit(solution)/shard_map/ppermute | solution.py:320
  81.6 1.6 collective-permute-start.23
  83.3 4.7 %collective-permute-done.22.down2 = bf16[256,1792]{1,0:T(8,128)(2,1)} collective-permute-done((bf16[256,1792]{1,0:T(8,128)(2,1)S(1)}, bf16[256,1792]{1,0:T(8,128)(2,1)}, u32[]{:S(2)}, u32[]{:S(2)}) %collective-permute-start.22) | collective-permute-done | bytes 917536 | tf_op jit(solution)/shard_map/ppermute | solution.py:324
  88.0 1.3 collective-permute-start.24
  89.3 1.6 copy-done.1
  90.9 2.0 %copy-done.7 = bf16[1024,1792]{1,0:T(8,128)(2,1)S(1)} copy-done((bf16[1024,1792]{1,0:T(8,128)(2,1)S(1)}, bf16[1024,1792]{1,0:T(8,128)(2,1)}, u32[]{:S(2)}) %copy-start.7) | copy-done | bytes 3670040
  92.9 2.1 %other_parts.1 = (bf16[256,1792]{1,0:T(8,128)(2,1)S(1)}, bf16[256,1792]{1,0:T(8,128)(2,1)S(1)}) custom-call(bf16[1024,1024]{1,0:T(8,128)(2,1)S(1)} %copy-done.1, bf16[1024,1792]{1,0:T(8,128)(2,1)S(1)} %copy-done.7), custom_call_target="tpu_custom_call" | custom-call | flops 1879048192 | bytes 1048576 | tf_op jit(solution)/shard_map/other_parts/pallas_call | solution.py:187
  95.1 0.0 collective-permute-done.29
  95.1 4.7 %collective-permute-done.27 = bf16[256,1792]{1,0:T(8,128)(2,1)S(1)} collective-permute-done((bf16[256,1792]{1,0:T(8,128)(2,1)S(1)}, bf16[256,1792]{1,0:T(8,128)(2,1)S(1)}, u32[]{:S(2)}, u32[]{:S(2)}) %collective-permute-start.27) | collective-permute-done | bytes 917536 | tf_op jit(solution)/shard_map/ppermute | solution.py:320
  99.8 1.6 fusion.1
  101.4 5.3 %collective-permute-start.28 = (bf16[256,1792]{1,0:T(8,128)(2,1)}, bf16[256,1792]{1,0:T(8,128)(2,1)}, u32[]{:S(2)}, u32[]{:S(2)}) collective-permute-start(bf16[256,1792]{1,0:T(8,128)(2,1)} %get-tuple-element.96), channel_id=1, source_target_pairs={{0,4},{4,8},{1,5},{5,9},{2,6},{6,10},{3,7},{7,11},{16,20},{20,24},... | collective-permute-start | bytes 2752520 | tf_op jit(solution)/shard_map/ppermute | solution.py:320
  106.7 1.6 collective-permute-start.30
  108.3 8.7 %early_products.1.total_ref = f32[1024,1792]{1,0:T(8,128)} custom-call(s32[2]{0:T(128)} %pad_add_fusion.where_ref, bf16[1024,1024]{1,0:T(8,128)(2,1)} %get-tuple-element.71.cot_ref, bf16[256,1792]{1,0:T(8,128)(2,1)} %get-tuple-element.75.own, bf16[256,1792]{1,0:T(8,128)(2,1)} %copy-done.11, bf16[256,1792]{1,0:T(8,128)(2,1)} %copy-done.10, ...), custom_call_target="tpu_custom_call" | custom-call | flops 1048576 | bytes 1048576 | tf_op jit(solution)/shard_map/early_products/pallas_call | solution.py:209
  117.0 0.0 collective-permute-done.23.up3
  117.0 0.0 collective-permute-done.24.down3
  117.0 3.5 %far_rows.1 = (bf16[128,1792]{1,0:T(8,128)(2,1)}, bf16[128,1792]{1,0:T(8,128)(2,1)}) custom-call(s32[2]{0:T(128)} %pad_add_fusion.where_ref, f32[1024,1792]{1,0:T(8,128)} %early_products.1.total_ref, bf16[1024,1024]{1,0:T(8,128)(2,1)} %get-tuple-element.71.cot_ref, bf16[256,1792]{1,0:T(8,128)(2,1)} %collective-permute-done.23.up3, ...), custom_call_target="tpu_custom_call" | custom-call | flops 469762048 | bytes 4587520 | tf_op jit(solution)/shard_map/far_rows/pallas_call | solution.py:258
  120.5 4.5 %collective-permute-start.25 = (bf16[128,1792]{1,0:T(8,128)(2,1)}, bf16[128,1792]{1,0:T(8,128)(2,1)S(1)}, u32[]{:S(2)}, u32[]{:S(2)}) collective-permute-start(bf16[128,1792]{1,0:T(8,128)(2,1)} %get-tuple-element.76), channel_id=1, source_target_pairs={{0,1},{1,2},{2,3},{3,0},{4,5},{5,6},{6,7},{7,4},{8,9},{9,10},{10,1... | collective-permute-start | bytes 1376264 | tf_op jit(solution)/shard_map/ppermute | solution.py:316
  125.0 1.0 collective-permute-start.26
  126.0 6.5 %near_rows.1 = (bf16[256,1792]{1,0:T(8,128)(2,1)}, bf16[128,1792]{1,0:T(8,128)(2,1)}, bf16[128,1792]{1,0:T(8,128)(2,1)}, bf16[128,1792]{1,0:T(8,128)(2,1)}, bf16[128,1792]{1,0:T(8,128)(2,1)}) custom-call(s32[2]{0:T(128)} %pad_add_fusion.where_ref, f32[1024,1792]{1,0:T(8,128)} %early_products.1.total_ref, bf16[1024,1024]{1,0:T(8,128)(2,1)} %get-tuple-element.71.cot_ref, ...), custom_call_target="tpu_custom_call" | custom-call | flops 1409286144 | bytes 10092544 | tf_op jit(solution)/shard_map/near_rows/pallas_call | solution.py:258
  132.5 2.2 %collective-permute-start.33 = (bf16[128,1792]{1,0:T(8,128)(2,1)}, bf16[128,1792]{1,0:T(8,128)(2,1)S(1)}, u32[]{:S(2)}, u32[]{:S(2)}) collective-permute-start(bf16[128,1792]{1,0:T(8,128)(2,1)} %get-tuple-element.87), channel_id=1, source_target_pairs={{0,1},{1,2},{2,3},{3,0},{4,5},{5,6},{6,7},{7,4},{8,9},{9,10},{10,1... | collective-permute-start | bytes 1376264 | tf_op jit(solution)/shard_map/ppermute | solution.py:316
  134.7 1.7 %collective-permute-done.25 = bf16[128,1792]{1,0:T(8,128)(2,1)S(1)} collective-permute-done((bf16[128,1792]{1,0:T(8,128)(2,1)}, bf16[128,1792]{1,0:T(8,128)(2,1)S(1)}, u32[]{:S(2)}, u32[]{:S(2)}) %collective-permute-start.25) | collective-permute-done | bytes 458784 | tf_op jit(solution)/shard_map/ppermute | solution.py:316
  136.4 1.7 %collective-permute-start.34 = (bf16[128,1792]{1,0:T(8,128)(2,1)}, bf16[128,1792]{1,0:T(8,128)(2,1)S(1)}, u32[]{:S(2)}, u32[]{:S(2)}) collective-permute-start(bf16[128,1792]{1,0:T(8,128)(2,1)} %get-tuple-element.88), channel_id=1, source_target_pairs={{0,3},{1,0},{2,1},{3,2},{4,7},{5,4},{6,5},{7,6},{8,11},{9,8},{10,9... | collective-permute-start | bytes 1376264 | tf_op jit(solution)/shard_map/ppermute | solution.py:316
  138.1 1.4 add_convert_fusion.1
  139.6 1.4 collective-permute-start.32
  141.0 1.4 add_convert_fusion.2
  142.4 0.0 copy-start.2
  142.5 0.0 copy-start.3
  142.5 0.0 copy-start.5
  142.5 5.1 %collective-permute-start.31 = (bf16[256,1792]{1,0:T(8,128)(2,1)S(1)}, bf16[256,1792]{1,0:T(8,128)(2,1)S(1)}, u32[]{:S(2)}, u32[]{:S(2)}) collective-permute-start(bf16[256,1792]{1,0:T(8,128)(2,1)S(1)} %add_convert_fusion.2), channel_id=1, source_target_pairs={{0,4},{4,8},{8,12},{1,5},{5,9},{9,13},{2,6},{6,10},{10,14},{3,7},{... | collective-permute-start | bytes 2752520 | tf_op jit(solution)/shard_map/ppermute | solution.py:320
  147.6 1.2 add_convert_fusion.3
  148.8 0.0 collective-permute-done.33.low_up
  148.9 1.6 collective-permute-start.35
  150.4 0.5 collective-permute-start.36
  151.0 6.5 %collective-permute-done.35.top_up = bf16[128,1792]{1,0:T(8,128)(2,1)S(1)} collective-permute-done((bf16[128,1792]{1,0:T(8,128)(2,1)S(1)}, bf16[128,1792]{1,0:T(8,128)(2,1)S(1)}, u32[]{:S(2)}, u32[]{:S(2)}) %collective-permute-start.35) | collective-permute-done | bytes 458784 | tf_op jit(solution)/shard_map/ppermute | solution.py:316
  157.4 2.7 %collective-permute-done.36.low_down = bf16[128,1792]{1,0:T(8,128)(2,1)S(1)} collective-permute-done((bf16[128,1792]{1,0:T(8,128)(2,1)S(1)}, bf16[128,1792]{1,0:T(8,128)(2,1)S(1)}, u32[]{:S(2)}, u32[]{:S(2)}) %collective-permute-start.36) | collective-permute-done | bytes 458784 | tf_op jit(solution)/shard_map/ppermute | solution.py:316
  160.1 2.1 %finish.1 = (bf16[256,1792]{1,0:T(8,128)(2,1)}, bf16[256,1792]{1,0:T(8,128)(2,1)}) custom-call(bf16[256,1792]{1,0:T(8,128)(2,1)S(1)} %bitcast.15, bf16[256,1792]{1,0:T(8,128)(2,1)S(1)} %bitcast.17, bf16[256,1792]{1,0:T(8,128)(2,1)S(1)} %copy-done.5, bf16[128,1792]{1,0:T(8,128)(2,1)S(1)} %collective-permute-done.35.top_up, ...), custom_call_target="tpu_custom_call" | custom-call | flops 4587520 | bytes 6422528 | tf_op jit(solution)/shard_map/finish/pallas_call | solution.py:299
  162.3 0.0 collective-permute-done.32
  162.3 0.0 collective-permute-done.31
  162.3 1.3 fusion.2
  (28 shorter events, 0.1 us)
Async XLA Ops:
  0.6 8.6 %copy-start = (s32[1,16]{1,0:T(1,128)S(1)}, s32[1,16]{1,0:T(1,128)}, u32[]{:S(2)}) copy-start(s32[1,16]{1,0:T(1,128)} %param.29) | copy-start | bytes 196
  6.9 39.3 %collective-permute-start.15 = (bf16[128,6656]{1,0:T(8,128)(2,1)}, bf16[128,6656]{1,0:T(8,128)(2,1)S(1)}, u32[]{:S(2)}, u32[]{:S(2)}) collective-permute-start(bf16[128,6656]{1,0:T(8,128)(2,1)} %get-tuple-element.69), channel_id=1, source_target_pairs={{0,1},{1,2},{2,3},{3,0},{4,5},{5,6},{6,7},{7,4},{8,9},{9,10},{10,1... | collective-permute-start | bytes 5111816 | tf_op jit(solution)/shard_map/ppermute | solution.py:316
  9.2 41.7 %collective-permute-start.16 = (bf16[128,6656]{1,0:T(8,128)(2,1)}, bf16[128,6656]{1,0:T(8,128)(2,1)S(1)}, u32[]{:S(2)}, u32[]{:S(2)}) collective-permute-start(bf16[128,6656]{1,0:T(8,128)(2,1)} %get-tuple-element.70), channel_id=1, source_target_pairs={{0,3},{1,0},{2,1},{3,2},{4,7},{5,4},{6,5},{7,6},{8,11},{9,8},{10,9... | collective-permute-start | bytes 5111816 | tf_op jit(solution)/shard_map/ppermute | solution.py:316
  10.5 17.7 %collective-permute-start.6 = (bf16[14,128,128]{2,1,0:T(8,128)(2,1)}, bf16[14,128,128]{2,1,0:T(8,128)(2,1)}, u32[]{:S(2)}, u32[]{:S(2)}) collective-permute-start(bf16[14,128,128]{2,1,0:T(8,128)(2,1)} %param.6), channel_id=1, source_target_pairs={{0,112},{16,96},{32,80},{48,64},{64,48},{80,32},{96,16},{112,0},{1... | collective-permute-start | bytes 1376264 | tf_op jit(solution)/shard_map/cond/branch_6_fun/ppermute | solution.py:341
  32.0 37.9 %copy-start.4 = (bf16[256,1792]{1,0:T(8,128)(2,1)S(1)}, bf16[256,1792]{1,0:T(8,128)(2,1)}, u32[]{:S(2)}) copy-start(bf16[256,1792]{1,0:T(8,128)(2,1)} %get-tuple-element.67.hidden) | copy-start | bytes 2752516
  32.0 37.9 %copy-start.6 = (bf16[256,1024]{1,0:T(8,128)(2,1)S(1)}, bf16[256,1024]{1,0:T(8,128)(2,1)}, u32[]{:S(2)}) copy-start(bf16[256,1024]{1,0:T(8,128)(2,1)} %get-tuple-element.68.own) | copy-start | bytes 1572868
  32.0 26.6 %collective-permute-start.20 = (bf16[256,1792]{1,0:T(8,128)(2,1)}, bf16[256,1792]{1,0:T(8,128)(2,1)S(1)}, u32[]{:S(2)}, u32[]{:S(2)}) collective-permute-start(bf16[256,1792]{1,0:T(8,128)(2,1)} %get-tuple-element.75.own), channel_id=1, source_target_pairs={{0,4},{4,8},{8,12},{1,5},{5,9},{9,13},{2,6},{6,10},{10,14},{3,7},{... | collective-permute-start | bytes 2752520 | tf_op jit(solution)/shard_map/ppermute | solution.py:320
  44.9 17.8 %collective-permute-start.19 = (bf16[256,1792]{1,0:T(8,128)(2,1)}, bf16[256,1792]{1,0:T(8,128)(2,1)S(1)}, u32[]{:S(2)}, u32[]{:S(2)}) collective-permute-start(bf16[256,1792]{1,0:T(8,128)(2,1)} %get-tuple-element.75.own), channel_id=1, source_target_pairs={{12,8},{8,4},{4,0},{13,9},{9,5},{5,1},{14,10},{10,6},{6,2},{15,11}... | collective-permute-start | bytes 2752520 | tf_op jit(solution)/shard_map/ppermute | solution.py:324
  46.2 1.2 copy-start.8
  47.5 18.9 %collective-permute-start.17 = (bf16[128,2816]{1,0:T(8,128)(2,1)S(1)}, bf16[128,2816]{1,0:T(8,128)(2,1)S(1)}, u32[]{:S(2)}, u32[]{:S(2)}) collective-permute-start(bf16[128,2816]{1,0:T(8,128)(2,1)S(1)} %slice.8), channel_id=1, source_target_pairs={{0,1},{1,2},{2,3},{3,0},{4,5},{5,6},{6,7},{7,4},{8,9},{9,10},{10,1... | collective-permute-start | bytes 2162696 | tf_op jit(solution)/shard_map/ppermute | solution.py:316
  50.8 19.0 %copy-start.9 = (bf16[128,6656]{1,0:T(8,128)(2,1)}, bf16[128,6656]{1,0:T(8,128)(2,1)S(1)}, u32[]{:S(2)}) copy-start(bf16[128,6656]{1,0:T(8,128)(2,1)S(1)} %collective-permute-done.16.go_down) | copy-start | bytes 5111812
  50.9 19.0 %collective-permute-start.18 = (bf16[128,2816]{1,0:T(8,128)(2,1)S(1)}, bf16[128,2816]{1,0:T(8,128)(2,1)S(1)}, u32[]{:S(2)}, u32[]{:S(2)}) collective-permute-start(bf16[128,2816]{1,0:T(8,128)(2,1)S(1)} %slice.9), channel_id=1, source_target_pairs={{0,3},{1,0},{2,1},{3,2},{4,7},{5,4},{6,5},{7,6},{8,11},{9,8},{10,9... | collective-permute-start | bytes 2162696 | tf_op jit(solution)/shard_map/ppermute | solution.py:316
  58.6 18.0 %copy-start.10 = (bf16[256,1792]{1,0:T(8,128)(2,1)}, bf16[256,1792]{1,0:T(8,128)(2,1)S(1)}, u32[]{:S(2)}) copy-start(bf16[256,1792]{1,0:T(8,128)(2,1)S(1)} %collective-permute-done.20.up1) | copy-start | bytes 2752516
  58.6 23.0 %collective-permute-start.21 = (bf16[256,1792]{1,0:T(8,128)(2,1)S(1)}, bf16[256,1792]{1,0:T(8,128)(2,1)}, u32[]{:S(2)}, u32[]{:S(2)}) collective-permute-start(bf16[256,1792]{1,0:T(8,128)(2,1)S(1)} %collective-permute-done.20.up1), channel_id=1, source_target_pairs={{4,8},{8,12},{5,9},{9,13},{6,10},{10,14},{7,11},{11,15},{20,24},{2... | collective-permute-start | bytes 2752520 | tf_op jit(solution)/shard_map/ppermute | solution.py:320
  62.7 13.9 %copy-start.11 = (bf16[256,1792]{1,0:T(8,128)(2,1)}, bf16[256,1792]{1,0:T(8,128)(2,1)S(1)}, u32[]{:S(2)}) copy-start(bf16[256,1792]{1,0:T(8,128)(2,1)S(1)} %collective-permute-done.19.down1) | copy-start | bytes 2752516
  62.7 25.3 %collective-permute-start.22 = (bf16[256,1792]{1,0:T(8,128)(2,1)S(1)}, bf16[256,1792]{1,0:T(8,128)(2,1)}, u32[]{:S(2)}, u32[]{:S(2)}) collective-permute-start(bf16[256,1792]{1,0:T(8,128)(2,1)S(1)} %collective-permute-done.19.down1), channel_id=1, source_target_pairs={{8,4},{4,0},{9,5},{5,1},{10,6},{6,2},{11,7},{7,3},{24,20},{20,16},... | collective-permute-start | bytes 2752520 | tf_op jit(solution)/shard_map/ppermute | solution.py:324
  76.6 18.5 %collective-permute-start.29 = (bf16[256,1792]{1,0:T(8,128)(2,1)S(1)}, bf16[256,1792]{1,0:T(8,128)(2,1)S(1)}, u32[]{:S(2)}, u32[]{:S(2)}) collective-permute-start(bf16[256,1792]{1,0:T(8,128)(2,1)S(1)} %get-tuple-element.74), channel_id=1, source_target_pairs={{12,8},{13,9},{14,10},{15,11},{28,24},{29,25},{30,26},{31,27},{44,... | collective-permute-start | bytes 2752520 | tf_op jit(solution)/shard_map/ppermute | solution.py:324
  77.3 22.5 %collective-permute-start.27 = (bf16[256,1792]{1,0:T(8,128)(2,1)S(1)}, bf16[256,1792]{1,0:T(8,128)(2,1)S(1)}, u32[]{:S(2)}, u32[]{:S(2)}) collective-permute-start(bf16[256,1792]{1,0:T(8,128)(2,1)S(1)} %get-tuple-element.79), channel_id=1, source_target_pairs={{0,4},{1,5},{2,6},{3,7},{16,20},{17,21},{18,22},{19,23},{32,36},{3... | collective-permute-start | bytes 2752520 | tf_op jit(solution)/shard_map/ppermute | solution.py:320
  81.6 35.3 %collective-permute-start.23 = (bf16[256,1792]{1,0:T(8,128)(2,1)}, bf16[256,1792]{1,0:T(8,128)(2,1)}, u32[]{:S(2)}, u32[]{:S(2)}) collective-permute-start(bf16[256,1792]{1,0:T(8,128)(2,1)} %collective-permute-done.21.up2), channel_id=1, source_target_pairs={{8,12},{9,13},{10,14},{11,15},{24,28},{25,29},{26,30},{27,31},{40,... | collective-permute-start | bytes 2752520 | tf_op jit(solution)/shard_map/ppermute | solution.py:320
  88.0 29.0 %collective-permute-start.24 = (bf16[256,1792]{1,0:T(8,128)(2,1)}, bf16[256,1792]{1,0:T(8,128)(2,1)}, u32[]{:S(2)}, u32[]{:S(2)}) collective-permute-start(bf16[256,1792]{1,0:T(8,128)(2,1)} %collective-permute-done.22.down2), channel_id=1, source_target_pairs={{4,0},{5,1},{6,2},{7,3},{20,16},{21,17},{22,18},{23,19},{36,32},{3... | collective-permute-start | bytes 2752520 | tf_op jit(solution)/shard_map/ppermute | solution.py:324
  89.3 1.6 copy-start.1
  90.9 2.0 %copy-start.7 = (bf16[1024,1792]{1,0:T(8,128)(2,1)S(1)}, bf16[1024,1792]{1,0:T(8,128)(2,1)}, u32[]{:S(2)}) copy-start(bf16[1024,1792]{1,0:T(8,128)(2,1)} %get-tuple-element.72.hid_ref) | copy-start | bytes 11010052
  101.4 36.7 %collective-permute-start.28 = (bf16[256,1792]{1,0:T(8,128)(2,1)}, bf16[256,1792]{1,0:T(8,128)(2,1)}, u32[]{:S(2)}, u32[]{:S(2)}) collective-permute-start(bf16[256,1792]{1,0:T(8,128)(2,1)} %get-tuple-element.96), channel_id=1, source_target_pairs={{0,4},{4,8},{1,5},{5,9},{2,6},{6,10},{3,7},{7,11},{16,20},{20,24},... | collective-permute-start | bytes 2752520 | tf_op jit(solution)/shard_map/ppermute | solution.py:320
  106.7 31.4 %collective-permute-start.30 = (bf16[256,1792]{1,0:T(8,128)(2,1)}, bf16[256,1792]{1,0:T(8,128)(2,1)}, u32[]{:S(2)}, u32[]{:S(2)}) collective-permute-start(bf16[256,1792]{1,0:T(8,128)(2,1)} %get-tuple-element.95), channel_id=1, source_target_pairs={{12,8},{8,4},{13,9},{9,5},{14,10},{10,6},{15,11},{11,7},{28,24},{2... | collective-permute-start | bytes 2752520 | tf_op jit(solution)/shard_map/ppermute | solution.py:324
  120.5 15.9 %collective-permute-start.25 = (bf16[128,1792]{1,0:T(8,128)(2,1)}, bf16[128,1792]{1,0:T(8,128)(2,1)S(1)}, u32[]{:S(2)}, u32[]{:S(2)}) collective-permute-start(bf16[128,1792]{1,0:T(8,128)(2,1)} %get-tuple-element.76), channel_id=1, source_target_pairs={{0,1},{1,2},{2,3},{3,0},{4,5},{5,6},{6,7},{7,4},{8,9},{9,10},{10,1... | collective-permute-start | bytes 1376264 | tf_op jit(solution)/shard_map/ppermute | solution.py:316
  125.0 13.1 %collective-permute-start.26 = (bf16[128,1792]{1,0:T(8,128)(2,1)}, bf16[128,1792]{1,0:T(8,128)(2,1)}, u32[]{:S(2)}, u32[]{:S(2)}) collective-permute-start(bf16[128,1792]{1,0:T(8,128)(2,1)} %get-tuple-element.77), channel_id=1, source_target_pairs={{0,3},{1,0},{2,1},{3,2},{4,7},{5,4},{6,5},{7,6},{8,11},{9,8},{10,9... | collective-permute-start | bytes 1376264 | tf_op jit(solution)/shard_map/ppermute | solution.py:316
  132.5 16.4 %collective-permute-start.33 = (bf16[128,1792]{1,0:T(8,128)(2,1)}, bf16[128,1792]{1,0:T(8,128)(2,1)S(1)}, u32[]{:S(2)}, u32[]{:S(2)}) collective-permute-start(bf16[128,1792]{1,0:T(8,128)(2,1)} %get-tuple-element.87), channel_id=1, source_target_pairs={{0,1},{1,2},{2,3},{3,0},{4,5},{5,6},{6,7},{7,4},{8,9},{9,10},{10,1... | collective-permute-start | bytes 1376264 | tf_op jit(solution)/shard_map/ppermute | solution.py:316
  136.4 12.5 %collective-permute-start.34 = (bf16[128,1792]{1,0:T(8,128)(2,1)}, bf16[128,1792]{1,0:T(8,128)(2,1)S(1)}, u32[]{:S(2)}, u32[]{:S(2)}) collective-permute-start(bf16[128,1792]{1,0:T(8,128)(2,1)} %get-tuple-element.88), channel_id=1, source_target_pairs={{0,3},{1,0},{2,1},{3,2},{4,7},{5,4},{6,5},{7,6},{8,11},{9,8},{10,9... | collective-permute-start | bytes 1376264 | tf_op jit(solution)/shard_map/ppermute | solution.py:316
  139.6 8.0 %copy-start.12 = (bf16[128,1792]{1,0:T(8,128)(2,1)S(1)}, bf16[128,1792]{1,0:T(8,128)(2,1)}, u32[]{:S(2)}) copy-start(bf16[128,1792]{1,0:T(8,128)(2,1)} %get-tuple-element.83) | copy-start | bytes 1376260
  139.6 8.0 %copy-start.13 = (bf16[128,1792]{1,0:T(8,128)(2,1)S(1)}, bf16[128,1792]{1,0:T(8,128)(2,1)}, u32[]{:S(2)}) copy-start(bf16[128,1792]{1,0:T(8,128)(2,1)} %get-tuple-element.85) | copy-start | bytes 1376260
  139.6 22.7 %collective-permute-start.32 = (bf16[256,1792]{1,0:T(8,128)(2,1)S(1)}, bf16[256,1792]{1,0:T(8,128)(2,1)S(1)}, u32[]{:S(2)}, u32[]{:S(2)}) collective-permute-start(bf16[256,1792]{1,0:T(8,128)(2,1)S(1)} %add_convert_fusion.1), channel_id=1, source_target_pairs={{12,8},{8,4},{4,0},{13,9},{9,5},{5,1},{14,10},{10,6},{6,2},{15,11}... | collective-permute-start | bytes 2752520 | tf_op jit(solution)/shard_map/ppermute | solution.py:324
  142.4 17.7 %copy-start.2 = (bf16[1,256,1792]{2,1,0:T(8,128)(2,1)S(1)}, bf16[1,256,1792]{2,1,0:T(8,128)(2,1)}, u32[]{:S(2)}) copy-start(bf16[1,256,1792]{2,1,0:T(8,128)(2,1)} %param.26) | copy-start | bytes 2752516
  142.5 17.7 %copy-start.3 = (bf16[1,256,1792]{2,1,0:T(8,128)(2,1)S(1)}, bf16[1,256,1792]{2,1,0:T(8,128)(2,1)}, u32[]{:S(2)}) copy-start(bf16[1,256,1792]{2,1,0:T(8,128)(2,1)} %param.27) | copy-start | bytes 2752516
  142.5 17.7 %copy-start.5 = (bf16[256,1792]{1,0:T(8,128)(2,1)S(1)}, bf16[256,1792]{1,0:T(8,128)(2,1)}, u32[]{:S(2)}) copy-start(bf16[256,1792]{1,0:T(8,128)(2,1)} %get-tuple-element.82.own_ref) | copy-start | bytes 2752516
  142.5 19.8 %collective-permute-start.31 = (bf16[256,1792]{1,0:T(8,128)(2,1)S(1)}, bf16[256,1792]{1,0:T(8,128)(2,1)S(1)}, u32[]{:S(2)}, u32[]{:S(2)}) collective-permute-start(bf16[256,1792]{1,0:T(8,128)(2,1)S(1)} %add_convert_fusion.2), channel_id=1, source_target_pairs={{0,4},{4,8},{8,12},{1,5},{5,9},{9,13},{2,6},{6,10},{10,14},{3,7},{... | collective-permute-start | bytes 2752520 | tf_op jit(solution)/shard_map/ppermute | solution.py:320
  148.9 8.6 %collective-permute-start.35 = (bf16[128,1792]{1,0:T(8,128)(2,1)S(1)}, bf16[128,1792]{1,0:T(8,128)(2,1)S(1)}, u32[]{:S(2)}, u32[]{:S(2)}) collective-permute-start(bf16[128,1792]{1,0:T(8,128)(2,1)S(1)} %get-tuple-element.89), channel_id=1, source_target_pairs={{0,1},{1,2},{2,3},{3,0},{4,5},{5,6},{6,7},{7,4},{8,9},{9,10},{10,1... | collective-permute-start | bytes 1376264 | tf_op jit(solution)/shard_map/ppermute | solution.py:316
  150.4 9.7 %collective-permute-start.36 = (bf16[128,1792]{1,0:T(8,128)(2,1)S(1)}, bf16[128,1792]{1,0:T(8,128)(2,1)S(1)}, u32[]{:S(2)}, u32[]{:S(2)}) collective-permute-start(bf16[128,1792]{1,0:T(8,128)(2,1)S(1)} %get-tuple-element.92), channel_id=1, source_target_pairs={{0,3},{1,0},{2,1},{3,2},{4,7},{5,4},{6,5},{7,6},{8,11},{9,8},{10,9... | collective-permute-start | bytes 1376264 | tf_op jit(solution)/shard_map/ppermute | solution.py:316

commit v5 on v4

--- a/solution.py
+++ b/solution.py
@@ -129,155 +129,115 @@
     )(where, chosen, outer, local_rows, gate, up, cot_rows)
 
 
-def some_features(scale, cot_ref, hid_ref, which, out_ref):
-    piece = cot_ref.shape[1] // SIDE
-    features = cot_ref[:, which * piece : (which + 1) * piece]
-    part = lax.dot_general(features, hid_ref[...], (((0,), (0,)), ((), ())), preferred_element_type=jnp.float32)
-    out_ref[...] = (scale * part).astype(jnp.bfloat16)
-
-
-def first_kernel(scale, hidden, own, go_up, go_down, last_up, last_down, cot_out, hid_out, up_out, down_out):
+def weight_kernel(scale, hidden, own, go_up, go_down, last_up, last_down, cot_out, up_out, down_out, mid_out, own_out, hid):
+    step = pl.program_id(0)
     rows, width = hidden.shape
     half, across = rows // 2, own.shape[1]
+    piece = across // SIDE
     near = width + across
     first, second = slice(near + width, near + width + across), slice(near + width + across, near + width + 2 * across)
-    cot_out[:rows] = own[...]
-    hid_out[:rows] = hidden[...]
-    far, other = slice(0, width), slice(near, near + width)
-    for n, (ref, tokens, features) in enumerate(
-        (
-            (go_down, other, first),
-            (go_down, far, second),
-            (last_up, far, slice(width, near)),
-            (last_down, far, slice(width, near)),
-            (go_up, far, first),
-            (go_up, other, second),
-        )
-    ):
-        to = slice(rows + n * half, rows + (n + 1) * half)
-        cot_out[to] = ref[:, features]
-        hid_out[to] = ref[:, tokens]
-    some_features(scale, cot_out, hid_out, 3, up_out)
-    some_features(scale, cot_out, hid_out, 1, down_out)
-
-
-def first_parts(scale, hidden, own, *moved):
+
+    @pl.when(step == 0)
+    def _():
+        cot_out[:rows] = own[...]
+        hid[:rows] = hidden[...]
+        far, other = slice(0, width), slice(near, near + width)
+        for n, (ref, tokens, features) in enumerate(
+            (
+                (go_down, other, first),
+                (go_down, far, second),
+                (last_up, far, slice(width, near)),
+                (last_down, far, slice(width, near)),
+                (go_up, far, first),
+                (go_up, other, second),
+            )
+        ):
+            to = slice(rows + n * half, rows + (n + 1) * half)
+            cot_out[to] = ref[:, features]
+            hid[to] = ref[:, tokens]
+
+    for n, (which, out_ref) in enumerate(((3, up_out), (1, down_out), (2, mid_out), (0, own_out))):
+
+        @pl.when(step == n)
+        def _(which=which, out_ref=out_ref):
+            features = cot_out[:, which * piece : (which + 1) * piece]
+            part = lax.dot_general(features, hid[...], (((0,), (0,)), ((), ())), preferred_element_type=jnp.float32)
+            out_ref[...] = (scale * part).astype(jnp.bfloat16)
+
+
+def weight_parts(scale, hidden, own, *moved):
     rows, width = hidden.shape
     across = own.shape[1]
-    sizes = [(SIDE * rows, across), (SIDE * rows, width), (across // SIDE, width), (across // SIDE, width)]
-    return pl.pallas_call(
-        functools.partial(first_kernel, scale),
+    sizes = [(SIDE * rows, across)] + [(across // SIDE, width)] * SIDE
+    whole = lambda shape: pl.BlockSpec(shape, lambda i: (0, 0))
+    return pl.pallas_call(
+        functools.partial(weight_kernel, scale),
+        grid=(SIDE,),
         out_shape=[jax.ShapeDtypeStruct(size, jnp.bfloat16) for size in sizes],
-        in_specs=[VMEM] * (2 + len(moved)),
-        out_specs=[VMEM] * 4,
+        in_specs=[whole(value.shape) for value in (hidden, own, *moved)],
+        out_specs=[whole(size) for size in sizes],
+        scratch_shapes=[pltpu.VMEM((SIDE * rows, width), jnp.bfloat16)],
         compiler_params=pltpu.CompilerParams(vmem_limit_bytes=48 * 2**20),
         cost_estimate=pl.CostEstimate(flops=2**20, bytes_accessed=2**20, transcendentals=0),
-        name="first_parts",
+        name="weight_parts",
     )(hidden, own, *moved)
 
 
-def other_kernel(scale, cot_ref, hid_ref, mid_out, own_out):
-    some_features(scale, cot_ref, hid_ref, 2, mid_out)
-    some_features(scale, cot_ref, hid_ref, 0, own_out)
-
-
-def other_parts(scale, cot, hid):
-    tokens, width = hid.shape
-    piece = cot.shape[1] // SIDE
-    return pl.pallas_call(
-        functools.partial(other_kernel, scale),
-        out_shape=[jax.ShapeDtypeStruct((piece, width), jnp.bfloat16)] * 2,
-        in_specs=[VMEM] * 2,
-        out_specs=[VMEM] * 2,
-        compiler_params=pltpu.CompilerParams(vmem_limit_bytes=32 * 2**20),
-        cost_estimate=pl.CostEstimate(flops=4 * tokens * piece * width, bytes_accessed=2**20, transcendentals=0),
-        name="other_parts",
-    )(cot, hid)
-
-
-def early_kernel(where_ref, cot_ref, own, down1, up1, up2, down2, total_out):
+def early_sum(z, cot_ref, own, down1, up1, up2, down2):
     piece = own.shape[0]
-    mid = jnp.where(where_ref[0] >= SIDE // 2, up2[...], down2[...])
+    mid = jnp.where(z >= SIDE // 2, up2[...], down2[...])
     total = 0.0
     for k, block in enumerate((own[...], down1[...], mid, up1[...])):
         total = total + jnp.dot(cot_ref[:, k * piece : (k + 1) * piece], block, preferred_element_type=jnp.float32)
-    total_out[...] = total
-
-
-def early_products(where, cot, *blocks):
-    rows, width = blocks[0].shape
-    return pl.pallas_call(
-        early_kernel,
-        grid=(SIDE,),
-        out_shape=jax.ShapeDtypeStruct((SIDE * rows, width), jnp.float32),
-        in_specs=[SMEM, pl.BlockSpec((rows, cot.shape[1]), lambda i: (i, 0))]
-        + [pl.BlockSpec((rows, width), lambda i: (0, 0))] * 5,
-        out_specs=pl.BlockSpec((rows, width), lambda i: (i, 0)),
-        compiler_params=pltpu.CompilerParams(vmem_limit_bytes=ALL_VMEM),
-        cost_estimate=pl.CostEstimate(flops=2**20, bytes_accessed=2**20, transcendentals=0),
-        name="early_products",
-    )(where, cot, *blocks)
-
-
-def with_last(z, total_ref, cot_ref, up3, down3, scale):
+    return total
+
+
+def with_last(z, total, cot_ref, up3, down3, scale):
     piece = up3.shape[0]
     last = jnp.where(z == 0, down3[...], up3[...])
     far = jnp.where(z == 0, cot_ref[:, 3 * piece :], cot_ref[:, piece : 2 * piece])
-    return (scale * (total_ref[...] + jnp.dot(far, last, preferred_element_type=jnp.float32))).astype(jnp.bfloat16)
-
-
-def far_kernel(scale, where_ref, total_ref, cot_ref, up3, down3, top_out, low_out):
+    return (scale * (total + jnp.dot(far, last, preferred_element_type=jnp.float32))).astype(jnp.bfloat16)
+
+
+def early_kernel(where_ref, cot_ref, own, down1, up1, up2, down2, total_out):
+    total_out[...] = early_sum(where_ref[0], cot_ref, own, down1, up1, up2, down2)
+
+
+def far_kernel(scale, where_ref, cot_ref, total_ref, up3, down3, top_out, low_out):
     half = top_out.shape[0]
-    value = with_last(where_ref[0], total_ref, cot_ref, up3, down3, scale)
+    value = with_last(where_ref[0], total_ref[...], cot_ref, up3, down3, scale)
     top_out[...] = value[:half]
     low_out[...] = value[half:]
 
 
-def near_kernel(scale, where_ref, total_ref, cot_ref, up3, down3, own_out, up_add, up_out, down_out, down_add):
-    step = pl.program_id(0)
-    half = up_add.shape[0]
-    value = with_last(where_ref[0], total_ref, cot_ref, up3, down3, scale)
-    targets = ((up_add, up_out), (down_out, down_add), (own_out.at[:half], own_out.at[half:]))
-    for n, (top, low) in enumerate(targets):
-
-        @pl.when(step == n)
-        def _(top=top, low=low):
-            top[...] = value[:half]
-            low[...] = value[half:]
-
-
-def last_products(which, where, total, cot, up3, down3, scale):
-    rows, width = up3.shape
-    half = rows // 2
-    part = lambda n: jax.ShapeDtypeStruct((n, width), jnp.bfloat16)
-    whole = lambda n: pl.BlockSpec((n, width), lambda i: (0, 0))
-    if which == "far":
-        body, outs, steps, chunk = far_kernel, [half, half], 1, lambda i: (2, 0)
-    else:
-        body, outs, steps, chunk = near_kernel, [rows, half, half, half, half], 3, lambda i: ((2 * i + 1) % 5 % 4, 0)
-    return pl.pallas_call(
-        functools.partial(body, scale),
-        grid=(steps,),
-        out_shape=[part(n) for n in outs],
-        in_specs=[
-            SMEM,
-            pl.BlockSpec((rows, width), chunk),
-            pl.BlockSpec((rows, cot.shape[1]), chunk),
-            whole(rows),
-            whole(rows),
-        ],
-        out_specs=[whole(n) for n in outs],
-        compiler_params=pltpu.CompilerParams(vmem_limit_bytes=ALL_VMEM),
-        cost_estimate=pl.CostEstimate(
-            flops=4 * steps * rows * rows * width, bytes_accessed=(6 * steps + 4) * rows * width, transcendentals=0
-        ),
-        name=which + "_rows",
-    )(where, total, cot, up3, down3)
-
-
-def finish_kernel(gate_ref, up_ref, own_ref, top_up, low_up, top_down, low_down, gate_out, up_out):
-    def write(first, second):
-        grad = own_ref[...].astype(jnp.float32) + first[...].astype(jnp.float32) + second[...].astype(jnp.float32)
+def near_kernel(scale, where_ref, cot_ref, own, down1, up1, up2, down2, up3, down3, *outs):
+    z = where_ref[0]
+    value = with_last(z, early_sum(z, cot_ref, own, down1, up1, up2, down2), cot_ref, up3, down3, scale)
+    for n, out_ref in enumerate(outs):
+
+        @pl.when(pl.program_id(0) == n)
+        def _(out_ref=out_ref):
+            out_ref[...] = value
+
+
+def rows_kernel(body, chunk, chunks, outs, kind, limit, cost, name, where, cot, *blocks):
+    width = blocks[0].shape[1]
+    whole = lambda shape: pl.BlockSpec(shape, lambda i: (0, 0))
+    return pl.pallas_call(
+        body,
+        grid=(chunks,),
+        out_shape=[jax.ShapeDtypeStruct((n, width), kind) for n in outs],
+        in_specs=[SMEM, pl.BlockSpec(*chunk)] + [whole(block.shape) for block in blocks],
+        out_specs=[whole((n, width)) for n in outs],
+        compiler_params=pltpu.CompilerParams(vmem_limit_bytes=limit * 2**20),
+        cost_estimate=pl.CostEstimate(flops=cost, bytes_accessed=2**20, transcendentals=0),
+        name=name,
+    )(where, cot, *blocks)
+
+
+def finish_kernel(gate_ref, up_ref, own_top, own_low, top_up, low_up, top_down, low_down, gate_out, up_out):
+    def write(own, first, second):
+        grad = own[...].astype(jnp.float32) + first[...].astype(jnp.float32) + second[...].astype(jnp.float32)
         gate = gate_ref[...].astype(jnp.float32)
         sig = jax.nn.sigmoid(gate)
         gate_out[...] = (grad * up_ref[...].astype(jnp.float32) * sig * (1.0 + gate * (1.0 - sig))).astype(jnp.bfloat16)
@@ -285,14 +245,14 @@
 
     @pl.when(pl.program_id(0) == 0)
     def _():
-        write(top_up, top_down)
+        write(own_top, top_up, top_down)
 
     @pl.when(pl.program_id(0) == 1)
     def _():
-        write(low_up, low_down)
-
-
-def finish(gate, up, own, top_up, low_up, top_down, low_down):
+        write(own_low, low_up, low_down)
+
+
+def finish(gate, up, *terms):
     rows, width = gate.shape
     block = pl.BlockSpec((rows // 2, width), lambda i: (i, 0))
     whole = pl.BlockSpec((rows // 2, width), lambda i: (0, 0))
@@ -300,12 +260,12 @@
         finish_kernel,
         grid=(2,),
         out_shape=[jax.ShapeDtypeStruct((rows, width), jnp.bfloat16)] * 2,
-        in_specs=[block, block, block, whole, whole, whole, whole],
+        in_specs=[block, block] + [whole] * 6,
         out_specs=[block, block],
         compiler_params=pltpu.CompilerParams(vmem_limit_bytes=16 * 2**20),
         cost_estimate=pl.CostEstimate(flops=10 * rows * width, bytes_accessed=14 * rows * width, transcendentals=rows * width),
         name="finish",
-    )(gate, up, own, top_up, low_up, top_down, low_down)
+    )(gate, up, *terms)
 
 
 def tie(*values):
@@ -352,18 +312,32 @@
     last_up, last_down = turn(go_up[:, :far], 1), turn(go_down[:, :far], -1)
 
     up2, down2 = up_line(up1, (1, 3)), down_line(down1, (1, 3))
-    cot, hid, part_up, part_down = first_parts(scale, hidden, cot_own, go_up, go_down, last_up, last_down)
+    cot, part_up, part_down, part_mid, part_own = weight_parts(scale, hidden, cot_own, go_up, go_down, last_up, last_down)
     sum_up, sum_down = up_line(part_up, (0, 1)), down_line(part_down, (0, 1))
     up3, down3 = up_line(up2, (2, 3)), down_line(down2, (2, 3))
-    total = early_products(where, cot, theta_new, down1, up1, up2, down2)
-    part_mid, part_own = other_parts(scale, cot, hid)
+    half, depth = rows // 2, cot.shape[1]
+    early = (theta_new, down1, up1, up2, down2)
+    across_x = ((rows, depth), lambda i: (2, 0))
+    (total,) = rows_kernel(early_kernel, across_x, 1, [rows], jnp.float32, 32, 2**20, "early_rows", where, cot, *early)
     sum_up, sum_down = add(part_mid, sum_up), add(part_mid, sum_down)
     sum_up, sum_down = up_line(sum_up, (0, 2)), down_line(sum_down, (0, 2))
 
-    far_top, far_low = last_products("far", where, total, cot, up3, down3, scale)
+    far_top, far_low = rows_kernel(
+        functools.partial(far_kernel, scale), across_x, 1, [half, half], jnp.bfloat16, 24, 2**20, "far_rows",
+        where, cot, total, up3, down3,
+    )
     far_top, far_low = turn(far_top, 1), turn(far_low, -1)
-    own, up_add, up_near, down_near, down_add = last_products("near", where, total, cot, up3, down3, scale)
+    near = functools.partial(near_kernel, scale)
+    cost = 2 * half * depth * width
+    up_near, down_near = rows_kernel(
+        near, ((half, depth), lambda i: (3 * (i + 1), 0)), 2, [half, half], jnp.bfloat16, 32, 2 * cost, "near_rows",
+        where, cot, *early, up3, down3,
+    )
     low_up, top_down = turn(up_near, 1), turn(down_near, -1)
+    up_add, down_add, own_top, own_low = rows_kernel(
+        near, ((half, depth), lambda i: (jnp.where(i < 2, 2 + 5 * i, i - 2), 0)), 4, [half] * 4, jnp.bfloat16, 32, 4 * cost,
+        "other_rows", where, cot, *early, up3, down3,
+    )
     far_top, far_low, sum_up, sum_down = tie(far_top, far_low, sum_up, sum_down)
     sum_up, sum_down = add(part_down, sum_up), add(part_up, sum_down)
     sum_up, sum_down = up_line(sum_up, (0, 3)), down_line(sum_down, (0, 3))
@@ -372,7 +346,7 @@
 
     top_up, low_down = turn(up_add, 1), turn(down_add, -1)
     grad_weight = part_own.astype(jnp.float32) + sum_up.astype(jnp.float32) + sum_down.astype(jnp.float32)
-    grad_gate, grad_up = finish(gate, upper, own, top_up, low_up, top_down, low_down)
+    grad_gate, grad_up = finish(gate, upper, own_top, own_low, top_up, low_up, top_down, low_down)
     return momentum_new[None], grad_weight.astype(jnp.bfloat16)[None], grad_gate[None], grad_up[None]
 
 

time: 166 us -> 157 us (0.946)
  waiting for transfers between devices: 47 us -> 71.6 us
  starting transfers between devices: 62.7 us -> 48.7 us
  Pallas kernels: 39 us -> 29 us
  other arithmetic: 7.7 us -> 2.83 us
  local copies, waits for them, and re-layouts: 5.55 us -> 0.72 us
    ppermute x6, waiting for transfers between devices: 7.2 us -> 22.2 us  [down_line(): lax.ppermute(value, 'z', [(SIDE - 1 - i, SIDE - 2 - i) for i in range(*st...]
    ppermute x6, starting transfers between devices: 30.9 us -> 16.9 us  [up_line(): return lax.ppermute(value, 'z', [(i, i + 1) for i in range(*step)])]
    pallas_call x5, Pallas kernels: 27.5 us -> 17.5 us  [the longest x4 8.85 us: rows_kernel(): pl.pallas_call(body, grid=(chunks,), out_shape=[jax.ShapeDtypeStruct((n,...]
    ppermute x1, waiting for transfers between devices: 10.7 us -> 20.4 us  [to_partner(): lax.ppermute(value, 'rep', [(i, i ^ by) for i in range(replicas)])]
    unnamed x28 -> x18, local copies, waits for them, and re-layouts: 4.88 us -> 0.04 us
    ppermute x10, waiting for transfers between devices: 16.8 us -> 12 us  [turn(): return lax.ppermute(value, 'x', [(i, (i + by) % SIDE) for i in range(SIDE)])]
    convert_element_type x4, other arithmetic: 5.72 us -> 1.02 us  [add(): return (a.astype(jnp.float32) + b.astype(jnp.float32)).astype(jnp.bfloat16)]
    ppermute x6, waiting for transfers between devices: 12.3 us -> 17 us  [up_line(): return lax.ppermute(value, 'z', [(i, i + 1) for i in range(*step)])]
  transfers between devices with their start and end apart: 23 -> 23, of which waited for: 10 -> 11; matrix products, arithmetic and copies ran while one was open for 4% -> 1% of each run, Pallas kernels for 20% -> 15%
where the time goes in v5:
time: 157 us; the launch traced here: 155 us
  waiting for transfers between devices  71.6 us (46%)
  starting transfers between devices  48.7 us (31%)
  Pallas kernels  29 us (18%)
  other arithmetic  2.83 us (2%)
  between operations  1.59 us (1%)
    ppermute x6, waiting for transfers between devices, down_line(): lax.ppermute(value, 'z', [(SIDE - 1 - i, SIDE - 2 - i) for i in range(*st...  22.2 us
    ppermute x1, waiting for transfers between devices, to_partner(): lax.ppermute(value, 'rep', [(i, i ^ by) for i in range(replicas)])  20.4 us
    ppermute x10, starting transfers between devices, turn(): return lax.ppermute(value, 'x', [(i, (i + by) % SIDE) for i in range(SIDE)])  17.2 us
    ppermute x6, waiting for transfers between devices, up_line(): return lax.ppermute(value, 'z', [(i, i + 1) for i in range(*step)])  17 us
    ppermute x6, starting transfers between devices, up_line(): return lax.ppermute(value, 'z', [(i, i + 1) for i in range(*step)])  16.9 us
    ppermute x10, waiting for transfers between devices, turn(): return lax.ppermute(value, 'x', [(i, (i + by) % SIDE) for i in range(SIDE)])  12 us
    pallas_call x4, Pallas kernels, rows_kernel(): pl.pallas_call(body, grid=(chunks,), out_shape=[jax.ShapeDtypeStruct((n,...  8.85 us
    pallas_call x1, Pallas kernels, weight_parts(): pl.pallas_call(functools.partial(weight_kernel, scale), grid=(SIDE,), out...  8.61 us
  transfers between devices with their start and end apart: 23, of which 11 were waited for; matrix products, arithmetic and copies ran while one was open for 1% of the time, Pallas kernels for 15%

profile of v5, /device:TPU:6, one launch (start us, length us, event | category | flops | bytes accessed | tf_op | source)
XLA Modules:
  0.0 154.5 jit_solution(9672028896896731746)
XLA Ops:
  0.6 0.0 copy-start
  0.7 0.6 pad_add_fusion.where_ref
  1.2 5.6 %prepare.1 = (bf16[14,128,128]{2,1,0:T(8,128)(2,1)}, bf16[256,1792]{1,0:T(8,128)(2,1)}, bf16[256,1024]{1,0:T(8,128)(2,1)}, bf16[128,6656]{1,0:T(8,128)(2,1)}, bf16[128,6656]{1,0:T(8,128)(2,1)}) custom-call(s32[2]{0:T(128)} %pad_add_fusion.where_ref, s32[1,14]{1,0:T(1,128)} %chosen_ref.3, bf16[256,1792]{1,0:T(8,128)(2,1)} %bitcast.18, ...), custom_call_target="tpu_custom_call" | custom-call | flops 1835008 | bytes 11534336 | tf_op jit(solution)/shard_map/prepare/pallas_call | solution.py:120
  6.8 2.3 %collective-permute-start.15 = (bf16[128,6656]{1,0:T(8,128)(2,1)}, bf16[128,6656]{1,0:T(8,128)(2,1)S(1)}, u32[]{:S(2)}, u32[]{:S(2)}) collective-permute-start(bf16[128,6656]{1,0:T(8,128)(2,1)} %get-tuple-element.69), channel_id=1, source_target_pairs={{0,1},{1,2},{2,3},{3,0},{4,5},{5,6},{6,7},{7,4},{8,9},{9,10},{10,1... | collective-permute-start | bytes 5111816 | tf_op jit(solution)/shard_map/ppermute | solution.py:276
  9.1 0.0 collective-permute-start.16
  9.1 0.6 constant_dynamic-slice_fusion
  10.4 28.5 %conditional.1 = (bf16[14,128,128]{2,1,0:T(8,128)(2,1)}) conditional(s32[]{:T(128)} %clamp.3, bf16[14,128,128]{2,1,0:T(8,128)(2,1)} %get-tuple-element.65, bf16[14,128,128]{2,1,0:T(8,128)(2,1)} %get-tuple-element.65, bf16[14,128,128]{2,1,0:T(8,128)(2,1)} %get-tuple-element.65, ...), branch_computations={%region_0.0_spmd, %region_1.0_spmd, %region_2.0_spmd, %region_3.0_... | conditional | bytes 1835056 | solution.py:308
  10.4 8.1 %collective-permute-start.5 = (bf16[14,128,128]{2,1,0:T(8,128)(2,1)}, bf16[14,128,128]{2,1,0:T(8,128)(2,1)}, u32[]{:S(2)}, u32[]{:S(2)}) collective-permute-start(bf16[14,128,128]{2,1,0:T(8,128)(2,1)} %param.5), channel_id=1, source_target_pairs={{0,96},{16,112},{32,64},{48,80},{64,32},{80,48},{96,0},{112,16},{1... | collective-permute-start | bytes 1376264 | tf_op jit(solution)/shard_map/cond/branch_5_fun/ppermute | solution.py:301
  18.5 20.4 %collective-permute-done.5 = bf16[14,128,128]{2,1,0:T(8,128)(2,1)} collective-permute-done((bf16[14,128,128]{2,1,0:T(8,128)(2,1)}, bf16[14,128,128]{2,1,0:T(8,128)(2,1)}, u32[]{:S(2)}, u32[]{:S(2)}) %collective-permute-start.5) | collective-permute-done | bytes 458784 | tf_op jit(solution)/shard_map/cond/branch_5_fun/ppermute | solution.py:301
  38.9 3.8 %outer_step.1 = (f32[256,1792]{1,0:T(8,128)}, bf16[256,1792]{1,0:T(8,128)(2,1)}) custom-call(s32[1,14]{1,0:T(1,128)} %chosen_ref.3, bf16[256,1792]{1,0:T(8,128)(2,1)} %bitcast.19, bf16[256,1792]{1,0:T(8,128)(2,1)} %bitcast.21, f32[256,1792]{1,0:T(8,128)} %bitcast.23, bf16[14,128,128]{2,1,0:T(8,128)(2,1)} %get-tuple-element.99.moved_ref), custom_call_target="tpu_custom_call" | custom-call | flops 3670016 | bytes 6422528 | tf_op jit(solution)/shard_map/outer_step/pallas_call | solution.py:47
  42.7 1.5 collective-permute-start.20
  44.2 1.3 collective-permute-start.19
  45.5 0.6 collective-permute-done.15.go_up
  46.1 3.5 %collective-permute-start.17 = (bf16[128,2816]{1,0:T(8,128)(2,1)S(1)}, bf16[128,2816]{1,0:T(8,128)(2,1)S(1)}, u32[]{:S(2)}, u32[]{:S(2)}) collective-permute-start(bf16[128,2816]{1,0:T(8,128)(2,1)S(1)} %slice.8), channel_id=1, source_target_pairs={{0,1},{1,2},{2,3},{3,0},{4,5},{5,6},{6,7},{7,4},{8,9},{9,10},{10,1... | collective-permute-start | bytes 2162696 | tf_op jit(solution)/shard_map/ppermute | solution.py:276
  49.6 0.0 collective-permute-done.16.go_down
  49.7 0.1 collective-permute-start.18
  49.8 7.7 %collective-permute-done.20.up1 = bf16[256,1792]{1,0:T(8,128)(2,1)S(1)} collective-permute-done((bf16[256,1792]{1,0:T(8,128)(2,1)}, bf16[256,1792]{1,0:T(8,128)(2,1)S(1)}, u32[]{:S(2)}, u32[]{:S(2)}) %collective-permute-start.20) | collective-permute-done | bytes 917536 | tf_op jit(solution)/shard_map/ppermute | solution.py:280
  57.5 0.7 collective-permute-start.21
  58.2 10.7 %collective-permute-done.19.down1 = bf16[256,1792]{1,0:T(8,128)(2,1)S(1)} collective-permute-done((bf16[256,1792]{1,0:T(8,128)(2,1)}, bf16[256,1792]{1,0:T(8,128)(2,1)S(1)}, u32[]{:S(2)}, u32[]{:S(2)}) %collective-permute-start.19) | collective-permute-done | bytes 917536 | tf_op jit(solution)/shard_map/ppermute | solution.py:284
  68.9 1.3 collective-permute-start.22
  70.2 0.0 collective-permute-done.17.last_up
  70.2 0.0 collective-permute-done.18.last_down
  70.2 8.6 %weight_parts.1 = (bf16[1024,1024]{1,0:T(8,128)(2,1)}, bf16[256,1792]{1,0:T(8,128)(2,1)S(1)}, bf16[256,1792]{1,0:T(8,128)(2,1)S(1)}, bf16[256,1792]{1,0:T(8,128)(2,1)S(1)}, bf16[256,1792]{1,0:T(8,128)(2,1)S(1)}) custom-call(bf16[256,1792]{1,0:T(8,128)(2,1)} %get-tuple-element.67.hidden, bf16[256,1024]{1,0:T(8,128)(2,1)S(1)} %copy-done.5, ...), custom_call_target="tpu_custom_call" | custom-call | flops 1048576 | bytes 1048576 | tf_op jit(solution)/shard_map/weight_parts/pallas_call | solution.py:173
  78.8 0.7 collective-permute-start.29
  79.5 4.7 %collective-permute-start.27 = (bf16[256,1792]{1,0:T(8,128)(2,1)S(1)}, bf16[256,1792]{1,0:T(8,128)(2,1)S(1)}, u32[]{:S(2)}, u32[]{:S(2)}) collective-permute-start(bf16[256,1792]{1,0:T(8,128)(2,1)S(1)} %get-tuple-element.78), channel_id=1, source_target_pairs={{0,4},{1,5},{2,6},{3,7},{16,20},{17,21},{18,22},{19,23},{32,36},{3... | collective-permute-start | bytes 2752520 | tf_op jit(solution)/shard_map/ppermute | solution.py:280
  84.2 0.0 collective-permute-done.21.up2
  84.2 0.7 collective-permute-start.23
  84.9 7.2 %collective-permute-done.22.down2 = bf16[256,1792]{1,0:T(8,128)(2,1)S(1)} collective-permute-done((bf16[256,1792]{1,0:T(8,128)(2,1)S(1)}, bf16[256,1792]{1,0:T(8,128)(2,1)S(1)}, u32[]{:S(2)}, u32[]{:S(2)}) %collective-permute-start.22) | collective-permute-done | bytes 917536 | tf_op jit(solution)/shard_map/ppermute | solution.py:284
  92.2 1.3 collective-permute-start.24
  93.5 9.3 %collective-permute-done.27 = bf16[256,1792]{1,0:T(8,128)(2,1)S(1)} collective-permute-done((bf16[256,1792]{1,0:T(8,128)(2,1)S(1)}, bf16[256,1792]{1,0:T(8,128)(2,1)S(1)}, u32[]{:S(2)}, u32[]{:S(2)}) %collective-permute-start.27) | collective-permute-done | bytes 917536 | tf_op jit(solution)/shard_map/ppermute | solution.py:280
  102.7 0.4 fusion.1
  103.1 4.6 %collective-permute-start.28 = (bf16[256,1792]{1,0:T(8,128)(2,1)S(1)}, bf16[256,1792]{1,0:T(8,128)(2,1)S(1)}, u32[]{:S(2)}, u32[]{:S(2)}) collective-permute-start(bf16[256,1792]{1,0:T(8,128)(2,1)S(1)} %get-tuple-element.96), channel_id=1, source_target_pairs={{0,4},{4,8},{1,5},{5,9},{2,6},{6,10},{3,7},{7,11},{16,20},{20,24},... | collective-permute-start | bytes 2752520 | tf_op jit(solution)/shard_map/ppermute | solution.py:280
  107.7 0.7 collective-permute-start.30
  108.4 1.7 %early_rows.1.total_ref = f32[256,1792]{1,0:T(8,128)S(1)} custom-call(s32[2]{0:T(128)S(1)} %copy-done.6, bf16[1024,1024]{1,0:T(8,128)(2,1)S(1)} %copy-done.1, bf16[256,1792]{1,0:T(8,128)(2,1)S(1)} %copy-done.2, bf16[256,1792]{1,0:T(8,128)(2,1)S(1)} %collective-permute-done.19.down1, bf16[256,1792]{1,0:T(8,128)(2,1)S(1)} %collective-permute-done.20.up1, ...), custom_call_target="tpu_custom_call" | custom-call | flops 1048576 | bytes 1048576 | tf_op jit(solution)/shard_map/early_rows/pallas_call | solution.py:226
  110.1 0.0 collective-permute-done.23.up3
  110.1 4.3 %collective-permute-done.24.down3 = bf16[256,1792]{1,0:T(8,128)(2,1)S(1)} collective-permute-done((bf16[256,1792]{1,0:T(8,128)(2,1)S(1)}, bf16[256,1792]{1,0:T(8,128)(2,1)S(1)}, u32[]{:S(2)}, u32[]{:S(2)}) %collective-permute-start.24) | collective-permute-done | bytes 917536 | tf_op jit(solution)/shard_map/ppermute | solution.py:284
  114.5 1.0 far_rows.1
  115.4 1.5 collective-permute-start.25
  116.9 0.6 collective-permute-start.26
  117.5 2.2 %near_rows.1 = (bf16[128,1792]{1,0:T(8,128)(2,1)S(1)}, bf16[128,1792]{1,0:T(8,128)(2,1)S(1)}) custom-call(s32[2]{0:T(128)S(1)} %copy-done.6, bf16[1024,1024]{1,0:T(8,128)(2,1)S(1)} %copy-done.1, bf16[256,1792]{1,0:T(8,128)(2,1)S(1)} %copy-done.2, bf16[256,1792]{1,0:T(8,128)(2,1)S(1)} %collective-permute-done.19.down1, ...), custom_call_target="tpu_custom_call" | custom-call | flops 939524096 | bytes 1048576 | tf_op jit(solution)/shard_map/near_rows/pallas_call | solution.py:226
  119.8 3.8 %collective-permute-start.33 = (bf16[128,1792]{1,0:T(8,128)(2,1)S(1)}, bf16[128,1792]{1,0:T(8,128)(2,1)S(1)}, u32[]{:S(2)}, u32[]{:S(2)}) collective-permute-start(bf16[128,1792]{1,0:T(8,128)(2,1)S(1)} %get-tuple-element.87), channel_id=1, source_target_pairs={{0,1},{1,2},{2,3},{3,0},{4,5},{5,6},{6,7},{7,4},{8,9},{9,10},{10,1... | collective-permute-start | bytes 1376264 | tf_op jit(solution)/shard_map/ppermute | solution.py:276
  123.6 4.0 %other_rows.1 = (bf16[128,1792]{1,0:T(8,128)(2,1)S(1)}, bf16[128,1792]{1,0:T(8,128)(2,1)S(1)}, bf16[128,1792]{1,0:T(8,128)(2,1)S(1)}, bf16[128,1792]{1,0:T(8,128)(2,1)S(1)}) custom-call(s32[2]{0:T(128)S(1)} %copy-done.6, bf16[1024,1024]{1,0:T(8,128)(2,1)S(1)} %copy-done.1, bf16[256,1792]{1,0:T(8,128)(2,1)S(1)} %copy-done.2, ...), custom_call_target="tpu_custom_call" | custom-call | flops 1879048192 | bytes 1048576 | tf_op jit(solution)/shard_map/other_rows/pallas_call | solution.py:226
  127.6 1.2 collective-permute-done.25
  128.8 3.1 %collective-permute-start.34 = (bf16[128,1792]{1,0:T(8,128)(2,1)S(1)}, bf16[128,1792]{1,0:T(8,128)(2,1)S(1)}, u32[]{:S(2)}, u32[]{:S(2)}) collective-permute-start(bf16[128,1792]{1,0:T(8,128)(2,1)S(1)} %get-tuple-element.88), channel_id=1, source_target_pairs={{0,3},{1,0},{2,1},{3,2},{4,7},{5,4},{6,5},{7,6},{8,11},{9,8},{10,9... | collective-permute-start | bytes 1376264 | tf_op jit(solution)/shard_map/ppermute | solution.py:276
  131.9 0.0 collective-permute-done.26
  131.9 0.0 collective-permute-done.28
  131.9 0.0 collective-permute-done.30
  131.9 0.2 add_convert_fusion.1
  132.1 1.3 collective-permute-start.32
  133.4 0.2 add_convert_fusion.2
  133.6 0.0 copy-start.3
  133.6 0.0 copy-start.4
  133.7 4.7 %collective-permute-start.31 = (bf16[256,1792]{1,0:T(8,128)(2,1)S(1)}, bf16[256,1792]{1,0:T(8,128)(2,1)S(1)}, u32[]{:S(2)}, u32[]{:S(2)}) collective-permute-start(bf16[256,1792]{1,0:T(8,128)(2,1)S(1)} %add_convert_fusion.2), channel_id=1, source_target_pairs={{0,4},{4,8},{8,12},{1,5},{5,9},{9,13},{2,6},{6,10},{10,14},{3,7},{... | collective-permute-start | bytes 2752520 | tf_op jit(solution)/shard_map/ppermute | solution.py:280
  138.4 0.2 add_convert_fusion.3
  138.6 0.0 collective-permute-done.33.low_up
  138.6 0.6 collective-permute-done.34.top_down
  139.3 2.0 %collective-permute-start.35 = (bf16[128,1792]{1,0:T(8,128)(2,1)S(1)}, bf16[128,1792]{1,0:T(8,128)(2,1)S(1)}, u32[]{:S(2)}, u32[]{:S(2)}) collective-permute-start(bf16[128,1792]{1,0:T(8,128)(2,1)S(1)} %get-tuple-element.89), channel_id=1, source_target_pairs={{0,1},{1,2},{2,3},{3,0},{4,5},{5,6},{6,7},{7,4},{8,9},{9,10},{10,1... | collective-permute-start | bytes 1376264 | tf_op jit(solution)/shard_map/ppermute | solution.py:276
  141.3 0.3 collective-permute-start.36
  141.6 6.5 %collective-permute-done.35.top_up = bf16[128,1792]{1,0:T(8,128)(2,1)S(1)} collective-permute-done((bf16[128,1792]{1,0:T(8,128)(2,1)S(1)}, bf16[128,1792]{1,0:T(8,128)(2,1)S(1)}, u32[]{:S(2)}, u32[]{:S(2)}) %collective-permute-start.35) | collective-permute-done | bytes 458784 | tf_op jit(solution)/shard_map/ppermute | solution.py:276
  148.0 3.1 %collective-permute-done.36.low_down = bf16[128,1792]{1,0:T(8,128)(2,1)S(1)} collective-permute-done((bf16[128,1792]{1,0:T(8,128)(2,1)S(1)}, bf16[128,1792]{1,0:T(8,128)(2,1)S(1)}, u32[]{:S(2)}, u32[]{:S(2)}) %collective-permute-start.36) | collective-permute-done | bytes 458784 | tf_op jit(solution)/shard_map/ppermute | solution.py:276
  151.1 2.1 %finish.1 = (bf16[256,1792]{1,0:T(8,128)(2,1)}, bf16[256,1792]{1,0:T(8,128)(2,1)}) custom-call(bf16[256,1792]{1,0:T(8,128)(2,1)S(1)} %bitcast.15, bf16[256,1792]{1,0:T(8,128)(2,1)S(1)} %bitcast.17, bf16[128,1792]{1,0:T(8,128)(2,1)S(1)} %get-tuple-element.81.own_top, bf16[128,1792]{1,0:T(8,128)(2,1)S(1)} %get-tuple-element.82.own_low, ...), custom_call_target="tpu_custom_call" | custom-call | flops 4587520 | bytes 6422528 | tf_op jit(solution)/shard_map/finish/pallas_call | solution.py:259
  153.2 0.0 collective-permute-done.32
  153.3 0.0 collective-permute-done.31
  153.3 1.3 fusion.2
  (18 shorter events, 0.1 us)
Async XLA Ops:
  0.6 8.5 %copy-start = (s32[1,16]{1,0:T(1,128)S(1)}, s32[1,16]{1,0:T(1,128)}, u32[]{:S(2)}) copy-start(s32[1,16]{1,0:T(1,128)} %param.29) | copy-start | bytes 196
  6.8 39.2 %collective-permute-start.15 = (bf16[128,6656]{1,0:T(8,128)(2,1)}, bf16[128,6656]{1,0:T(8,128)(2,1)S(1)}, u32[]{:S(2)}, u32[]{:S(2)}) collective-permute-start(bf16[128,6656]{1,0:T(8,128)(2,1)} %get-tuple-element.69), channel_id=1, source_target_pairs={{0,1},{1,2},{2,3},{3,0},{4,5},{5,6},{6,7},{7,4},{8,9},{9,10},{10,1... | collective-permute-start | bytes 5111816 | tf_op jit(solution)/shard_map/ppermute | solution.py:276
  9.1 40.5 %collective-permute-start.16 = (bf16[128,6656]{1,0:T(8,128)(2,1)}, bf16[128,6656]{1,0:T(8,128)(2,1)S(1)}, u32[]{:S(2)}, u32[]{:S(2)}) collective-permute-start(bf16[128,6656]{1,0:T(8,128)(2,1)} %get-tuple-element.70), channel_id=1, source_target_pairs={{0,3},{1,0},{2,1},{3,2},{4,7},{5,4},{6,5},{7,6},{8,11},{9,8},{10,9... | collective-permute-start | bytes 5111816 | tf_op jit(solution)/shard_map/ppermute | solution.py:276
  10.4 28.5 %collective-permute-start.5 = (bf16[14,128,128]{2,1,0:T(8,128)(2,1)}, bf16[14,128,128]{2,1,0:T(8,128)(2,1)}, u32[]{:S(2)}, u32[]{:S(2)}) collective-permute-start(bf16[14,128,128]{2,1,0:T(8,128)(2,1)} %param.5), channel_id=1, source_target_pairs={{0,96},{16,112},{32,64},{48,80},{64,32},{80,48},{96,0},{112,16},{1... | collective-permute-start | bytes 1376264 | tf_op jit(solution)/shard_map/cond/branch_5_fun/ppermute | solution.py:301
  42.7 27.5 %copy-start.5 = (bf16[256,1024]{1,0:T(8,128)(2,1)S(1)}, bf16[256,1024]{1,0:T(8,128)(2,1)}, u32[]{:S(2)}) copy-start(bf16[256,1024]{1,0:T(8,128)(2,1)} %get-tuple-element.68.own) | copy-start | bytes 1572868
  42.7 14.8 %collective-permute-start.20 = (bf16[256,1792]{1,0:T(8,128)(2,1)}, bf16[256,1792]{1,0:T(8,128)(2,1)S(1)}, u32[]{:S(2)}, u32[]{:S(2)}) collective-permute-start(bf16[256,1792]{1,0:T(8,128)(2,1)} %get-tuple-element.74.own), channel_id=1, source_target_pairs={{0,4},{4,8},{8,12},{1,5},{5,9},{9,13},{2,6},{6,10},{10,14},{3,7},{... | collective-permute-start | bytes 2752520 | tf_op jit(solution)/shard_map/ppermute | solution.py:280
  44.2 24.7 %collective-permute-start.19 = (bf16[256,1792]{1,0:T(8,128)(2,1)}, bf16[256,1792]{1,0:T(8,128)(2,1)S(1)}, u32[]{:S(2)}, u32[]{:S(2)}) collective-permute-start(bf16[256,1792]{1,0:T(8,128)(2,1)} %get-tuple-element.74.own), channel_id=1, source_target_pairs={{12,8},{8,4},{4,0},{13,9},{9,5},{5,1},{14,10},{10,6},{6,2},{15,11}... | collective-permute-start | bytes 2752520 | tf_op jit(solution)/shard_map/ppermute | solution.py:284
  46.1 24.1 %copy-start.7 = (bf16[128,6656]{1,0:T(8,128)(2,1)}, bf16[128,6656]{1,0:T(8,128)(2,1)S(1)}, u32[]{:S(2)}) copy-start(bf16[128,6656]{1,0:T(8,128)(2,1)S(1)} %collective-permute-done.15.go_up) | copy-start | bytes 5111812
  46.1 24.0 %collective-permute-start.17 = (bf16[128,2816]{1,0:T(8,128)(2,1)S(1)}, bf16[128,2816]{1,0:T(8,128)(2,1)S(1)}, u32[]{:S(2)}, u32[]{:S(2)}) collective-permute-start(bf16[128,2816]{1,0:T(8,128)(2,1)S(1)} %slice.8), channel_id=1, source_target_pairs={{0,1},{1,2},{2,3},{3,0},{4,5},{5,6},{6,7},{7,4},{8,9},{9,10},{10,1... | collective-permute-start | bytes 2162696 | tf_op jit(solution)/shard_map/ppermute | solution.py:276
  49.6 20.5 %copy-start.8 = (bf16[128,6656]{1,0:T(8,128)(2,1)}, bf16[128,6656]{1,0:T(8,128)(2,1)S(1)}, u32[]{:S(2)}) copy-start(bf16[128,6656]{1,0:T(8,128)(2,1)S(1)} %collective-permute-done.16.go_down) | copy-start | bytes 5111812
  49.7 20.5 %collective-permute-start.18 = (bf16[128,2816]{1,0:T(8,128)(2,1)S(1)}, bf16[128,2816]{1,0:T(8,128)(2,1)S(1)}, u32[]{:S(2)}, u32[]{:S(2)}) collective-permute-start(bf16[128,2816]{1,0:T(8,128)(2,1)S(1)} %slice.9), channel_id=1, source_target_pairs={{0,3},{1,0},{2,1},{3,2},{4,7},{5,4},{6,5},{7,6},{8,11},{9,8},{10,9... | collective-permute-start | bytes 2162696 | tf_op jit(solution)/shard_map/ppermute | solution.py:276
  57.5 26.7 %collective-permute-start.21 = (bf16[256,1792]{1,0:T(8,128)(2,1)S(1)}, bf16[256,1792]{1,0:T(8,128)(2,1)S(1)}, u32[]{:S(2)}, u32[]{:S(2)}) collective-permute-start(bf16[256,1792]{1,0:T(8,128)(2,1)S(1)} %collective-permute-done.20.up1), channel_id=1, source_target_pairs={{4,8},{8,12},{5,9},{9,13},{6,10},{10,14},{7,11},{11,15},{20,24},{2... | collective-permute-start | bytes 2752520 | tf_op jit(solution)/shard_map/ppermute | solution.py:280
  68.9 23.3 %collective-permute-start.22 = (bf16[256,1792]{1,0:T(8,128)(2,1)S(1)}, bf16[256,1792]{1,0:T(8,128)(2,1)S(1)}, u32[]{:S(2)}, u32[]{:S(2)}) collective-permute-start(bf16[256,1792]{1,0:T(8,128)(2,1)S(1)} %collective-permute-done.19.down1), channel_id=1, source_target_pairs={{8,4},{4,0},{9,5},{5,1},{10,6},{6,2},{11,7},{7,3},{24,20},{20,16},... | collective-permute-start | bytes 2752520 | tf_op jit(solution)/shard_map/ppermute | solution.py:284
  78.8 14.6 %collective-permute-start.29 = (bf16[256,1792]{1,0:T(8,128)(2,1)S(1)}, bf16[256,1792]{1,0:T(8,128)(2,1)S(1)}, u32[]{:S(2)}, u32[]{:S(2)}) collective-permute-start(bf16[256,1792]{1,0:T(8,128)(2,1)S(1)} %get-tuple-element.72), channel_id=1, source_target_pairs={{12,8},{13,9},{14,10},{15,11},{28,24},{29,25},{30,26},{31,27},{44,... | collective-permute-start | bytes 2752520 | tf_op jit(solution)/shard_map/ppermute | solution.py:284
  79.5 23.2 %collective-permute-start.27 = (bf16[256,1792]{1,0:T(8,128)(2,1)S(1)}, bf16[256,1792]{1,0:T(8,128)(2,1)S(1)}, u32[]{:S(2)}, u32[]{:S(2)}) collective-permute-start(bf16[256,1792]{1,0:T(8,128)(2,1)S(1)} %get-tuple-element.78), channel_id=1, source_target_pairs={{0,4},{1,5},{2,6},{3,7},{16,20},{17,21},{18,22},{19,23},{32,36},{3... | collective-permute-start | bytes 2752520 | tf_op jit(solution)/shard_map/ppermute | solution.py:280
  84.2 25.9 %collective-permute-start.23 = (bf16[256,1792]{1,0:T(8,128)(2,1)S(1)}, bf16[256,1792]{1,0:T(8,128)(2,1)S(1)}, u32[]{:S(2)}, u32[]{:S(2)}) collective-permute-start(bf16[256,1792]{1,0:T(8,128)(2,1)S(1)} %collective-permute-done.21.up2), channel_id=1, source_target_pairs={{8,12},{9,13},{10,14},{11,15},{24,28},{25,29},{26,30},{27,31},{40,... | collective-permute-start | bytes 2752520 | tf_op jit(solution)/shard_map/ppermute | solution.py:280
  92.2 22.3 %collective-permute-start.24 = (bf16[256,1792]{1,0:T(8,128)(2,1)S(1)}, bf16[256,1792]{1,0:T(8,128)(2,1)S(1)}, u32[]{:S(2)}, u32[]{:S(2)}) collective-permute-start(bf16[256,1792]{1,0:T(8,128)(2,1)S(1)} %collective-permute-done.22.down2), channel_id=1, source_target_pairs={{4,0},{5,1},{6,2},{7,3},{20,16},{21,17},{22,18},{23,19},{36,32},{3... | collective-permute-start | bytes 2752520 | tf_op jit(solution)/shard_map/ppermute | solution.py:284
  102.7 5.7 %copy-start.1 = (bf16[1024,1024]{1,0:T(8,128)(2,1)S(1)}, bf16[1024,1024]{1,0:T(8,128)(2,1)}, u32[]{:S(2)}) copy-start(bf16[1024,1024]{1,0:T(8,128)(2,1)} %get-tuple-element.73.cot_ref) | copy-start | bytes 6291460
  102.7 5.7 %copy-start.2 = (bf16[256,1792]{1,0:T(8,128)(2,1)S(1)}, bf16[256,1792]{1,0:T(8,128)(2,1)}, u32[]{:S(2)}) copy-start(bf16[256,1792]{1,0:T(8,128)(2,1)} %get-tuple-element.74.own) | copy-start | bytes 2752516
  102.7 5.7 %copy-start.6 = (s32[2]{0:T(128)S(1)}, s32[2]{0:T(128)}, u32[]{:S(2)}) copy-start(s32[2]{0:T(128)} %pad_add_fusion.where_ref) | copy-start | bytes 28
  103.1 28.8 %collective-permute-start.28 = (bf16[256,1792]{1,0:T(8,128)(2,1)S(1)}, bf16[256,1792]{1,0:T(8,128)(2,1)S(1)}, u32[]{:S(2)}, u32[]{:S(2)}) collective-permute-start(bf16[256,1792]{1,0:T(8,128)(2,1)S(1)} %get-tuple-element.96), channel_id=1, source_target_pairs={{0,4},{4,8},{1,5},{5,9},{2,6},{6,10},{3,7},{7,11},{16,20},{20,24},... | collective-permute-start | bytes 2752520 | tf_op jit(solution)/shard_map/ppermute | solution.py:280
  107.7 24.2 %collective-permute-start.30 = (bf16[256,1792]{1,0:T(8,128)(2,1)S(1)}, bf16[256,1792]{1,0:T(8,128)(2,1)S(1)}, u32[]{:S(2)}, u32[]{:S(2)}) collective-permute-start(bf16[256,1792]{1,0:T(8,128)(2,1)S(1)} %get-tuple-element.95), channel_id=1, source_target_pairs={{12,8},{8,4},{13,9},{9,5},{14,10},{10,6},{15,11},{11,7},{28,24},{2... | collective-permute-start | bytes 2752520 | tf_op jit(solution)/shard_map/ppermute | solution.py:284
  115.4 13.4 %collective-permute-start.25 = (bf16[128,1792]{1,0:T(8,128)(2,1)S(1)}, bf16[128,1792]{1,0:T(8,128)(2,1)S(1)}, u32[]{:S(2)}, u32[]{:S(2)}) collective-permute-start(bf16[128,1792]{1,0:T(8,128)(2,1)S(1)} %get-tuple-element.75), channel_id=1, source_target_pairs={{0,1},{1,2},{2,3},{3,0},{4,5},{5,6},{6,7},{7,4},{8,9},{9,10},{10,1... | collective-permute-start | bytes 1376264 | tf_op jit(solution)/shard_map/ppermute | solution.py:276
  116.9 15.0 %collective-permute-start.26 = (bf16[128,1792]{1,0:T(8,128)(2,1)S(1)}, bf16[128,1792]{1,0:T(8,128)(2,1)S(1)}, u32[]{:S(2)}, u32[]{:S(2)}) collective-permute-start(bf16[128,1792]{1,0:T(8,128)(2,1)S(1)} %get-tuple-element.76), channel_id=1, source_target_pairs={{0,3},{1,0},{2,1},{3,2},{4,7},{5,4},{6,5},{7,6},{8,11},{9,8},{10,9... | collective-permute-start | bytes 1376264 | tf_op jit(solution)/shard_map/ppermute | solution.py:276
  119.8 18.8 %collective-permute-start.33 = (bf16[128,1792]{1,0:T(8,128)(2,1)S(1)}, bf16[128,1792]{1,0:T(8,128)(2,1)S(1)}, u32[]{:S(2)}, u32[]{:S(2)}) collective-permute-start(bf16[128,1792]{1,0:T(8,128)(2,1)S(1)} %get-tuple-element.87), channel_id=1, source_target_pairs={{0,1},{1,2},{2,3},{3,0},{4,5},{5,6},{6,7},{7,4},{8,9},{9,10},{10,1... | collective-permute-start | bytes 1376264 | tf_op jit(solution)/shard_map/ppermute | solution.py:276
  128.8 10.4 %collective-permute-start.34 = (bf16[128,1792]{1,0:T(8,128)(2,1)S(1)}, bf16[128,1792]{1,0:T(8,128)(2,1)S(1)}, u32[]{:S(2)}, u32[]{:S(2)}) collective-permute-start(bf16[128,1792]{1,0:T(8,128)(2,1)S(1)} %get-tuple-element.88), channel_id=1, source_target_pairs={{0,3},{1,0},{2,1},{3,2},{4,7},{5,4},{6,5},{7,6},{8,11},{9,8},{10,9... | collective-permute-start | bytes 1376264 | tf_op jit(solution)/shard_map/ppermute | solution.py:276
  132.1 21.1 %collective-permute-start.32 = (bf16[256,1792]{1,0:T(8,128)(2,1)S(1)}, bf16[256,1792]{1,0:T(8,128)(2,1)S(1)}, u32[]{:S(2)}, u32[]{:S(2)}) collective-permute-start(bf16[256,1792]{1,0:T(8,128)(2,1)S(1)} %add_convert_fusion.1), channel_id=1, source_target_pairs={{12,8},{8,4},{4,0},{13,9},{9,5},{5,1},{14,10},{10,6},{6,2},{15,11}... | collective-permute-start | bytes 2752520 | tf_op jit(solution)/shard_map/ppermute | solution.py:284
  133.6 17.5 %copy-start.3 = (bf16[1,256,1792]{2,1,0:T(8,128)(2,1)S(1)}, bf16[1,256,1792]{2,1,0:T(8,128)(2,1)}, u32[]{:S(2)}) copy-start(bf16[1,256,1792]{2,1,0:T(8,128)(2,1)} %param.26) | copy-start | bytes 2752516
  133.6 17.5 %copy-start.4 = (bf16[1,256,1792]{2,1,0:T(8,128)(2,1)S(1)}, bf16[1,256,1792]{2,1,0:T(8,128)(2,1)}, u32[]{:S(2)}) copy-start(bf16[1,256,1792]{2,1,0:T(8,128)(2,1)} %param.27) | copy-start | bytes 2752516
  133.7 19.6 %collective-permute-start.31 = (bf16[256,1792]{1,0:T(8,128)(2,1)S(1)}, bf16[256,1792]{1,0:T(8,128)(2,1)S(1)}, u32[]{:S(2)}, u32[]{:S(2)}) collective-permute-start(bf16[256,1792]{1,0:T(8,128)(2,1)S(1)} %add_convert_fusion.2), channel_id=1, source_target_pairs={{0,4},{4,8},{8,12},{1,5},{5,9},{9,13},{2,6},{6,10},{10,14},{3,7},{... | collective-permute-start | bytes 2752520 | tf_op jit(solution)/shard_map/ppermute | solution.py:280
  139.3 8.8 %collective-permute-start.35 = (bf16[128,1792]{1,0:T(8,128)(2,1)S(1)}, bf16[128,1792]{1,0:T(8,128)(2,1)S(1)}, u32[]{:S(2)}, u32[]{:S(2)}) collective-permute-start(bf16[128,1792]{1,0:T(8,128)(2,1)S(1)} %get-tuple-element.89), channel_id=1, source_target_pairs={{0,1},{1,2},{2,3},{3,0},{4,5},{5,6},{6,7},{7,4},{8,9},{9,10},{10,1... | collective-permute-start | bytes 1376264 | tf_op jit(solution)/shard_map/ppermute | solution.py:276
  141.3 9.8 %collective-permute-start.36 = (bf16[128,1792]{1,0:T(8,128)(2,1)S(1)}, bf16[128,1792]{1,0:T(8,128)(2,1)S(1)}, u32[]{:S(2)}, u32[]{:S(2)}) collective-permute-start(bf16[128,1792]{1,0:T(8,128)(2,1)S(1)} %get-tuple-element.92), channel_id=1, source_target_pairs={{0,3},{1,0},{2,1},{3,2},{4,7},{5,4},{6,5},{7,6},{8,11},{9,8},{10,9... | collective-permute-start | bytes 1376264 | tf_op jit(solution)/shard_map/ppermute | solution.py:276
